TPU v7x, 32 devices: a whole 2x2x4 slice. The times are simulated.
32 devices in a mesh: grp: 2 (over y), blk: 4 (over z), col: 2 (over x), rep: 2 (over core).
Axes of the slice: x: 2, y: 2, z: 4, core: 2. Of those that a mesh axis runs over, the one named last changes fastest.
Arguments:
- coords: float32 [3, 131072], P(None, ('grp', 'blk')), parts along dimension 1, may hold values from 0 to 1
- observations: float32 [131072], P(('grp', 'blk')), parts along dimension 0, may hold values from -6 to 6
- nugget: float32 [131072], P(('grp', 'blk')), parts along dimension 0, may hold values from 0.1 to 1
- tile_pairs: int32 [2, 8192], P(None, ('grp', 'blk', 'col', 'rep')), parts along dimension 1, may hold values from 0 to 511, as said below
- tile_live: int32 [32], P(('grp', 'blk', 'col', 'rep')), parts along dimension 0, may hold values from 64 to 256, as said below
Outputs:
- solution_field: float32 [131072], P(('grp', 'blk')), parts along dimension 0
- residual: float32 [131072], P(('grp', 'blk')), parts along dimension 0
There are 2 independent parts, one for each index of `grp`. A program takes and returns all parts, laid end to end along the dimension named above; each array names one. Nothing has to cross between parts.
Inputs may be any that keep to these rules, and one draw needn't show every extreme that they name: `tile_pairs`: entries name point blocks. Every slot has its row block, or else its column block, among the 128 blocks of its own device's index of blk; most slots have the row block there. Call the slot's other block its column block when the row block is the device's own, else its row block. Of one device's slots, at most (259) // 4 have their other block among the blocks of any one index of blk, and on every device some index gets exactly that many. Slots at or beyond a device's live count are ignored. `tile_live`: some device has all 256 slots live.
All inputs are finite; a program needn't handle non-finite values.
Results may differ from a plain program's by a relative error of at most 0.0003.
Values sent between devices are 32-bit elements; how exact they have to be, the bound alone decides.
No kernel may reach another device: no remote copies, remote signals or barrier semaphores. Data moves between devices by JAX's collectives and lax.ppermute only.
A program may use at most 128 MiB of HBM per device.

v0:
```python
import functools

import jax
import jax.numpy as jnp
from jax import lax
from jax.experimental import pallas as pl
from jax.experimental.pallas import tpu as pltpu
from jax.sharding import PartitionSpec as P

BS = 128
ITERS = 3
SUPPORT = 0.3
HALF_LOG2E = 0.7213475204444817
DEPTH = 48
UNROLL = 4
ARRAYS = 4
MIB = 1024 * 1024
VMEM = pl.BlockSpec(memory_space=pltpu.VMEM)
SMEM = pl.BlockSpec(memory_space=pltpu.SMEM)
ANY = pl.BlockSpec(memory_space=pl.ANY)
BF16 = jnp.bfloat16
F32 = jnp.float32


class Sizes:
    def __init__(self, points, slots):
        self.blks = lax.axis_size("blk")
        self.reps = lax.axis_size("rep")
        self.plane = lax.axis_size("col") * self.reps
        self.devs = self.blks * self.plane
        self.points = points
        self.slots = slots
        self.local_blocks = points // BS
        self.blocks = self.local_blocks * self.blks
        self.own = self.local_blocks // self.plane
        self.capacity = 2 * self.plane * slots + 1024
        per_row = slots * self.devs // self.blocks
        self.first_mib = 6 + self.blocks * DEPTH * BS * 2 // MIB
        self.kept = min(448, (48 - self.first_mib) * 16) // ARRAYS
        self.scale = 16.0 / (BS * per_row) / 256.0

    def me(self):
        return (lax.axis_index("blk") * lax.axis_size("col") + lax.axis_index("col")) * self.reps + lax.axis_index(
            "rep"
        )


def swap(x, axis, code):
    return lax.ppermute(x, axis, [(i, i ^ code) for i in range(lax.axis_size(axis))])


def along_blk(x):
    return jnp.concatenate([x] + [swap(x, "blk", k) for k in range(1, lax.axis_size("blk"))], axis=0)


def over_plane(x):
    reps = lax.axis_size("rep")
    found = {0: x}
    for c in range(1, lax.axis_size("col")):
        found[c * reps] = swap(x, "col", c)
    for start in sorted(found):
        for r in range(1, reps):
            found[start + r] = swap(found[start], "rep", r)
    return [found[k] for k in sorted(found)]


def assemble(sz, refs, rows, target):
    me = sz.me()
    for k, ref in enumerate(refs):
        for z in range(ref.shape[0] // rows):
            start = pl.multiple_of(jnp.bitwise_xor(me, z * sz.plane + k) * rows, 8)
            target[pl.ds(start, rows), :] = ref[z * rows : (z + 1) * rows, :]


def split3(x):
    high = x.astype(BF16).astype(F32)
    rest = x - high
    middle = rest.astype(BF16).astype(F32)
    return high, middle, rest - middle


def features_of(rows, factor, unit, norm):
    feature = lax.broadcasted_iota(jnp.int32, (8, BS), 0)
    x, y, z = ((row - 0.5) * (4.0 / SUPPORT) for row in rows)
    feats = jnp.where(feature == unit, 1.0, 0.0)
    for place, row in ((0, factor * x), (1, factor * y), (2, factor * z), (norm, x * x + y * y + z * z)):
        feats = jnp.where(feature == place, row, feats)
    return split3(feats)


def block_row(ref, c, part, k):
    return ref[c, pl.ds(k, 1), :] if len(ref.shape) == 3 else ref[pl.ds(c * part + k, 1), :]


def lhs_kernel(sz, home_ref, out_ref):
    quarter = lax.axis_index("col") * sz.reps + lax.axis_index("rep")
    for i in range(sz.own):
        h, m, l = features_of([block_row(home_ref, c, None, quarter * sz.own + i) for c in range(3)], 1.0, 3, 4)
        feats = jnp.concatenate([h, h, m, m, h, l, jnp.zeros((BS - DEPTH, BS), F32)], axis=0)
        out_ref[i * BS : (i + 1) * BS, :] = feats.T.astype(BF16)
    out_ref[sz.own * BS :, :] = jnp.zeros((BS, BS), BF16)


def list_kernel(sz, *refs):
    me = sz.me()
    out_ref, count_ref, target, other, place, value, key_column, key_row, entry_row = refs[sz.plane :]
    lines = sz.slots // BS
    at = 2 * lines * sz.devs
    for base in range(0, at, 2 * lines):
        pairs_ref = refs[base // (2 * lines * sz.blks)]
        start = base % (2 * lines * sz.blks)
        rows = pairs_ref[start : start + lines, :]
        cols = pairs_ref[start + lines : start + 2 * lines, :]
        target[base : base + lines, :] = rows
        other[base : base + lines, :] = cols
        target[base + lines : base + 2 * lines, :] = cols
        other[base + lines : base + 2 * lines, :] = rows
    local = target[...] - me * sz.own
    mine = jnp.logical_and(local >= 0, local < sz.own)
    flags = jnp.where(mine, 1.0, 0.0)
    a = lax.broadcasted_iota(jnp.int32, (BS, BS), 0)
    b = lax.broadcasted_iota(jnp.int32, (BS, BS), 1)
    ahead = jnp.where(a < b, 1.0, 0.0).astype(BF16)
    before = jnp.dot(flags.astype(BF16), ahead, preferred_element_type=F32)
    totals = jnp.broadcast_to(jnp.sum(flags, axis=1, keepdims=True), (at, BS))
    a = lax.broadcasted_iota(jnp.int32, (at, at), 0)
    b = lax.broadcasted_iota(jnp.int32, (at, at), 1)
    above = jnp.dot(jnp.where(b < a, 1.0, 0.0).astype(BF16), totals.astype(BF16), preferred_element_type=F32)
    place[...] = jnp.where(mine, above + before, -1.0)
    ends = jnp.sum(jnp.where(lax.broadcasted_iota(jnp.int32, (at, BS), 1) == 0, above + totals, 0.0), axis=1, keepdims=True)
    starts = ends - totals[:, 0:1]
    value[...] = (local + 256 * other[...]).astype(F32)
    count = jnp.sum(flags).astype(jnp.int32)
    sub = lax.broadcasted_iota(jnp.int32, (BS, BS), 0)
    lane = lax.broadcasted_iota(jnp.int32, (1, BS), 1)

    chunks = jnp.maximum(lax.shift_right_logical(count + BS - 1, 7), 1)

    def key_of(found, slot):
        entry = jnp.where(slot < count, found.astype(jnp.int32), sz.own)
        return entry.astype(F32), (jnp.bitwise_and(entry, 255) * 65536 + slot).astype(F32)

    def compact(c, unused):
        slot = (sub + c * BS).astype(F32)
        base = (c * BS).astype(F32)
        first = jnp.sum(jnp.where(ends <= base, 1.0, 0.0)).astype(jnp.int32)
        last = jnp.sum(jnp.where(starts < base + BS, 1.0, 0.0)).astype(jnp.int32)
        first = jnp.minimum(lax.shift_right_logical(first, 2), at // 4)
        last = lax.shift_right_logical(last + 3, 2)

        def lines(g, total):
            for u in range(4):
                r = 4 * g + u
                hit = place[pl.ds(r, 1), :] == slot
                total = jnp.where(hit, value[pl.ds(r, 1), :], total)
            return total

        total = lax.fori_loop(first, last, lines, jnp.zeros((BS, BS), F32))
        entry, key = key_of(jnp.sum(total.T, axis=0, keepdims=True), lane + c * BS)
        entry_row[pl.ds(c, 1), :] = entry
        key_row[pl.ds(c, 1), :] = key
        unused_entry, key = key_of(jnp.sum(total, axis=1, keepdims=True), sub[:, 0:1] + c * BS)
        key_column[pl.ds(pl.multiple_of(c * BS, BS), BS), :] = jnp.broadcast_to(key, (BS, BS))
        return unused

    lax.fori_loop(0, chunks, compact, 0)

    bound = lane.astype(F32) * 65536.0

    def tally(c, carry):
        keys = key_column[pl.ds(pl.multiple_of(c * BS, BS), BS), :]
        from_here, after = carry
        return from_here + jnp.where(keys >= bound, 1.0, 0.0), after + jnp.where(keys >= bound + 65536.0, 1.0, 0.0)

    zero = jnp.zeros((BS, BS), F32)
    from_here, after = lax.fori_loop(0, chunks, tally, (zero, zero))
    from_here = jnp.sum(from_here, axis=0, keepdims=True)
    each = from_here - jnp.sum(after, axis=0, keepdims=True)
    odd = jnp.where(lane < sz.own, each - 2.0 * jnp.floor(0.5 * each), 0.0)
    wide_odd = jnp.broadcast_to(odd, (BS, BS))
    odd_column = wide_odd.T
    odd_before = jnp.dot(wide_odd.astype(BF16), ahead, preferred_element_type=F32)[0:1, :]
    start = (chunks * BS).astype(F32) - from_here + odd_before
    null_place = jnp.where(odd > 0.0, start + each, -1.0)
    null_entry = (lane + 256 * sz.blocks).astype(F32)
    full = count + jnp.sum(odd).astype(jnp.int32)
    count_ref[0] = full

    def rank(c, unused):
        keys = key_row[pl.ds(c, 1), :]

        def below(k, total):
            lower = key_column[pl.ds(pl.multiple_of(k * BS, BS), BS), :] < keys
            return total + jnp.where(lower, 1.0, 0.0)

        past = (sub + 1).astype(F32) * 65536.0 <= keys
        total = lax.fori_loop(0, chunks, below, jnp.where(past, odd_column, 0.0))
        place[pl.ds(c, 1), :] = jnp.sum(total, axis=0, keepdims=True)
        return unused

    lax.fori_loop(0, chunks, rank, 0)

    def arrange(c, unused):
        slot = (sub + c * BS).astype(F32)

        def line(r, total):
            hit = place[pl.ds(r, 1), :] == slot
            return total + jnp.where(hit, entry_row[pl.ds(r, 1), :], 0.0)

        total = lax.fori_loop(0, chunks, line, jnp.where(null_place == slot, null_entry, 0.0))
        found = jnp.sum(total.T, axis=0, keepdims=True).astype(jnp.int32)
        out_ref[pl.ds(c, 1), :] = jnp.where(lane + c * BS < full, found, sz.own)
        return unused

    lax.fori_loop(0, jnp.maximum(lax.shift_right_logical(full + BS - 1, 7), 1), arrange, 0)


def entry_of(list_ref, k):
    entry = list_ref[k]
    return jnp.bitwise_and(entry, 255), lax.shift_right_logical(entry, 8)


def squared_of(features, *others):
    return jnp.dot(features, jnp.concatenate(others, axis=1), preferred_element_type=F32)


def taper_of(squared):
    squared = jnp.maximum(squared, 1e-20)
    remain = jnp.maximum(4.0 - jnp.exp2(jnp.log(squared) * HALF_LOG2E), 0.0)
    twice = remain * remain
    return twice * twice * (5.0 - remain)


def kept_groups(sz, count, at):
    first = at * (sz.kept // UNROLL)
    last = jnp.minimum(lax.div(count + (UNROLL - 1), UNROLL), first + sz.kept // UNROLL)
    return first, jnp.maximum(first, last)


def vector_row(vec_ref, j):
    return vec_ref[pl.ds(jnp.minimum(j, vec_ref.shape[0] - 1), 1), :]


def own_features(lhs_ref, i):
    return lhs_ref[pl.ds(pl.multiple_of(i * BS, BS), BS), :DEPTH]


def other_features(rhs_ref, j):
    return rhs_ref[pl.ds(pl.multiple_of(j * DEPTH, DEPTH), DEPTH), :]


def clear(*accs):
    for acc in accs:
        acc[...] = jnp.zeros_like(acc)


def generate(sz, list_ref, count, lhs_ref, rhs_ref, tile_refs, squares):
    top = jnp.maximum(lax.div(count + (UNROLL - 1), UNROLL) - 1, 0)

    def squared(g, u):
        k = jnp.minimum(g, top) * UNROLL + u
        i, j = entry_of(list_ref, k)
        unused, twin = entry_of(list_ref, k + 1)
        return squared_of(own_features(lhs_ref, i), other_features(rhs_ref, j), other_features(rhs_ref, twin))

    def fill(u, both):
        squares[u * BS : (u + 1) * BS, :] = both[:, :BS]
        squares[(u + 1) * BS : (u + 2) * BS, :] = both[:, BS:]

    for u in range(0, UNROLL, 2):
        fill(u, squared(0, u))
    for at, tile_ref in enumerate(tile_refs):

        def group(g, unused, at=at, tile_ref=tile_ref):
            for u in range(0, UNROLL, 2):
                tiles = taper_of(squares[u * BS : (u + 2) * BS, :])
                fill(u, squared(g + 1, u))
                start = pl.multiple_of((g * UNROLL + u - at * sz.kept) * BS, BS)
                tile_ref[pl.ds(start, 2 * BS), :] = tiles
            return unused

        lax.fori_loop(*kept_groups(sz, count, at), group, 0)


def sweep(sz, list_ref, count, tile_refs, vec_ref, acc, acc_ones=None):
    accs = [acc] if acc_ones is None else [acc, acc_ones]
    clear(*accs)
    carry = (jnp.int32(-1),) + tuple(jnp.zeros((BS, BS), F32) for unused in accs)
    for at, tile_ref in enumerate(tile_refs):

        def group(g, carry, at=at, tile_ref=tile_ref):
            before, *totals = carry
            for u in range(0, UNROLL, 2):
                i, j = entry_of(list_ref, g * UNROLL + u)
                unused, twin = entry_of(list_ref, g * UNROLL + u + 1)
                keep = jnp.where(i == before, 1.0, 0.0)
                start = (g * UNROLL + u - at * sz.kept) * BS
                tile = tile_ref[pl.ds(pl.multiple_of(start, BS), BS), :]
                twin_tile = tile_ref[pl.ds(pl.multiple_of(start + BS, BS), BS), :]
                terms = [tile * vector_row(vec_ref, j) + twin_tile * vector_row(vec_ref, twin), tile + twin_tile]
                totals = [total * keep + term for total, term in zip(totals, terms)]
                for ref, total in zip(accs, totals):
                    ref[pl.ds(pl.multiple_of(i * BS, BS), BS), :] = total
                before = i
            return (before, *totals)

        carry = lax.fori_loop(*kept_groups(sz, count, at), group, carry)


def extras(sz, list_ref, count, vec_ref, acc, acc_ones, remake):
    def extra(k, unused):
        i, j = entry_of(list_ref, k)
        tile = taper_of(squared_of(*remake(i, j)))
        rows = pl.ds(pl.multiple_of(i * BS, BS), BS)
        acc[rows, :] += tile * vector_row(vec_ref, j)
        if acc_ones is not None:
            acc_ones[rows, :] += tile
        return unused

    kept = sz.kept * ARRAYS
    lax.fori_loop(kept, jnp.maximum(count, kept), extra, 0)


def finish(sz, acc, out_ref):
    unit = jnp.ones((8, BS), BF16)
    across = (((1,), (1,)), ((), ()))
    for i in range(sz.own):
        whole = acc[i * BS : (i + 1) * BS, :]
        high = whole.astype(BF16)
        low = (whole - high.astype(F32)).astype(BF16)
        y = lax.dot_general(unit, high, across, preferred_element_type=F32)
        y = y + lax.dot_general(unit, low, across, preferred_element_type=F32)
        out_ref[i : i + 1, :] = y[0:1, :] * sz.scale


def total_of(x):
    return jnp.sum(jnp.sum(x, axis=0, keepdims=True), axis=1, keepdims=True)


def place_block(piece_ref, part, first, rhs_ref):
    def one(k, unused):
        h, m, l = features_of([block_row(piece_ref, c, part, k) for c in range(3)], -2.0, 4, 3)
        feats = jnp.concatenate([h, m, h, m, l, h], axis=0).astype(BF16)
        rhs_ref[pl.ds(pl.multiple_of((first + k) * DEPTH, DEPTH), DEPTH), :] = feats
        return unused

    lax.fori_loop(0, part, one, 0, unroll=4)


def first_kernel(sz, *refs):
    list_ref, count_ref, lhs_ref, nugget_any, obs_any, home_ref = refs[:6]
    coord_refs = refs[6 : 6 + (sz.blks - 1) * sz.reps]
    refs = refs[6 + (sz.blks - 1) * sz.reps :]
    tile_refs = refs[:ARRAYS]
    spare_ref, obs_ref, diag_ref, mapped_ref, norm_ref = refs[ARRAYS : ARRAYS + 5]
    rhs_ref, acc, acc_ones, total_row, squares, nugget_ref, done, fetched = refs[ARRAYS + 5 :]
    blk, rep = lax.axis_index("blk"), lax.axis_index("rep")
    home = pl.ds(pl.multiple_of(blk * sz.local_blocks, 8), sz.local_blocks)
    fetch = pltpu.make_async_copy(nugget_any, nugget_ref, fetched.at[0])
    fetch_obs = pltpu.make_async_copy(obs_any, obs_ref.at[home, :], fetched.at[1])
    fetch.start()
    fetch_obs.start()
    for at, piece_ref in enumerate(coord_refs):
        code, turn = at // sz.reps + 1, at % sz.reps
        part = sz.local_blocks // sz.reps
        first = jnp.bitwise_xor(blk, code) * sz.local_blocks + jnp.bitwise_xor(rep, turn) * part
        first = pl.multiple_of(first, 8)
        place_block(piece_ref, part, first, rhs_ref)
        obs_ref[pl.ds(first, part), :] = piece_ref[3 * part : 4 * part, :]
    place_block(home_ref, sz.local_blocks, blk * sz.local_blocks, rhs_ref)
    far = lax.broadcasted_iota(jnp.int32, (DEPTH, BS), 0) == 3
    rhs_ref[sz.blocks * DEPTH :, :] = jnp.where(far, 1e6, 0.0).astype(BF16)
    count = count_ref[0]
    generate(sz, list_ref, count, lhs_ref, rhs_ref, tile_refs, squares)
    fetch_obs.wait()
    sweep(sz, list_ref, count, tile_refs, obs_ref, acc, acc_ones)
    extras(
        sz,
        list_ref,
        count,
        obs_ref,
        acc,
        acc_ones,
        lambda i, j: (own_features(lhs_ref, i), other_features(rhs_ref, j)),
    )

    @pl.when(count > sz.kept * ARRAYS)
    def save():
        copy = pltpu.make_async_copy(rhs_ref, spare_ref, done)
        copy.start()
        copy.wait()

    finish(sz, acc_ones, total_row)
    finish(sz, acc, mapped_ref)
    quarter = lax.axis_index("col") * sz.reps + rep
    own = pl.ds(pl.multiple_of(sz.me() * sz.own, 8), sz.own)
    fetch.wait()
    diag = nugget_ref[pl.ds(pl.multiple_of(quarter * sz.own, 8), sz.own), :] + total_row[...]
    diag_ref[...] = diag
    mapped_ref[...] += diag * obs_ref[own, :]
    norm_ref[...] = jnp.broadcast_to(total_of(obs_ref[...] * obs_ref[...]), (8, BS))


def step_kernel(sz, last, *refs):
    list_ref, count_ref, lhs_ref, spare_ref, diag_ref, norm_ref, field_ref, resid_ref, dirn_ref = refs[:9]
    pieces = refs[9 : 9 + sz.plane]
    tile_refs = refs[9 + sz.plane : 9 + sz.plane + ARRAYS]
    rest = refs[9 + sz.plane + ARRAYS :]
    mapped_ref, next_norm_ref, next_field_ref, next_resid_ref, next_dirn_ref = rest[:5]
    if last:
        dot_ref, dirn = rest[5:7]
    else:
        dirn = next_dirn_ref
    mapped, acc, features, others, done = rest[-5:]
    me = sz.me()
    assemble(sz, pieces, sz.own, mapped)
    norm = norm_ref[0:1, 0:1]
    step = norm / total_of(dirn_ref[...] * mapped[...])
    resid = resid_ref[...] - step * mapped[...]
    next_norm = total_of(resid * resid)
    dirn[...] = resid + (next_norm / norm) * dirn_ref[...]
    next_norm_ref[...] = jnp.broadcast_to(next_norm, (8, BS))
    home = pl.ds(pl.multiple_of(lax.axis_index("blk") * sz.local_blocks, 8), sz.local_blocks)
    own = pl.ds(pl.multiple_of(me * sz.own, 8), sz.own)
    field = step * dirn_ref[home, :]
    if last:
        next_field_ref[...] = field_ref[...] + field
        next_resid_ref[...] = resid_ref[home, :] - step * mapped[home, :]
        next_dirn_ref[...] = dirn[home, :]
    else:
        next_field_ref[...] = field
        next_resid_ref[...] = resid

    def remake(i, j):
        for source, start, size, target in ((lhs_ref, i, BS, features), (spare_ref, j, DEPTH, others)):
            copy = pltpu.make_async_copy(source.at[pl.ds(pl.multiple_of(start * size, size), size), :], target, done)
            copy.start()
            copy.wait()
        return features[:, :DEPTH], others[...]

    sweep(sz, list_ref, count_ref[0], tile_refs, dirn, acc)
    extras(sz, list_ref, count_ref[0], dirn, acc, None, remake)
    finish(sz, acc, mapped_ref)
    ours = mapped_ref[...] + diag_ref[...] * dirn[own, :]
    mapped_ref[...] = ours
    if last:
        dot_ref[...] = jnp.broadcast_to(total_of(ours * dirn[own, :]), dot_ref.shape)


def last_kernel(sz, *refs):
    norm_ref, field_ref, resid_ref, dirn_ref = refs[:4]
    pieces = refs[4 : 4 + sz.plane]
    out_field_ref, out_resid_ref = refs[4 + sz.plane :]
    product = jnp.zeros((8, BS), F32)
    for ref in pieces:
        for z in range(sz.blks):
            product = product + ref[sz.own + 8 * z : sz.own + 8 * (z + 1), :]
    step = norm_ref[0:1, :] / product[0:1, :]
    out_field_ref[...] = field_ref[...] + step * dirn_ref[...]
    quarter = lax.axis_index("col") * sz.reps + lax.axis_index("rep")
    for k, ref in enumerate(pieces):
        rows = pl.ds(pl.multiple_of(jnp.bitwise_xor(quarter, k) * sz.own, 8), sz.own)
        out_resid_ref[rows, :] = resid_ref[rows, :] - step * ref[: sz.own, :]


def call(kernel, mib, in_specs, shapes, out_specs, scratch, flops, *args):
    return pl.pallas_call(
        kernel,
        in_specs=in_specs,
        out_shape=shapes,
        out_specs=out_specs,
        scratch_shapes=scratch,
        compiler_params=pltpu.CompilerParams(vmem_limit_bytes=mib * MIB),
        cost_estimate=pl.CostEstimate(flops=flops, bytes_accessed=1 << 20, transcendentals=0),
    )(*args)


def array(*shape, dtype=F32):
    return jax.ShapeDtypeStruct(shape, dtype)


def local(coords, observations, nugget, tile_pairs, tile_live):
    sz = Sizes(observations.shape[0], tile_pairs.shape[1])
    own, blocks, home = sz.own, sz.blocks, sz.local_blocks
    alive = jnp.arange(sz.slots, dtype=jnp.int32) < tile_live[0]
    pairs = jnp.where(alive, tile_pairs, -1).reshape(2 * sz.slots // BS, BS)
    rep = lax.axis_index("rep")
    part = home // sz.reps
    obs_rows = observations.reshape(home, BS)
    rows = coords.reshape(3, home, BS)
    half = lax.dynamic_slice_in_dim(jnp.concatenate([rows, obs_rows[None]], axis=0), rep * part, part, axis=1)
    half = half.reshape(4 * part, BS)
    nears = [swap(half, "blk", z) for z in range(1, sz.blks)]
    pair_arrays = over_plane(along_blk(pairs))

    lhs = call(
        functools.partial(lhs_kernel, sz),
        12,
        [VMEM],
        array((own + 1) * BS, BS, dtype=BF16),
        VMEM,
        [],
        10_000_000,
        rows,
    )
    lines = 2 * sz.slots // BS * sz.devs
    table, count = call(
        functools.partial(list_kernel, sz),
        12,
        [VMEM] * sz.plane,
        (array(sz.capacity // BS, BS, dtype=jnp.int32), array(1, dtype=jnp.int32)),
        (VMEM, SMEM),
        [pltpu.VMEM((lines, BS), jnp.int32)] * 2
        + [pltpu.VMEM((lines, BS), F32)] * 2
        + [pltpu.VMEM((sz.capacity, BS), F32)]
        + [pltpu.VMEM((sz.capacity // BS, BS), F32)] * 2,
        10_000_000,
        *pair_arrays,
    )
    table, lhs, *nears = lax.optimization_barrier((table.reshape(sz.capacity), lhs, *nears))
    coord_arrays = []
    for near in nears:
        coord_arrays += [near] + [swap(near, "rep", r) for r in range(1, sz.reps)]
    tall = pltpu.VMEM(((own + 1) * BS, BS), F32)
    kept = [pltpu.VMEM((sz.kept * BS, BS), F32)] * ARRAYS
    *tiles, spare, obs, diag, mapped, norm = call(
        functools.partial(first_kernel, sz),
        sz.first_mib,
        [SMEM, SMEM, VMEM, ANY, ANY] + [VMEM] * (1 + len(coord_arrays)),
        kept
        + [
            pltpu.HBM(((blocks + 1) * DEPTH, BS), BF16),
            array(blocks, BS),
            array(own, BS),
            array(own, BS),
            array(8, BS),
        ],
        [VMEM] * ARRAYS + [ANY] + [VMEM] * 4,
        [
            pltpu.VMEM(((blocks + 1) * DEPTH, BS), BF16),
            tall,
            tall,
            pltpu.VMEM((own, BS), F32),
            pltpu.VMEM((UNROLL * BS, BS), F32),
            pltpu.VMEM((home, BS), F32),
            pltpu.SemaphoreType.DMA,
            pltpu.SemaphoreType.DMA((2,)),
        ],
        100_000_000,
        table,
        count,
        lhs,
        pltpu.with_memory_space_constraint(nugget.reshape(home, BS), pltpu.HBM),
        pltpu.with_memory_space_constraint(obs_rows, pltpu.HBM),
        rows,
        *coord_arrays,
    )
    tiles = [pltpu.with_memory_space_constraint(tile, pltpu.VMEM) for tile in tiles]
    spare = pltpu.with_memory_space_constraint(spare, pltpu.HBM)
    field, resid, dirn = norm, obs, obs
    for sweep_index in range(1, ITERS):
        last = sweep_index + 1 == ITERS
        span = home if last else blocks
        outs = [array(own, BS), array(8, BS), array(home, BS), array(span, BS), array(span, BS)]
        mapped, norm, field, resid, dirn, *dot = call(
            functools.partial(step_kernel, sz, last),
            5,
            [SMEM, SMEM, ANY, ANY] + [VMEM] * (5 + sz.plane + ARRAYS),
            outs + [array(8, BS)] * last,
            [VMEM] * (len(outs) + last),
            [pltpu.VMEM((blocks, BS), F32)] * (1 + last)
            + [tall, pltpu.VMEM((BS, BS), BF16), pltpu.VMEM((DEPTH, BS), BF16), pltpu.SemaphoreType.DMA],
            100_000_000,
            table,
            count,
            lhs,
            spare,
            diag,
            norm,
            field,
            resid,
            dirn,
            *over_plane(along_blk(mapped)),
            *tiles,
        )
    ends = over_plane(jnp.concatenate([mapped, along_blk(dot[0])], axis=0))
    field, resid = call(
        functools.partial(last_kernel, sz),
        4,
        [VMEM] * (4 + sz.plane),
        (array(home, BS), array(home, BS)),
        (VMEM, VMEM),
        [],
        100_000,
        norm,
        field,
        resid,
        dirn,
        *ends,
    )
    return field.reshape(sz.points), resid.reshape(sz.points)


def solution(mesh):
    in_specs = (
        P(None, ("grp", "blk")),
        P(("grp", "blk")),
        P(("grp", "blk")),
        P(None, ("grp", "blk", "col", "rep")),
        P(("grp", "blk", "col", "rep")),
    )
    out_specs = (P(("grp", "blk")), P(("grp", "blk")))
    return jax.shard_map(local, mesh=mesh, in_specs=in_specs, out_specs=out_specs, check_vma=False)
```

profile of v0, /device:TPU:0, one launch (start us, length us, event | category | flops | bytes accessed | tf_op | source)
XLA Modules:
  0.0 107.4 jit_solution(16441167535844140601)
XLA Ops:
  1.3 0.7 broadcast_select_fusion
  2.0 5.0 %collective-permute-start.2 = (s32[4,128]{1,0:T(4,128)S(1)}, s32[4,128]{1,0:T(4,128)S(1)}, u32[]{:S(2)}, u32[]{:S(2)}) collective-permute-start(s32[4,128]{1,0:T(4,128)S(1)} %reshape.28), channel_id=1, source_target_pairs={{0,12},{4,8},{8,4},{12,0},{1,13},{5,9},{9,5},{13,1},{2,14},{6,10},... | collective-permute-start | bytes 6152 | tf_op jit(solution)/shard_map/ppermute | solution.py:49
  7.0 0.6 collective-permute-start
  7.7 1.0 copy.9
  8.6 0.8 fusion
  9.4 3.8 %collective-permute-start.8 = (f32[256,128]{1,0:T(8,128)S(1)}, f32[256,128]{1,0:T(8,128)S(1)}, u32[]{:S(2)}, u32[]{:S(2)}) collective-permute-start(f32[256,128]{1,0:T(8,128)S(1)} %bitcast.22), channel_id=1, source_target_pairs={{0,12},{4,8},{8,4},{12,0},{1,13},{5,9},{9,5},{13,1},{2,14},{6,10},... | collective-permute-start | bytes 393224 | tf_op jit(solution)/shard_map/ppermute | solution.py:49
  13.2 0.0 collective-permute-start.7
  13.2 0.0 collective-permute-done.2
  13.2 0.6 collective-permute-start.6
  13.9 0.0 collective-permute-done.1
  13.9 1.7 %collective-permute-start.4 = (s32[16,128]{1,0:T(8,128)S(1)}, s32[16,128]{1,0:T(8,128)S(1)}, u32[]{:S(2)}, u32[]{:S(2)}) collective-permute-start(s32[16,128]{1,0:T(8,128)S(1)} %pad_add_fusion.refs_0_), channel_id=1, source_target_pairs={{0,2},{2,0},{1,3},{3,1},{4,6},{6,4},{5,7},{7,5},{8,10},{10,8},{9,1... | collective-permute-start | bytes 24584 | tf_op jit(solution)/shard_map/ppermute | solution.py:49
  15.6 2.0 %collective-permute-done.4.refs_2_ = s32[16,128]{1,0:T(8,128)S(1)} collective-permute-done((s32[16,128]{1,0:T(8,128)S(1)}, s32[16,128]{1,0:T(8,128)S(1)}, u32[]{:S(2)}, u32[]{:S(2)}) %collective-permute-start.4) | collective-permute-done | bytes 8224 | tf_op jit(solution)/shard_map/ppermute | solution.py:49
  17.6 0.4 shard_map.69.refs_2_
  18.0 0.8 collective-permute-done.5.refs_3_
  18.8 2.2 %shard_map.68 = (s32[24,128]{1,0:T(8,128)S(1)}, s32[1]{0:T(128)}) custom-call(s32[16,128]{1,0:T(8,128)S(1)} %pad_add_fusion.refs_0_, s32[16,128]{1,0:T(8,128)S(1)} %collective-permute-done.3.refs_1_, s32[16,128]{1,0:T(8,128)S(1)} %collective-permute-done.4.refs_2_, s32[16,128]{1,0:T(8,128)S(1)} %collective-permute-done.5.refs_3_), custom_call_target="tpu_custom_call" | custom-call | flops 10000000 | bytes 1048576 | tf_op jit(solution)/shard_map/pallas_call | solution.py:467
  21.0 2.4 %collective-permute-done.7.refs_8_ = f32[256,128]{1,0:T(8,128)S(1)} collective-permute-done((f32[256,128]{1,0:T(8,128)S(1)}, f32[256,128]{1,0:T(8,128)S(1)}, u32[]{:S(2)}, u32[]{:S(2)}) %collective-permute-start.7) | collective-permute-done | bytes 131104 | tf_op jit(solution)/shard_map/ppermute | solution.py:49
  23.4 0.5 collective-permute-start.10
  23.9 0.0 collective-permute-start.11
  23.9 0.8 collective-permute-done.9.refs_7_
  24.8 0.2 collective-permute-done.10.refs_9_
  25.0 0.3 collective-permute-done.11.refs_11_
  25.3 22.8 %shard_map.70 = (f32[14336,128]{1,0:T(8,128)S(1)}, f32[14336,128]{1,0:T(8,128)S(1)}, f32[14336,128]{1,0:T(8,128)S(1)}, f32[14336,128]{1,0:T(8,128)S(1)}, bf16[24...) custom-call(s32[3072]{0:T(1024)S(1)} %bitcast.16, ...), custom_call_target="tpu_custom_call" | custom-call | flops 100000000 | bytes 1048576 | tf_op jit(solution)/shard_map/pallas_call | solution.py:467
  48.1 11.3 %collective-permute-start.14 = (f32[32,128]{1,0:T(8,128)S(1)}, f32[32,128]{1,0:T(8,128)S(1)}, u32[]{:S(2)}, u32[]{:S(2)}) collective-permute-start(f32[32,128]{1,0:T(8,128)S(1)} %get-tuple-element.42), channel_id=1, source_target_pairs={{0,12},{4,8},{8,4},{12,0},{1,13},{5,9},{9,5},{13,1},{2,14},{6,10},... | collective-permute-start | bytes 49160 | tf_op jit(solution)/shard_map/ppermute | solution.py:49
  59.4 0.6 collective-permute-start.12
  60.1 3.1 %collective-permute-done.12 = f32[32,128]{1,0:T(8,128)S(1)} collective-permute-done((f32[32,128]{1,0:T(8,128)S(1)}, f32[32,128]{1,0:T(8,128)S(1)}, u32[]{:S(2)}, u32[]{:S(2)}) %collective-permute-start.12) | collective-permute-done | bytes 16416 | tf_op jit(solution)/shard_map/ppermute | solution.py:49
  63.2 0.9 collective-permute-done.13
  64.1 1.4 %collective-permute-start.16 = (f32[128,128]{1,0:T(8,128)S(1)}, f32[128,128]{1,0:T(8,128)S(1)}, u32[]{:S(2)}, u32[]{:S(2)}) collective-permute-start(f32[128,128]{1,0:T(8,128)S(1)} %constant_dynamic-update-slice_fusion.refs_9_), channel_id=1, source_target_pairs={{0,2},{2,0},{1,3},{3,1},{4,6},{6,4},{5,7},{7,5},{8,10},{10,8},{9,1... | collective-permute-start | bytes 196616 | tf_op jit(solution)/shard_map/ppermute | solution.py:49
  65.4 2.3 %collective-permute-start.15 = (f32[128,128]{1,0:T(8,128)S(1)}, f32[128,128]{1,0:T(8,128)S(1)}, u32[]{:S(2)}, u32[]{:S(2)}) collective-permute-start(f32[128,128]{1,0:T(8,128)S(1)} %constant_dynamic-update-slice_fusion.refs_9_), channel_id=1, source_target_pairs={{0,1},{1,0},{2,3},{3,2},{4,5},{5,4},{6,7},{7,6},{8,9},{9,8},{10,11... | collective-permute-start | bytes 196616 | tf_op jit(solution)/shard_map/ppermute | solution.py:49
  67.7 0.7 collective-permute-done.16.refs_11_
  68.4 1.0 collective-permute-start.17
  69.3 0.9 collective-permute-done.17.refs_12_
  70.2 5.3 %shard_map.71 = (f32[32,128]{1,0:T(8,128)S(1)}, f32[8,128]{1,0:T(8,128)S(1)}, f32[128,128]{1,0:T(8,128)S(1)}, f32[512,128]{1,0:T(8,128)S(1)}, f32[512,128]{1,0:T(8,128)S(1)}) custom-call(s32[3072]{0:T(1024)S(1)} %bitcast.17, s32[1]{0:T(128)} %get-tuple-element.33.refs_1_, bf16[4224,128]{1,0:T(8,128)(2,1)S(1)} %shard_map.69.refs_2_, ...), custom_call_target="tpu_custom_call" | custom-call | flops 100000000 | bytes 1048576 | tf_op jit(solution)/shard_map/pallas_call | solution.py:467
  75.5 2.8 %collective-permute-start.20 = (f32[32,128]{1,0:T(8,128)S(1)}, f32[32,128]{1,0:T(8,128)S(1)}, u32[]{:S(2)}, u32[]{:S(2)}) collective-permute-start(f32[32,128]{1,0:T(8,128)S(1)} %get-tuple-element.51), channel_id=1, source_target_pairs={{0,12},{4,8},{8,4},{12,0},{1,13},{5,9},{9,5},{13,1},{2,14},{6,10},... | collective-permute-start | bytes 49160 | tf_op jit(solution)/shard_map/ppermute | solution.py:49
  78.3 1.7 %collective-permute-start.18 = (f32[32,128]{1,0:T(8,128)S(1)}, f32[32,128]{1,0:T(8,128)S(1)}, u32[]{:S(2)}, u32[]{:S(2)}) collective-permute-start(f32[32,128]{1,0:T(8,128)S(1)} %get-tuple-element.51), channel_id=1, source_target_pairs={{0,4},{4,0},{8,12},{12,8},{1,5},{5,1},{9,13},{13,9},{2,6},{6,2},{1... | collective-permute-start | bytes 49160 | tf_op jit(solution)/shard_map/ppermute | solution.py:49
  80.0 2.3 %collective-permute-done.18 = f32[32,128]{1,0:T(8,128)S(1)} collective-permute-done((f32[32,128]{1,0:T(8,128)S(1)}, f32[32,128]{1,0:T(8,128)S(1)}, u32[]{:S(2)}, u32[]{:S(2)}) %collective-permute-start.18) | collective-permute-done | bytes 16416 | tf_op jit(solution)/shard_map/ppermute | solution.py:49
  82.2 0.7 collective-permute-done.19
  83.0 1.9 %collective-permute-start.22 = (f32[128,128]{1,0:T(8,128)S(1)}, f32[128,128]{1,0:T(8,128)S(1)}, u32[]{:S(2)}, u32[]{:S(2)}) collective-permute-start(f32[128,128]{1,0:T(8,128)S(1)} %constant_dynamic-update-slice_fusion.4.refs_9_), channel_id=1, source_target_pairs={{0,2},{2,0},{1,3},{3,1},{4,6},{6,4},{5,7},{7,5},{8,10},{10,8},{9,1... | collective-permute-start | bytes 196616 | tf_op jit(solution)/shard_map/ppermute | solution.py:49
  84.8 2.5 %collective-permute-done.22.refs_11_ = f32[128,128]{1,0:T(8,128)S(1)} collective-permute-done((f32[128,128]{1,0:T(8,128)S(1)}, f32[128,128]{1,0:T(8,128)S(1)}, u32[]{:S(2)}, u32[]{:S(2)}) %collective-permute-start.22) | collective-permute-done | bytes 65568 | tf_op jit(solution)/shard_map/ppermute | solution.py:49
  87.3 1.2 %collective-permute-done.23.refs_12_ = f32[128,128]{1,0:T(8,128)S(1)} collective-permute-done((f32[128,128]{1,0:T(8,128)S(1)}, f32[128,128]{1,0:T(8,128)S(1)}, u32[]{:S(2)}, u32[]{:S(2)}) %collective-permute-start.23) | collective-permute-done | bytes 65568 | tf_op jit(solution)/shard_map/ppermute | solution.py:49
  88.6 5.4 %shard_map.72 = (f32[32,128]{1,0:T(8,128)S(1)}, f32[8,128]{1,0:T(8,128)S(1)}, f32[128,128]{1,0:T(8,128)S(1)}, f32[128,128]{1,0:T(8,128)S(1)}, f32[128,128]{1,0:T(8,128)S(1)}, /*index=5*/f32[8,128]{1,0:T(8,128)S(1)}) custom-call(s32[3072]{0:T(1024)S(1)} %bitcast.18, s32[1]{0:T(128)} %get-tuple-element.33.refs_1_, bf16[4224,128]{1,0:T(8,128)(2,1)S(1)} %shard_map.69.refs_2_, ...), custom_call_target="tpu_custom_call" | custom-call | flops 100000000 | bytes 1048576 | tf_op jit(solution)/shard_map/pallas_call | solution.py:467
  93.9 3.1 %collective-permute-start.26 = (f32[8,128]{1,0:T(8,128)S(1)}, f32[8,128]{1,0:T(8,128)S(1)}, u32[]{:S(2)}, u32[]{:S(2)}) collective-permute-start(f32[8,128]{1,0:T(8,128)S(1)} %get-tuple-element.57), channel_id=1, source_target_pairs={{0,12},{4,8},{8,4},{12,0},{1,13},{5,9},{9,5},{13,1},{2,14},{6,10},... | collective-permute-start | bytes 12296 | tf_op jit(solution)/shard_map/ppermute | solution.py:49
  97.1 1.3 %collective-permute-start.24 = (f32[8,128]{1,0:T(8,128)S(1)}, f32[8,128]{1,0:T(8,128)S(1)}, u32[]{:S(2)}, u32[]{:S(2)}) collective-permute-start(f32[8,128]{1,0:T(8,128)S(1)} %get-tuple-element.57), channel_id=1, source_target_pairs={{0,4},{4,0},{8,12},{12,8},{1,5},{5,1},{9,13},{13,9},{2,6},{6,2},{1... | collective-permute-start | bytes 12296 | tf_op jit(solution)/shard_map/ppermute | solution.py:49
  98.4 2.3 %collective-permute-done.24 = f32[8,128]{1,0:T(8,128)S(1)} collective-permute-done((f32[8,128]{1,0:T(8,128)S(1)}, f32[8,128]{1,0:T(8,128)S(1)}, u32[]{:S(2)}, u32[]{:S(2)}) %collective-permute-start.24) | collective-permute-done | bytes 4128 | tf_op jit(solution)/shard_map/ppermute | solution.py:49
  100.7 0.9 collective-permute-done.25
  101.6 1.9 %collective-permute-start.28 = (f32[64,128]{1,0:T(8,128)S(1)}, f32[64,128]{1,0:T(8,128)S(1)}, u32[]{:S(2)}, u32[]{:S(2)}) collective-permute-start(f32[64,128]{1,0:T(8,128)S(1)} %constant_dynamic-update-slice_fusion.8.refs_4_), channel_id=1, source_target_pairs={{0,2},{2,0},{1,3},{3,1},{4,6},{6,4},{5,7},{7,5},{8,10},{10,8},{9,1... | collective-permute-start | bytes 98312 | tf_op jit(solution)/shard_map/ppermute | solution.py:49
  103.5 2.1 %collective-permute-done.28.refs_6_ = f32[64,128]{1,0:T(8,128)S(1)} collective-permute-done((f32[64,128]{1,0:T(8,128)S(1)}, f32[64,128]{1,0:T(8,128)S(1)}, u32[]{:S(2)}, u32[]{:S(2)}) %collective-permute-start.28) | collective-permute-done | bytes 32800 | tf_op jit(solution)/shard_map/ppermute | solution.py:49
  105.6 1.2 %collective-permute-done.29.refs_7_ = f32[64,128]{1,0:T(8,128)S(1)} collective-permute-done((f32[64,128]{1,0:T(8,128)S(1)}, f32[64,128]{1,0:T(8,128)S(1)}, u32[]{:S(2)}, u32[]{:S(2)}) %collective-permute-start.29) | collective-permute-done | bytes 32800 | tf_op jit(solution)/shard_map/ppermute | solution.py:49
  106.8 0.7 shard_map.73
  (37 shorter events, 0.1 us)
Async XLA Ops:
  2.0 11.3 %collective-permute-start.2 = (s32[4,128]{1,0:T(4,128)S(1)}, s32[4,128]{1,0:T(4,128)S(1)}, u32[]{:S(2)}, u32[]{:S(2)}) collective-permute-start(s32[4,128]{1,0:T(4,128)S(1)} %reshape.28), channel_id=1, source_target_pairs={{0,12},{4,8},{8,4},{12,0},{1,13},{5,9},{9,5},{13,1},{2,14},{6,10},... | collective-permute-start | bytes 6152 | tf_op jit(solution)/shard_map/ppermute | solution.py:49
  7.0 6.8 %collective-permute-start.1 = (s32[4,128]{1,0:T(4,128)S(1)}, s32[4,128]{1,0:T(4,128)S(1)}, u32[]{:S(2)}, u32[]{:S(2)}) collective-permute-start(s32[4,128]{1,0:T(4,128)S(1)} %reshape.28), channel_id=1, source_target_pairs={{0,8},{4,12},{8,0},{12,4},{1,9},{5,13},{9,1},{13,5},{2,10},{6,14},... | collective-permute-start | bytes 6152 | tf_op jit(solution)/shard_map/ppermute | solution.py:49
  7.0 6.8 %collective-permute-start = (s32[4,128]{1,0:T(4,128)S(1)}, s32[4,128]{1,0:T(4,128)S(1)}, u32[]{:S(2)}, u32[]{:S(2)}) collective-permute-start(s32[4,128]{1,0:T(4,128)S(1)} %reshape.28), channel_id=1, source_target_pairs={{0,4},{4,0},{8,12},{12,8},{1,5},{5,1},{9,13},{13,9},{2,6},{6,2},{1... | collective-permute-start | bytes 6152 | tf_op jit(solution)/shard_map/ppermute | solution.py:49
  9.4 11.6 %collective-permute-start.8 = (f32[256,128]{1,0:T(8,128)S(1)}, f32[256,128]{1,0:T(8,128)S(1)}, u32[]{:S(2)}, u32[]{:S(2)}) collective-permute-start(f32[256,128]{1,0:T(8,128)S(1)} %bitcast.22), channel_id=1, source_target_pairs={{0,12},{4,8},{8,4},{12,0},{1,13},{5,9},{9,5},{13,1},{2,14},{6,10},... | collective-permute-start | bytes 393224 | tf_op jit(solution)/shard_map/ppermute | solution.py:49
  13.2 10.2 %collective-permute-start.7 = (f32[256,128]{1,0:T(8,128)S(1)}, f32[256,128]{1,0:T(8,128)S(1)}, u32[]{:S(2)}, u32[]{:S(2)}) collective-permute-start(f32[256,128]{1,0:T(8,128)S(1)} %bitcast.23), channel_id=1, source_target_pairs={{0,8},{4,12},{8,0},{12,4},{1,9},{5,13},{9,1},{13,5},{2,10},{6,14},... | collective-permute-start | bytes 393224 | tf_op jit(solution)/shard_map/ppermute | solution.py:49
  13.2 10.2 %collective-permute-start.6 = (f32[256,128]{1,0:T(8,128)S(1)}, f32[256,128]{1,0:T(8,128)S(1)}, u32[]{:S(2)}, u32[]{:S(2)}) collective-permute-start(f32[256,128]{1,0:T(8,128)S(1)} %bitcast.24), channel_id=1, source_target_pairs={{0,4},{4,0},{8,12},{12,8},{1,5},{5,1},{9,13},{13,9},{2,6},{6,2},{1... | collective-permute-start | bytes 393224 | tf_op jit(solution)/shard_map/ppermute | solution.py:49
  13.9 3.7 %collective-permute-start.4 = (s32[16,128]{1,0:T(8,128)S(1)}, s32[16,128]{1,0:T(8,128)S(1)}, u32[]{:S(2)}, u32[]{:S(2)}) collective-permute-start(s32[16,128]{1,0:T(8,128)S(1)} %pad_add_fusion.refs_0_), channel_id=1, source_target_pairs={{0,2},{2,0},{1,3},{3,1},{4,6},{6,4},{5,7},{7,5},{8,10},{10,8},{9,1... | collective-permute-start | bytes 24584 | tf_op jit(solution)/shard_map/ppermute | solution.py:49
  15.6 2.4 %collective-permute-start.3 = (s32[16,128]{1,0:T(8,128)S(1)}, s32[16,128]{1,0:T(8,128)S(1)}, u32[]{:S(2)}, u32[]{:S(2)}) collective-permute-start(s32[16,128]{1,0:T(8,128)S(1)} %pad_add_fusion.refs_0_), channel_id=1, source_target_pairs={{0,1},{1,0},{2,3},{3,2},{4,5},{5,4},{6,7},{7,6},{8,9},{9,8},{10,11... | collective-permute-start | bytes 24584 | tf_op jit(solution)/shard_map/ppermute | solution.py:49
  17.6 1.2 %collective-permute-start.5 = (s32[16,128]{1,0:T(8,128)S(1)}, s32[16,128]{1,0:T(8,128)S(1)}, u32[]{:S(2)}, u32[]{:S(2)}) collective-permute-start(s32[16,128]{1,0:T(8,128)S(1)} %collective-permute-done.4.refs_2_), channel_id=1, source_target_pairs={{0,1},{1,0},{2,3},{3,2},{4,5},{5,4},{6,7},{7,6},{8,9},{9,8},{10,11... | collective-permute-start | bytes 24584 | tf_op jit(solution)/shard_map/ppermute | solution.py:49
  23.4 1.3 %collective-permute-start.9 = (f32[256,128]{1,0:T(8,128)S(1)}, f32[256,128]{1,0:T(8,128)S(1)}, u32[]{:S(2)}, u32[]{:S(2)}) collective-permute-start(f32[256,128]{1,0:T(8,128)S(1)} %collective-permute-done.6.refs_6_), channel_id=1, source_target_pairs={{0,1},{1,0},{2,3},{3,2},{4,5},{5,4},{6,7},{7,6},{8,9},{9,8},{10,11... | collective-permute-start | bytes 393224 | tf_op jit(solution)/shard_map/ppermute | solution.py:49
  23.4 1.5 %collective-permute-start.10 = (f32[256,128]{1,0:T(8,128)S(1)}, f32[256,128]{1,0:T(8,128)S(1)}, u32[]{:S(2)}, u32[]{:S(2)}) collective-permute-start(f32[256,128]{1,0:T(8,128)S(1)} %collective-permute-done.7.refs_8_), channel_id=1, source_target_pairs={{0,1},{1,0},{2,3},{3,2},{4,5},{5,4},{6,7},{7,6},{8,9},{9,8},{10,11... | collective-permute-start | bytes 393224 | tf_op jit(solution)/shard_map/ppermute | solution.py:49
  23.9 1.3 %collective-permute-start.11 = (f32[256,128]{1,0:T(8,128)S(1)}, f32[256,128]{1,0:T(8,128)S(1)}, u32[]{:S(2)}, u32[]{:S(2)}) collective-permute-start(f32[256,128]{1,0:T(8,128)S(1)} %collective-permute-done.8.refs_10_), channel_id=1, source_target_pairs={{0,1},{1,0},{2,3},{3,2},{4,5},{5,4},{6,7},{7,6},{8,9},{9,8},{10,11... | collective-permute-start | bytes 393224 | tf_op jit(solution)/shard_map/ppermute | solution.py:49
  48.1 16.0 %collective-permute-start.14 = (f32[32,128]{1,0:T(8,128)S(1)}, f32[32,128]{1,0:T(8,128)S(1)}, u32[]{:S(2)}, u32[]{:S(2)}) collective-permute-start(f32[32,128]{1,0:T(8,128)S(1)} %get-tuple-element.42), channel_id=1, source_target_pairs={{0,12},{4,8},{8,4},{12,0},{1,13},{5,9},{9,5},{13,1},{2,14},{6,10},... | collective-permute-start | bytes 49160 | tf_op jit(solution)/shard_map/ppermute | solution.py:49
  59.4 4.6 %collective-permute-start.13 = (f32[32,128]{1,0:T(8,128)S(1)}, f32[32,128]{1,0:T(8,128)S(1)}, u32[]{:S(2)}, u32[]{:S(2)}) collective-permute-start(f32[32,128]{1,0:T(8,128)S(1)} %get-tuple-element.42), channel_id=1, source_target_pairs={{0,8},{4,12},{8,0},{12,4},{1,9},{5,13},{9,1},{13,5},{2,10},{6,14},... | collective-permute-start | bytes 49160 | tf_op jit(solution)/shard_map/ppermute | solution.py:49
  59.4 3.7 %collective-permute-start.12 = (f32[32,128]{1,0:T(8,128)S(1)}, f32[32,128]{1,0:T(8,128)S(1)}, u32[]{:S(2)}, u32[]{:S(2)}) collective-permute-start(f32[32,128]{1,0:T(8,128)S(1)} %get-tuple-element.42), channel_id=1, source_target_pairs={{0,4},{4,0},{8,12},{12,8},{1,5},{5,1},{9,13},{13,9},{2,6},{6,2},{1... | collective-permute-start | bytes 49160 | tf_op jit(solution)/shard_map/ppermute | solution.py:49
  64.1 4.3 %collective-permute-start.16 = (f32[128,128]{1,0:T(8,128)S(1)}, f32[128,128]{1,0:T(8,128)S(1)}, u32[]{:S(2)}, u32[]{:S(2)}) collective-permute-start(f32[128,128]{1,0:T(8,128)S(1)} %constant_dynamic-update-slice_fusion.refs_9_), channel_id=1, source_target_pairs={{0,2},{2,0},{1,3},{3,1},{4,6},{6,4},{5,7},{7,5},{8,10},{10,8},{9,1... | collective-permute-start | bytes 196616 | tf_op jit(solution)/shard_map/ppermute | solution.py:49
  65.4 3.9 %collective-permute-start.15 = (f32[128,128]{1,0:T(8,128)S(1)}, f32[128,128]{1,0:T(8,128)S(1)}, u32[]{:S(2)}, u32[]{:S(2)}) collective-permute-start(f32[128,128]{1,0:T(8,128)S(1)} %constant_dynamic-update-slice_fusion.refs_9_), channel_id=1, source_target_pairs={{0,1},{1,0},{2,3},{3,2},{4,5},{5,4},{6,7},{7,6},{8,9},{9,8},{10,11... | collective-permute-start | bytes 196616 | tf_op jit(solution)/shard_map/ppermute | solution.py:49
  68.4 1.9 %collective-permute-start.17 = (f32[128,128]{1,0:T(8,128)S(1)}, f32[128,128]{1,0:T(8,128)S(1)}, u32[]{:S(2)}, u32[]{:S(2)}) collective-permute-start(f32[128,128]{1,0:T(8,128)S(1)} %collective-permute-done.16.refs_11_), channel_id=1, source_target_pairs={{0,1},{1,0},{2,3},{3,2},{4,5},{5,4},{6,7},{7,6},{8,9},{9,8},{10,11... | collective-permute-start | bytes 196616 | tf_op jit(solution)/shard_map/ppermute | solution.py:49
  75.5 7.4 %collective-permute-start.20 = (f32[32,128]{1,0:T(8,128)S(1)}, f32[32,128]{1,0:T(8,128)S(1)}, u32[]{:S(2)}, u32[]{:S(2)}) collective-permute-start(f32[32,128]{1,0:T(8,128)S(1)} %get-tuple-element.51), channel_id=1, source_target_pairs={{0,12},{4,8},{8,4},{12,0},{1,13},{5,9},{9,5},{13,1},{2,14},{6,10},... | collective-permute-start | bytes 49160 | tf_op jit(solution)/shard_map/ppermute | solution.py:49
  78.3 4.6 %collective-permute-start.19 = (f32[32,128]{1,0:T(8,128)S(1)}, f32[32,128]{1,0:T(8,128)S(1)}, u32[]{:S(2)}, u32[]{:S(2)}) collective-permute-start(f32[32,128]{1,0:T(8,128)S(1)} %get-tuple-element.51), channel_id=1, source_target_pairs={{0,8},{4,12},{8,0},{12,4},{1,9},{5,13},{9,1},{13,5},{2,10},{6,14},... | collective-permute-start | bytes 49160 | tf_op jit(solution)/shard_map/ppermute | solution.py:49
  78.3 3.9 %collective-permute-start.18 = (f32[32,128]{1,0:T(8,128)S(1)}, f32[32,128]{1,0:T(8,128)S(1)}, u32[]{:S(2)}, u32[]{:S(2)}) collective-permute-start(f32[32,128]{1,0:T(8,128)S(1)} %get-tuple-element.51), channel_id=1, source_target_pairs={{0,4},{4,0},{8,12},{12,8},{1,5},{5,1},{9,13},{13,9},{2,6},{6,2},{1... | collective-permute-start | bytes 49160 | tf_op jit(solution)/shard_map/ppermute | solution.py:49
  83.0 4.3 %collective-permute-start.22 = (f32[128,128]{1,0:T(8,128)S(1)}, f32[128,128]{1,0:T(8,128)S(1)}, u32[]{:S(2)}, u32[]{:S(2)}) collective-permute-start(f32[128,128]{1,0:T(8,128)S(1)} %constant_dynamic-update-slice_fusion.4.refs_9_), channel_id=1, source_target_pairs={{0,2},{2,0},{1,3},{3,1},{4,6},{6,4},{5,7},{7,5},{8,10},{10,8},{9,1... | collective-permute-start | bytes 196616 | tf_op jit(solution)/shard_map/ppermute | solution.py:49
  84.8 2.5 %collective-permute-start.21 = (f32[128,128]{1,0:T(8,128)S(1)}, f32[128,128]{1,0:T(8,128)S(1)}, u32[]{:S(2)}, u32[]{:S(2)}) collective-permute-start(f32[128,128]{1,0:T(8,128)S(1)} %constant_dynamic-update-slice_fusion.4.refs_9_), channel_id=1, source_target_pairs={{0,1},{1,0},{2,3},{3,2},{4,5},{5,4},{6,7},{7,6},{8,9},{9,8},{10,11... | collective-permute-start | bytes 196616 | tf_op jit(solution)/shard_map/ppermute | solution.py:49
  87.3 1.3 %collective-permute-start.23 = (f32[128,128]{1,0:T(8,128)S(1)}, f32[128,128]{1,0:T(8,128)S(1)}, u32[]{:S(2)}, u32[]{:S(2)}) collective-permute-start(f32[128,128]{1,0:T(8,128)S(1)} %collective-permute-done.22.refs_11_), channel_id=1, source_target_pairs={{0,1},{1,0},{2,3},{3,2},{4,5},{5,4},{6,7},{7,6},{8,9},{9,8},{10,11... | collective-permute-start | bytes 196616 | tf_op jit(solution)/shard_map/ppermute | solution.py:49
  93.9 7.6 %collective-permute-start.26 = (f32[8,128]{1,0:T(8,128)S(1)}, f32[8,128]{1,0:T(8,128)S(1)}, u32[]{:S(2)}, u32[]{:S(2)}) collective-permute-start(f32[8,128]{1,0:T(8,128)S(1)} %get-tuple-element.57), channel_id=1, source_target_pairs={{0,12},{4,8},{8,4},{12,0},{1,13},{5,9},{9,5},{13,1},{2,14},{6,10},... | collective-permute-start | bytes 12296 | tf_op jit(solution)/shard_map/ppermute | solution.py:49
  97.1 4.5 %collective-permute-start.25 = (f32[8,128]{1,0:T(8,128)S(1)}, f32[8,128]{1,0:T(8,128)S(1)}, u32[]{:S(2)}, u32[]{:S(2)}) collective-permute-start(f32[8,128]{1,0:T(8,128)S(1)} %get-tuple-element.57), channel_id=1, source_target_pairs={{0,8},{4,12},{8,0},{12,4},{1,9},{5,13},{9,1},{13,5},{2,10},{6,14},... | collective-permute-start | bytes 12296 | tf_op jit(solution)/shard_map/ppermute | solution.py:49
  97.1 3.6 %collective-permute-start.24 = (f32[8,128]{1,0:T(8,128)S(1)}, f32[8,128]{1,0:T(8,128)S(1)}, u32[]{:S(2)}, u32[]{:S(2)}) collective-permute-start(f32[8,128]{1,0:T(8,128)S(1)} %get-tuple-element.57), channel_id=1, source_target_pairs={{0,4},{4,0},{8,12},{12,8},{1,5},{5,1},{9,13},{13,9},{2,6},{6,2},{1... | collective-permute-start | bytes 12296 | tf_op jit(solution)/shard_map/ppermute | solution.py:49
  101.6 4.0 %collective-permute-start.28 = (f32[64,128]{1,0:T(8,128)S(1)}, f32[64,128]{1,0:T(8,128)S(1)}, u32[]{:S(2)}, u32[]{:S(2)}) collective-permute-start(f32[64,128]{1,0:T(8,128)S(1)} %constant_dynamic-update-slice_fusion.8.refs_4_), channel_id=1, source_target_pairs={{0,2},{2,0},{1,3},{3,1},{4,6},{6,4},{5,7},{7,5},{8,10},{10,8},{9,1... | collective-permute-start | bytes 98312 | tf_op jit(solution)/shard_map/ppermute | solution.py:49
  103.5 2.1 %collective-permute-start.27 = (f32[64,128]{1,0:T(8,128)S(1)}, f32[64,128]{1,0:T(8,128)S(1)}, u32[]{:S(2)}, u32[]{:S(2)}) collective-permute-start(f32[64,128]{1,0:T(8,128)S(1)} %constant_dynamic-update-slice_fusion.8.refs_4_), channel_id=1, source_target_pairs={{0,1},{1,0},{2,3},{3,2},{4,5},{5,4},{6,7},{7,6},{8,9},{9,8},{10,11... | collective-permute-start | bytes 98312 | tf_op jit(solution)/shard_map/ppermute | solution.py:49
  105.5 1.2 %collective-permute-start.29 = (f32[64,128]{1,0:T(8,128)S(1)}, f32[64,128]{1,0:T(8,128)S(1)}, u32[]{:S(2)}, u32[]{:S(2)}) collective-permute-start(f32[64,128]{1,0:T(8,128)S(1)} %collective-permute-done.28.refs_6_), channel_id=1, source_target_pairs={{0,1},{1,0},{2,3},{3,2},{4,5},{5,4},{6,7},{7,6},{8,9},{9,8},{10,11... | collective-permute-start | bytes 98312 | tf_op jit(solution)/shard_map/ppermute | solution.py:49
where the time goes:
time: 107 us
  starting transfers between devices  41.6 us (39%)
  Pallas kernels  36.6 us (34%)
  waiting for transfers between devices  25.3 us (24%)
  other arithmetic  1.48 us (1%)
  between operations  1.39 us (1%)
    ppermute x30, starting transfers between devices, swap(): lax.ppermute(x, axis, [(i, i ^ code) for i in range(lax.axis_size(axis))])  41.6 us
    pallas_call x6, Pallas kernels, call(): pl.pallas_call(kernel, in_specs=in_specs, out_shape=shapes, out_specs=out...  36.6 us
    ppermute x30, waiting for transfers between devices, swap(): lax.ppermute(x, axis, [(i, i ^ code) for i in range(lax.axis_size(axis))])  25.3 us
  transfers between devices with their start and end apart: 30, of which 18 were waited for; matrix products, arithmetic and copies ran while one was open for 2% of the time, Pallas kernels for 2%

commit v1 on v0

--- a/solution.py
+++ b/solution.py
@@ -220,8 +220,8 @@
     return jnp.bitwise_and(entry, 255), lax.shift_right_logical(entry, 8)
 
 
-def squared_of(features, *others):
-    return jnp.dot(features, jnp.concatenate(others, axis=1), preferred_element_type=F32)
+def squared_of(features, others):
+    return jnp.dot(features, others, preferred_element_type=F32)
 
 
 def taper_of(squared):
@@ -258,25 +258,21 @@
     top = jnp.maximum(lax.div(count + (UNROLL - 1), UNROLL) - 1, 0)
 
     def squared(g, u):
-        k = jnp.minimum(g, top) * UNROLL + u
-        i, j = entry_of(list_ref, k)
-        unused, twin = entry_of(list_ref, k + 1)
-        return squared_of(own_features(lhs_ref, i), other_features(rhs_ref, j), other_features(rhs_ref, twin))
-
-    def fill(u, both):
-        squares[u * BS : (u + 1) * BS, :] = both[:, :BS]
-        squares[(u + 1) * BS : (u + 2) * BS, :] = both[:, BS:]
-
-    for u in range(0, UNROLL, 2):
-        fill(u, squared(0, u))
+        i, j = entry_of(list_ref, jnp.minimum(g, top) * UNROLL + u)
+        return squared_of(own_features(lhs_ref, i), other_features(rhs_ref, j))
+
+    for u in range(UNROLL):
+        squares[u * BS : (u + 1) * BS, :] = squared(0, u)
     for at, tile_ref in enumerate(tile_refs):
 
         def group(g, unused, at=at, tile_ref=tile_ref):
-            for u in range(0, UNROLL, 2):
-                tiles = taper_of(squares[u * BS : (u + 2) * BS, :])
-                fill(u, squared(g + 1, u))
+            for u in range(UNROLL):
+                following = squared(g + 1, u)
                 start = pl.multiple_of((g * UNROLL + u - at * sz.kept) * BS, BS)
-                tile_ref[pl.ds(start, 2 * BS), :] = tiles
+                for r in range(0, BS, 8):
+                    here = slice(u * BS + r, u * BS + r + 8)
+                    tile_ref[pl.ds(start + r, 8), :] = taper_of(squares[here, :])
+                    squares[here, :] = following[r : r + 8, :]
             return unused
 
         lax.fori_loop(*kept_groups(sz, count, at), group, 0)
@@ -285,24 +281,29 @@
 def sweep(sz, list_ref, count, tile_refs, vec_ref, acc, acc_ones=None):
     accs = [acc] if acc_ones is None else [acc, acc_ones]
     clear(*accs)
-    carry = (jnp.int32(-1),) + tuple(jnp.zeros((BS, BS), F32) for unused in accs)
+    zero = jnp.zeros((8, BS), F32)
+    carry = (jnp.int32(-1),) + ((zero,) * (BS // 8),) * len(accs)
     for at, tile_ref in enumerate(tile_refs):
 
         def group(g, carry, at=at, tile_ref=tile_ref):
             before, *totals = carry
+            totals = [list(total) for total in totals]
             for u in range(0, UNROLL, 2):
                 i, j = entry_of(list_ref, g * UNROLL + u)
                 unused, twin = entry_of(list_ref, g * UNROLL + u + 1)
                 keep = jnp.where(i == before, 1.0, 0.0)
-                start = (g * UNROLL + u - at * sz.kept) * BS
-                tile = tile_ref[pl.ds(pl.multiple_of(start, BS), BS), :]
-                twin_tile = tile_ref[pl.ds(pl.multiple_of(start + BS, BS), BS), :]
-                terms = [tile * vector_row(vec_ref, j) + twin_tile * vector_row(vec_ref, twin), tile + twin_tile]
-                totals = [total * keep + term for total, term in zip(totals, terms)]
-                for ref, total in zip(accs, totals):
-                    ref[pl.ds(pl.multiple_of(i * BS, BS), BS), :] = total
+                start = pl.multiple_of((g * UNROLL + u - at * sz.kept) * BS, BS)
+                base = pl.multiple_of(i * BS, BS)
+                row = jnp.broadcast_to(vector_row(vec_ref, j), (8, BS))
+                twin_row = jnp.broadcast_to(vector_row(vec_ref, twin), (8, BS))
+                for k in range(BS // 8):
+                    tile = tile_ref[pl.ds(start + 8 * k, 8), :]
+                    twin_tile = tile_ref[pl.ds(start + BS + 8 * k, 8), :]
+                    for ref, total, term in zip(accs, totals, (tile * row + twin_tile * twin_row, tile + twin_tile)):
+                        total[k] = total[k] * keep + term
+                        ref[pl.ds(base + 8 * k, 8), :] = total[k]
                 before = i
-            return (before, *totals)
+            return (before, *(tuple(total) for total in totals))
 
         carry = lax.fori_loop(*kept_groups(sz, count, at), group, carry)
 

time: 107 us -> 106 us (level); the launches traced: 107 us -> 105 us
  starting transfers between devices: 41.6 us -> 31.2 us
  Pallas kernels: 36.6 us -> 46.6 us
  waiting for transfers between devices: 25.3 us -> 23.6 us
    ppermute x30, starting transfers between devices: 41.6 us -> 31.2 us  [swap(): lax.ppermute(x, axis, [(i, i ^ code) for i in range(lax.axis_size(axis))])]
    pallas_call x6, Pallas kernels: 36.6 us -> 46.6 us  [call(): pl.pallas_call(kernel, in_specs=in_specs, out_shape=shapes, out_specs=out...]
    ppermute x30, waiting for transfers between devices: 25.3 us -> 23.6 us  [swap(): lax.ppermute(x, axis, [(i, i ^ code) for i in range(lax.axis_size(axis))])]
  transfers between devices with their start and end apart: 30 -> 30, of which waited for: 18 -> 15; matrix products, arithmetic and copies ran while one was open for 2% -> 2% of each run, Pallas kernels for 2% -> 3%
where the time goes in v1:
time: 106 us; the launch traced here: 105 us
  Pallas kernels  46.6 us (44%)
  starting transfers between devices  31.2 us (29%)
  waiting for transfers between devices  23.6 us (22%)
  other arithmetic  1.48 us (1%)
  between operations  1.43 us (1%)
    pallas_call x6, Pallas kernels, call(): pl.pallas_call(kernel, in_specs=in_specs, out_shape=shapes, out_specs=out...  46.6 us
    ppermute x30, starting transfers between devices, swap(): lax.ppermute(x, axis, [(i, i ^ code) for i in range(lax.axis_size(axis))])  31.2 us
    ppermute x30, waiting for transfers between devices, swap(): lax.ppermute(x, axis, [(i, i ^ code) for i in range(lax.axis_size(axis))])  23.6 us
  transfers between devices with their start and end apart: 30, of which 15 were waited for; matrix products, arithmetic and copies ran while one was open for 2% of the time, Pallas kernels for 3%

profile of v1, /device:TPU:0, one launch (start us, length us, event | category | flops | bytes accessed | tf_op | source)
XLA Modules:
  0.0 105.3 jit_solution(11079665107457615465)
XLA Ops:
  1.3 0.7 broadcast_select_fusion
  2.0 5.0 %collective-permute-start.2 = (s32[4,128]{1,0:T(4,128)S(1)}, s32[4,128]{1,0:T(4,128)S(1)}, u32[]{:S(2)}, u32[]{:S(2)}) collective-permute-start(s32[4,128]{1,0:T(4,128)S(1)} %reshape.28), channel_id=1, source_target_pairs={{0,12},{4,8},{8,4},{12,0},{1,13},{5,9},{9,5},{13,1},{2,14},{6,10},... | collective-permute-start | bytes 6152 | tf_op jit(solution)/shard_map/ppermute | solution.py:49
  7.0 0.0 collective-permute-start.1
  7.0 0.6 collective-permute-start
  7.7 1.0 copy.9
  8.6 0.8 fusion
  9.4 3.8 %collective-permute-start.8 = (f32[256,128]{1,0:T(8,128)S(1)}, f32[256,128]{1,0:T(8,128)S(1)}, u32[]{:S(2)}, u32[]{:S(2)}) collective-permute-start(f32[256,128]{1,0:T(8,128)S(1)} %bitcast.22), channel_id=1, source_target_pairs={{0,12},{4,8},{8,4},{12,0},{1,13},{5,9},{9,5},{13,1},{2,14},{6,10},... | collective-permute-start | bytes 393224 | tf_op jit(solution)/shard_map/ppermute | solution.py:49
  13.2 0.6 collective-permute-start.6
  13.9 1.7 %collective-permute-start.4 = (s32[16,128]{1,0:T(8,128)S(1)}, s32[16,128]{1,0:T(8,128)S(1)}, u32[]{:S(2)}, u32[]{:S(2)}) collective-permute-start(s32[16,128]{1,0:T(8,128)S(1)} %pad_add_fusion.refs_0_), channel_id=1, source_target_pairs={{0,2},{2,0},{1,3},{3,1},{4,6},{6,4},{5,7},{7,5},{8,10},{10,8},{9,1... | collective-permute-start | bytes 24584 | tf_op jit(solution)/shard_map/ppermute | solution.py:49
  15.6 2.0 %collective-permute-done.4.refs_2_ = s32[16,128]{1,0:T(8,128)S(1)} collective-permute-done((s32[16,128]{1,0:T(8,128)S(1)}, s32[16,128]{1,0:T(8,128)S(1)}, u32[]{:S(2)}, u32[]{:S(2)}) %collective-permute-start.4) | collective-permute-done | bytes 8224 | tf_op jit(solution)/shard_map/ppermute | solution.py:49
  17.6 0.0 collective-permute-start.5
  17.6 0.4 shard_map.69.refs_2_
  18.0 0.0 collective-permute-done.3.refs_1_
  18.0 0.8 collective-permute-done.5.refs_3_
  18.8 2.8 %shard_map.68 = (s32[24,128]{1,0:T(8,128)S(1)}, s32[1]{0:T(128)}) custom-call(s32[16,128]{1,0:T(8,128)S(1)} %pad_add_fusion.refs_0_, s32[16,128]{1,0:T(8,128)S(1)} %collective-permute-done.3.refs_1_, s32[16,128]{1,0:T(8,128)S(1)} %collective-permute-done.4.refs_2_, s32[16,128]{1,0:T(8,128)S(1)} %collective-permute-done.5.refs_3_), custom_call_target="tpu_custom_call" | custom-call | flops 10000000 | bytes 1048576 | tf_op jit(solution)/shard_map/pallas_call | solution.py:468
  21.6 1.9 %collective-permute-done.7.refs_8_ = f32[256,128]{1,0:T(8,128)S(1)} collective-permute-done((f32[256,128]{1,0:T(8,128)S(1)}, f32[256,128]{1,0:T(8,128)S(1)}, u32[]{:S(2)}, u32[]{:S(2)}) %collective-permute-start.7) | collective-permute-done | bytes 131104 | tf_op jit(solution)/shard_map/ppermute | solution.py:49
  23.4 0.5 collective-permute-start.10
  23.9 0.0 collective-permute-start.11
  23.9 0.8 collective-permute-done.9.refs_7_
  24.8 0.2 collective-permute-done.10.refs_9_
  25.0 0.3 collective-permute-done.11.refs_11_
  25.3 30.1 %shard_map.70 = (f32[14336,128]{1,0:T(8,128)S(1)}, f32[14336,128]{1,0:T(8,128)S(1)}, f32[14336,128]{1,0:T(8,128)S(1)}, f32[14336,128]{1,0:T(8,128)S(1)}, bf16[24...) custom-call(s32[3072]{0:T(1024)S(1)} %bitcast.16, ...), custom_call_target="tpu_custom_call" | custom-call | flops 100000000 | bytes 1048576 | tf_op jit(solution)/shard_map/pallas_call | solution.py:468
  55.4 0.3 collective-permute-start.14
  55.7 2.3 %collective-permute-start.13 = (f32[32,128]{1,0:T(8,128)S(1)}, f32[32,128]{1,0:T(8,128)S(1)}, u32[]{:S(2)}, u32[]{:S(2)}) collective-permute-start(f32[32,128]{1,0:T(8,128)S(1)} %get-tuple-element.42), channel_id=1, source_target_pairs={{0,8},{4,12},{8,0},{12,4},{1,9},{5,13},{9,1},{13,5},{2,10},{6,14},... | collective-permute-start | bytes 49160 | tf_op jit(solution)/shard_map/ppermute | solution.py:49
  58.0 1.9 %collective-permute-start.12 = (f32[32,128]{1,0:T(8,128)S(1)}, f32[32,128]{1,0:T(8,128)S(1)}, u32[]{:S(2)}, u32[]{:S(2)}) collective-permute-start(f32[32,128]{1,0:T(8,128)S(1)} %get-tuple-element.42), channel_id=1, source_target_pairs={{0,4},{4,0},{8,12},{12,8},{1,5},{5,1},{9,13},{13,9},{2,6},{6,2},{1... | collective-permute-start | bytes 49160 | tf_op jit(solution)/shard_map/ppermute | solution.py:49
  59.8 1.9 %collective-permute-done.12 = f32[32,128]{1,0:T(8,128)S(1)} collective-permute-done((f32[32,128]{1,0:T(8,128)S(1)}, f32[32,128]{1,0:T(8,128)S(1)}, u32[]{:S(2)}, u32[]{:S(2)}) %collective-permute-start.12) | collective-permute-done | bytes 16416 | tf_op jit(solution)/shard_map/ppermute | solution.py:49
  61.7 0.0 collective-permute-done.13
  61.7 0.0 collective-permute-done.14
  61.7 2.3 %collective-permute-start.16 = (f32[128,128]{1,0:T(8,128)S(1)}, f32[128,128]{1,0:T(8,128)S(1)}, u32[]{:S(2)}, u32[]{:S(2)}) collective-permute-start(f32[128,128]{1,0:T(8,128)S(1)} %constant_dynamic-update-slice_fusion.refs_9_), channel_id=1, source_target_pairs={{0,2},{2,0},{1,3},{3,1},{4,6},{6,4},{5,7},{7,5},{8,10},{10,8},{9,1... | collective-permute-start | bytes 196616 | tf_op jit(solution)/shard_map/ppermute | solution.py:49
  64.0 2.2 %collective-permute-done.16.refs_11_ = f32[128,128]{1,0:T(8,128)S(1)} collective-permute-done((f32[128,128]{1,0:T(8,128)S(1)}, f32[128,128]{1,0:T(8,128)S(1)}, u32[]{:S(2)}, u32[]{:S(2)}) %collective-permute-start.16) | collective-permute-done | bytes 65568 | tf_op jit(solution)/shard_map/ppermute | solution.py:49
  66.3 1.2 %collective-permute-done.17.refs_12_ = f32[128,128]{1,0:T(8,128)S(1)} collective-permute-done((f32[128,128]{1,0:T(8,128)S(1)}, f32[128,128]{1,0:T(8,128)S(1)}, u32[]{:S(2)}, u32[]{:S(2)}) %collective-permute-start.17) | collective-permute-done | bytes 65568 | tf_op jit(solution)/shard_map/ppermute | solution.py:49
  67.5 6.3 %shard_map.71 = (f32[32,128]{1,0:T(8,128)S(1)}, f32[8,128]{1,0:T(8,128)S(1)}, f32[128,128]{1,0:T(8,128)S(1)}, f32[512,128]{1,0:T(8,128)S(1)}, f32[512,128]{1,0:T(8,128)S(1)}) custom-call(s32[3072]{0:T(1024)S(1)} %bitcast.17, s32[1]{0:T(128)} %get-tuple-element.33.refs_1_, bf16[4224,128]{1,0:T(8,128)(2,1)S(1)} %shard_map.69.refs_2_, ...), custom_call_target="tpu_custom_call" | custom-call | flops 100000000 | bytes 1048576 | tf_op jit(solution)/shard_map/pallas_call | solution.py:468
  73.9 1.8 %collective-permute-start.20 = (f32[32,128]{1,0:T(8,128)S(1)}, f32[32,128]{1,0:T(8,128)S(1)}, u32[]{:S(2)}, u32[]{:S(2)}) collective-permute-start(f32[32,128]{1,0:T(8,128)S(1)} %get-tuple-element.51), channel_id=1, source_target_pairs={{0,12},{4,8},{8,4},{12,0},{1,13},{5,9},{9,5},{13,1},{2,14},{6,10},... | collective-permute-start | bytes 49160 | tf_op jit(solution)/shard_map/ppermute | solution.py:49
  75.6 1.6 %collective-permute-start.19 = (f32[32,128]{1,0:T(8,128)S(1)}, f32[32,128]{1,0:T(8,128)S(1)}, u32[]{:S(2)}, u32[]{:S(2)}) collective-permute-start(f32[32,128]{1,0:T(8,128)S(1)} %get-tuple-element.51), channel_id=1, source_target_pairs={{0,8},{4,12},{8,0},{12,4},{1,9},{5,13},{9,1},{13,5},{2,10},{6,14},... | collective-permute-start | bytes 49160 | tf_op jit(solution)/shard_map/ppermute | solution.py:49
  77.2 1.1 %collective-permute-start.18 = (f32[32,128]{1,0:T(8,128)S(1)}, f32[32,128]{1,0:T(8,128)S(1)}, u32[]{:S(2)}, u32[]{:S(2)}) collective-permute-start(f32[32,128]{1,0:T(8,128)S(1)} %get-tuple-element.51), channel_id=1, source_target_pairs={{0,4},{4,0},{8,12},{12,8},{1,5},{5,1},{9,13},{13,9},{2,6},{6,2},{1... | collective-permute-start | bytes 49160 | tf_op jit(solution)/shard_map/ppermute | solution.py:49
  78.3 2.7 %collective-permute-done.18 = f32[32,128]{1,0:T(8,128)S(1)} collective-permute-done((f32[32,128]{1,0:T(8,128)S(1)}, f32[32,128]{1,0:T(8,128)S(1)}, u32[]{:S(2)}, u32[]{:S(2)}) %collective-permute-start.18) | collective-permute-done | bytes 16416 | tf_op jit(solution)/shard_map/ppermute | solution.py:49
  81.0 1.2 %collective-permute-start.22 = (f32[128,128]{1,0:T(8,128)S(1)}, f32[128,128]{1,0:T(8,128)S(1)}, u32[]{:S(2)}, u32[]{:S(2)}) collective-permute-start(f32[128,128]{1,0:T(8,128)S(1)} %constant_dynamic-update-slice_fusion.4.refs_9_), channel_id=1, source_target_pairs={{0,2},{2,0},{1,3},{3,1},{4,6},{6,4},{5,7},{7,5},{8,10},{10,8},{9,1... | collective-permute-start | bytes 196616 | tf_op jit(solution)/shard_map/ppermute | solution.py:49
  82.3 3.1 %collective-permute-done.22.refs_11_ = f32[128,128]{1,0:T(8,128)S(1)} collective-permute-done((f32[128,128]{1,0:T(8,128)S(1)}, f32[128,128]{1,0:T(8,128)S(1)}, u32[]{:S(2)}, u32[]{:S(2)}) %collective-permute-start.22) | collective-permute-done | bytes 65568 | tf_op jit(solution)/shard_map/ppermute | solution.py:49
  85.4 1.2 %collective-permute-done.23.refs_12_ = f32[128,128]{1,0:T(8,128)S(1)} collective-permute-done((f32[128,128]{1,0:T(8,128)S(1)}, f32[128,128]{1,0:T(8,128)S(1)}, u32[]{:S(2)}, u32[]{:S(2)}) %collective-permute-start.23) | collective-permute-done | bytes 65568 | tf_op jit(solution)/shard_map/ppermute | solution.py:49
  86.6 6.4 %shard_map.72 = (f32[32,128]{1,0:T(8,128)S(1)}, f32[8,128]{1,0:T(8,128)S(1)}, f32[128,128]{1,0:T(8,128)S(1)}, f32[128,128]{1,0:T(8,128)S(1)}, f32[128,128]{1,0:T(8,128)S(1)}, /*index=5*/f32[8,128]{1,0:T(8,128)S(1)}) custom-call(s32[3072]{0:T(1024)S(1)} %bitcast.18, s32[1]{0:T(128)} %get-tuple-element.33.refs_1_, bf16[4224,128]{1,0:T(8,128)(2,1)S(1)} %shard_map.69.refs_2_, ...), custom_call_target="tpu_custom_call" | custom-call | flops 100000000 | bytes 1048576 | tf_op jit(solution)/shard_map/pallas_call | solution.py:468
  93.0 1.4 %collective-permute-start.26 = (f32[8,128]{1,0:T(8,128)S(1)}, f32[8,128]{1,0:T(8,128)S(1)}, u32[]{:S(2)}, u32[]{:S(2)}) collective-permute-start(f32[8,128]{1,0:T(8,128)S(1)} %get-tuple-element.57), channel_id=1, source_target_pairs={{0,12},{4,8},{8,4},{12,0},{1,13},{5,9},{9,5},{13,1},{2,14},{6,10},... | collective-permute-start | bytes 12296 | tf_op jit(solution)/shard_map/ppermute | solution.py:49
  94.5 1.3 %collective-permute-start.25 = (f32[8,128]{1,0:T(8,128)S(1)}, f32[8,128]{1,0:T(8,128)S(1)}, u32[]{:S(2)}, u32[]{:S(2)}) collective-permute-start(f32[8,128]{1,0:T(8,128)S(1)} %get-tuple-element.57), channel_id=1, source_target_pairs={{0,8},{4,12},{8,0},{12,4},{1,9},{5,13},{9,1},{13,5},{2,10},{6,14},... | collective-permute-start | bytes 12296 | tf_op jit(solution)/shard_map/ppermute | solution.py:49
  95.8 1.7 %collective-permute-start.24 = (f32[8,128]{1,0:T(8,128)S(1)}, f32[8,128]{1,0:T(8,128)S(1)}, u32[]{:S(2)}, u32[]{:S(2)}) collective-permute-start(f32[8,128]{1,0:T(8,128)S(1)} %get-tuple-element.57), channel_id=1, source_target_pairs={{0,4},{4,0},{8,12},{12,8},{1,5},{5,1},{9,13},{13,9},{2,6},{6,2},{1... | collective-permute-start | bytes 12296 | tf_op jit(solution)/shard_map/ppermute | solution.py:49
  97.5 1.9 %collective-permute-done.24 = f32[8,128]{1,0:T(8,128)S(1)} collective-permute-done((f32[8,128]{1,0:T(8,128)S(1)}, f32[8,128]{1,0:T(8,128)S(1)}, u32[]{:S(2)}, u32[]{:S(2)}) %collective-permute-start.24) | collective-permute-done | bytes 4128 | tf_op jit(solution)/shard_map/ppermute | solution.py:49
  99.4 1.9 %collective-permute-start.28 = (f32[64,128]{1,0:T(8,128)S(1)}, f32[64,128]{1,0:T(8,128)S(1)}, u32[]{:S(2)}, u32[]{:S(2)}) collective-permute-start(f32[64,128]{1,0:T(8,128)S(1)} %constant_dynamic-update-slice_fusion.8.refs_4_), channel_id=1, source_target_pairs={{0,2},{2,0},{1,3},{3,1},{4,6},{6,4},{5,7},{7,5},{8,10},{10,8},{9,1... | collective-permute-start | bytes 98312 | tf_op jit(solution)/shard_map/ppermute | solution.py:49
  101.4 2.1 %collective-permute-done.28.refs_6_ = f32[64,128]{1,0:T(8,128)S(1)} collective-permute-done((f32[64,128]{1,0:T(8,128)S(1)}, f32[64,128]{1,0:T(8,128)S(1)}, u32[]{:S(2)}, u32[]{:S(2)}) %collective-permute-start.28) | collective-permute-done | bytes 32800 | tf_op jit(solution)/shard_map/ppermute | solution.py:49
  103.4 1.2 %collective-permute-done.29.refs_7_ = f32[64,128]{1,0:T(8,128)S(1)} collective-permute-done((f32[64,128]{1,0:T(8,128)S(1)}, f32[64,128]{1,0:T(8,128)S(1)}, u32[]{:S(2)}, u32[]{:S(2)}) %collective-permute-start.29) | collective-permute-done | bytes 32800 | tf_op jit(solution)/shard_map/ppermute | solution.py:49
  104.6 0.7 shard_map.73
  (37 shorter events, 0.1 us)
Async XLA Ops:
  2.0 11.3 %collective-permute-start.2 = (s32[4,128]{1,0:T(4,128)S(1)}, s32[4,128]{1,0:T(4,128)S(1)}, u32[]{:S(2)}, u32[]{:S(2)}) collective-permute-start(s32[4,128]{1,0:T(4,128)S(1)} %reshape.28), channel_id=1, source_target_pairs={{0,12},{4,8},{8,4},{12,0},{1,13},{5,9},{9,5},{13,1},{2,14},{6,10},... | collective-permute-start | bytes 6152 | tf_op jit(solution)/shard_map/ppermute | solution.py:49
  7.0 6.8 %collective-permute-start.1 = (s32[4,128]{1,0:T(4,128)S(1)}, s32[4,128]{1,0:T(4,128)S(1)}, u32[]{:S(2)}, u32[]{:S(2)}) collective-permute-start(s32[4,128]{1,0:T(4,128)S(1)} %reshape.28), channel_id=1, source_target_pairs={{0,8},{4,12},{8,0},{12,4},{1,9},{5,13},{9,1},{13,5},{2,10},{6,14},... | collective-permute-start | bytes 6152 | tf_op jit(solution)/shard_map/ppermute | solution.py:49
  7.0 6.8 %collective-permute-start = (s32[4,128]{1,0:T(4,128)S(1)}, s32[4,128]{1,0:T(4,128)S(1)}, u32[]{:S(2)}, u32[]{:S(2)}) collective-permute-start(s32[4,128]{1,0:T(4,128)S(1)} %reshape.28), channel_id=1, source_target_pairs={{0,4},{4,0},{8,12},{12,8},{1,5},{5,1},{9,13},{13,9},{2,6},{6,2},{1... | collective-permute-start | bytes 6152 | tf_op jit(solution)/shard_map/ppermute | solution.py:49
  9.4 12.1 %collective-permute-start.8 = (f32[256,128]{1,0:T(8,128)S(1)}, f32[256,128]{1,0:T(8,128)S(1)}, u32[]{:S(2)}, u32[]{:S(2)}) collective-permute-start(f32[256,128]{1,0:T(8,128)S(1)} %bitcast.22), channel_id=1, source_target_pairs={{0,12},{4,8},{8,4},{12,0},{1,13},{5,9},{9,5},{13,1},{2,14},{6,10},... | collective-permute-start | bytes 393224 | tf_op jit(solution)/shard_map/ppermute | solution.py:49
  13.2 10.2 %collective-permute-start.7 = (f32[256,128]{1,0:T(8,128)S(1)}, f32[256,128]{1,0:T(8,128)S(1)}, u32[]{:S(2)}, u32[]{:S(2)}) collective-permute-start(f32[256,128]{1,0:T(8,128)S(1)} %bitcast.23), channel_id=1, source_target_pairs={{0,8},{4,12},{8,0},{12,4},{1,9},{5,13},{9,1},{13,5},{2,10},{6,14},... | collective-permute-start | bytes 393224 | tf_op jit(solution)/shard_map/ppermute | solution.py:49
  13.2 10.2 %collective-permute-start.6 = (f32[256,128]{1,0:T(8,128)S(1)}, f32[256,128]{1,0:T(8,128)S(1)}, u32[]{:S(2)}, u32[]{:S(2)}) collective-permute-start(f32[256,128]{1,0:T(8,128)S(1)} %bitcast.24), channel_id=1, source_target_pairs={{0,4},{4,0},{8,12},{12,8},{1,5},{5,1},{9,13},{13,9},{2,6},{6,2},{1... | collective-permute-start | bytes 393224 | tf_op jit(solution)/shard_map/ppermute | solution.py:49
  13.9 3.7 %collective-permute-start.4 = (s32[16,128]{1,0:T(8,128)S(1)}, s32[16,128]{1,0:T(8,128)S(1)}, u32[]{:S(2)}, u32[]{:S(2)}) collective-permute-start(s32[16,128]{1,0:T(8,128)S(1)} %pad_add_fusion.refs_0_), channel_id=1, source_target_pairs={{0,2},{2,0},{1,3},{3,1},{4,6},{6,4},{5,7},{7,5},{8,10},{10,8},{9,1... | collective-permute-start | bytes 24584 | tf_op jit(solution)/shard_map/ppermute | solution.py:49
  15.6 2.4 %collective-permute-start.3 = (s32[16,128]{1,0:T(8,128)S(1)}, s32[16,128]{1,0:T(8,128)S(1)}, u32[]{:S(2)}, u32[]{:S(2)}) collective-permute-start(s32[16,128]{1,0:T(8,128)S(1)} %pad_add_fusion.refs_0_), channel_id=1, source_target_pairs={{0,1},{1,0},{2,3},{3,2},{4,5},{5,4},{6,7},{7,6},{8,9},{9,8},{10,11... | collective-permute-start | bytes 24584 | tf_op jit(solution)/shard_map/ppermute | solution.py:49
  17.6 1.2 %collective-permute-start.5 = (s32[16,128]{1,0:T(8,128)S(1)}, s32[16,128]{1,0:T(8,128)S(1)}, u32[]{:S(2)}, u32[]{:S(2)}) collective-permute-start(s32[16,128]{1,0:T(8,128)S(1)} %collective-permute-done.4.refs_2_), channel_id=1, source_target_pairs={{0,1},{1,0},{2,3},{3,2},{4,5},{5,4},{6,7},{7,6},{8,9},{9,8},{10,11... | collective-permute-start | bytes 24584 | tf_op jit(solution)/shard_map/ppermute | solution.py:49
  23.4 1.3 %collective-permute-start.9 = (f32[256,128]{1,0:T(8,128)S(1)}, f32[256,128]{1,0:T(8,128)S(1)}, u32[]{:S(2)}, u32[]{:S(2)}) collective-permute-start(f32[256,128]{1,0:T(8,128)S(1)} %collective-permute-done.6.refs_6_), channel_id=1, source_target_pairs={{0,1},{1,0},{2,3},{3,2},{4,5},{5,4},{6,7},{7,6},{8,9},{9,8},{10,11... | collective-permute-start | bytes 393224 | tf_op jit(solution)/shard_map/ppermute | solution.py:49
  23.4 1.5 %collective-permute-start.10 = (f32[256,128]{1,0:T(8,128)S(1)}, f32[256,128]{1,0:T(8,128)S(1)}, u32[]{:S(2)}, u32[]{:S(2)}) collective-permute-start(f32[256,128]{1,0:T(8,128)S(1)} %collective-permute-done.7.refs_8_), channel_id=1, source_target_pairs={{0,1},{1,0},{2,3},{3,2},{4,5},{5,4},{6,7},{7,6},{8,9},{9,8},{10,11... | collective-permute-start | bytes 393224 | tf_op jit(solution)/shard_map/ppermute | solution.py:49
  23.9 1.3 %collective-permute-start.11 = (f32[256,128]{1,0:T(8,128)S(1)}, f32[256,128]{1,0:T(8,128)S(1)}, u32[]{:S(2)}, u32[]{:S(2)}) collective-permute-start(f32[256,128]{1,0:T(8,128)S(1)} %collective-permute-done.8.refs_10_), channel_id=1, source_target_pairs={{0,1},{1,0},{2,3},{3,2},{4,5},{5,4},{6,7},{7,6},{8,9},{9,8},{10,11... | collective-permute-start | bytes 393224 | tf_op jit(solution)/shard_map/ppermute | solution.py:49
  55.4 6.3 %collective-permute-start.14 = (f32[32,128]{1,0:T(8,128)S(1)}, f32[32,128]{1,0:T(8,128)S(1)}, u32[]{:S(2)}, u32[]{:S(2)}) collective-permute-start(f32[32,128]{1,0:T(8,128)S(1)} %get-tuple-element.42), channel_id=1, source_target_pairs={{0,12},{4,8},{8,4},{12,0},{1,13},{5,9},{9,5},{13,1},{2,14},{6,10},... | collective-permute-start | bytes 49160 | tf_op jit(solution)/shard_map/ppermute | solution.py:49
  55.7 6.0 %collective-permute-start.13 = (f32[32,128]{1,0:T(8,128)S(1)}, f32[32,128]{1,0:T(8,128)S(1)}, u32[]{:S(2)}, u32[]{:S(2)}) collective-permute-start(f32[32,128]{1,0:T(8,128)S(1)} %get-tuple-element.42), channel_id=1, source_target_pairs={{0,8},{4,12},{8,0},{12,4},{1,9},{5,13},{9,1},{13,5},{2,10},{6,14},... | collective-permute-start | bytes 49160 | tf_op jit(solution)/shard_map/ppermute | solution.py:49
  58.0 3.7 %collective-permute-start.12 = (f32[32,128]{1,0:T(8,128)S(1)}, f32[32,128]{1,0:T(8,128)S(1)}, u32[]{:S(2)}, u32[]{:S(2)}) collective-permute-start(f32[32,128]{1,0:T(8,128)S(1)} %get-tuple-element.42), channel_id=1, source_target_pairs={{0,4},{4,0},{8,12},{12,8},{1,5},{5,1},{9,13},{13,9},{2,6},{6,2},{1... | collective-permute-start | bytes 49160 | tf_op jit(solution)/shard_map/ppermute | solution.py:49
  61.7 4.5 %collective-permute-start.16 = (f32[128,128]{1,0:T(8,128)S(1)}, f32[128,128]{1,0:T(8,128)S(1)}, u32[]{:S(2)}, u32[]{:S(2)}) collective-permute-start(f32[128,128]{1,0:T(8,128)S(1)} %constant_dynamic-update-slice_fusion.refs_9_), channel_id=1, source_target_pairs={{0,2},{2,0},{1,3},{3,1},{4,6},{6,4},{5,7},{7,5},{8,10},{10,8},{9,1... | collective-permute-start | bytes 196616 | tf_op jit(solution)/shard_map/ppermute | solution.py:49
  64.0 2.3 %collective-permute-start.15 = (f32[128,128]{1,0:T(8,128)S(1)}, f32[128,128]{1,0:T(8,128)S(1)}, u32[]{:S(2)}, u32[]{:S(2)}) collective-permute-start(f32[128,128]{1,0:T(8,128)S(1)} %constant_dynamic-update-slice_fusion.refs_9_), channel_id=1, source_target_pairs={{0,1},{1,0},{2,3},{3,2},{4,5},{5,4},{6,7},{7,6},{8,9},{9,8},{10,11... | collective-permute-start | bytes 196616 | tf_op jit(solution)/shard_map/ppermute | solution.py:49
  66.3 1.3 %collective-permute-start.17 = (f32[128,128]{1,0:T(8,128)S(1)}, f32[128,128]{1,0:T(8,128)S(1)}, u32[]{:S(2)}, u32[]{:S(2)}) collective-permute-start(f32[128,128]{1,0:T(8,128)S(1)} %collective-permute-done.16.refs_11_), channel_id=1, source_target_pairs={{0,1},{1,0},{2,3},{3,2},{4,5},{5,4},{6,7},{7,6},{8,9},{9,8},{10,11... | collective-permute-start | bytes 196616 | tf_op jit(solution)/shard_map/ppermute | solution.py:49
  73.9 7.1 %collective-permute-start.20 = (f32[32,128]{1,0:T(8,128)S(1)}, f32[32,128]{1,0:T(8,128)S(1)}, u32[]{:S(2)}, u32[]{:S(2)}) collective-permute-start(f32[32,128]{1,0:T(8,128)S(1)} %get-tuple-element.51), channel_id=1, source_target_pairs={{0,12},{4,8},{8,4},{12,0},{1,13},{5,9},{9,5},{13,1},{2,14},{6,10},... | collective-permute-start | bytes 49160 | tf_op jit(solution)/shard_map/ppermute | solution.py:49
  75.6 5.4 %collective-permute-start.19 = (f32[32,128]{1,0:T(8,128)S(1)}, f32[32,128]{1,0:T(8,128)S(1)}, u32[]{:S(2)}, u32[]{:S(2)}) collective-permute-start(f32[32,128]{1,0:T(8,128)S(1)} %get-tuple-element.51), channel_id=1, source_target_pairs={{0,8},{4,12},{8,0},{12,4},{1,9},{5,13},{9,1},{13,5},{2,10},{6,14},... | collective-permute-start | bytes 49160 | tf_op jit(solution)/shard_map/ppermute | solution.py:49
  77.2 3.7 %collective-permute-start.18 = (f32[32,128]{1,0:T(8,128)S(1)}, f32[32,128]{1,0:T(8,128)S(1)}, u32[]{:S(2)}, u32[]{:S(2)}) collective-permute-start(f32[32,128]{1,0:T(8,128)S(1)} %get-tuple-element.51), channel_id=1, source_target_pairs={{0,4},{4,0},{8,12},{12,8},{1,5},{5,1},{9,13},{13,9},{2,6},{6,2},{1... | collective-permute-start | bytes 49160 | tf_op jit(solution)/shard_map/ppermute | solution.py:49
  81.0 4.3 %collective-permute-start.22 = (f32[128,128]{1,0:T(8,128)S(1)}, f32[128,128]{1,0:T(8,128)S(1)}, u32[]{:S(2)}, u32[]{:S(2)}) collective-permute-start(f32[128,128]{1,0:T(8,128)S(1)} %constant_dynamic-update-slice_fusion.4.refs_9_), channel_id=1, source_target_pairs={{0,2},{2,0},{1,3},{3,1},{4,6},{6,4},{5,7},{7,5},{8,10},{10,8},{9,1... | collective-permute-start | bytes 196616 | tf_op jit(solution)/shard_map/ppermute | solution.py:49
  82.3 3.1 %collective-permute-start.21 = (f32[128,128]{1,0:T(8,128)S(1)}, f32[128,128]{1,0:T(8,128)S(1)}, u32[]{:S(2)}, u32[]{:S(2)}) collective-permute-start(f32[128,128]{1,0:T(8,128)S(1)} %constant_dynamic-update-slice_fusion.4.refs_9_), channel_id=1, source_target_pairs={{0,1},{1,0},{2,3},{3,2},{4,5},{5,4},{6,7},{7,6},{8,9},{9,8},{10,11... | collective-permute-start | bytes 196616 | tf_op jit(solution)/shard_map/ppermute | solution.py:49
  85.3 1.3 %collective-permute-start.23 = (f32[128,128]{1,0:T(8,128)S(1)}, f32[128,128]{1,0:T(8,128)S(1)}, u32[]{:S(2)}, u32[]{:S(2)}) collective-permute-start(f32[128,128]{1,0:T(8,128)S(1)} %collective-permute-done.22.refs_11_), channel_id=1, source_target_pairs={{0,1},{1,0},{2,3},{3,2},{4,5},{5,4},{6,7},{7,6},{8,9},{9,8},{10,11... | collective-permute-start | bytes 196616 | tf_op jit(solution)/shard_map/ppermute | solution.py:49
  93.0 6.4 %collective-permute-start.26 = (f32[8,128]{1,0:T(8,128)S(1)}, f32[8,128]{1,0:T(8,128)S(1)}, u32[]{:S(2)}, u32[]{:S(2)}) collective-permute-start(f32[8,128]{1,0:T(8,128)S(1)} %get-tuple-element.57), channel_id=1, source_target_pairs={{0,12},{4,8},{8,4},{12,0},{1,13},{5,9},{9,5},{13,1},{2,14},{6,10},... | collective-permute-start | bytes 12296 | tf_op jit(solution)/shard_map/ppermute | solution.py:49
  94.5 5.0 %collective-permute-start.25 = (f32[8,128]{1,0:T(8,128)S(1)}, f32[8,128]{1,0:T(8,128)S(1)}, u32[]{:S(2)}, u32[]{:S(2)}) collective-permute-start(f32[8,128]{1,0:T(8,128)S(1)} %get-tuple-element.57), channel_id=1, source_target_pairs={{0,8},{4,12},{8,0},{12,4},{1,9},{5,13},{9,1},{13,5},{2,10},{6,14},... | collective-permute-start | bytes 12296 | tf_op jit(solution)/shard_map/ppermute | solution.py:49
  95.8 3.6 %collective-permute-start.24 = (f32[8,128]{1,0:T(8,128)S(1)}, f32[8,128]{1,0:T(8,128)S(1)}, u32[]{:S(2)}, u32[]{:S(2)}) collective-permute-start(f32[8,128]{1,0:T(8,128)S(1)} %get-tuple-element.57), channel_id=1, source_target_pairs={{0,4},{4,0},{8,12},{12,8},{1,5},{5,1},{9,13},{13,9},{2,6},{6,2},{1... | collective-permute-start | bytes 12296 | tf_op jit(solution)/shard_map/ppermute | solution.py:49
  99.4 4.0 %collective-permute-start.28 = (f32[64,128]{1,0:T(8,128)S(1)}, f32[64,128]{1,0:T(8,128)S(1)}, u32[]{:S(2)}, u32[]{:S(2)}) collective-permute-start(f32[64,128]{1,0:T(8,128)S(1)} %constant_dynamic-update-slice_fusion.8.refs_4_), channel_id=1, source_target_pairs={{0,2},{2,0},{1,3},{3,1},{4,6},{6,4},{5,7},{7,5},{8,10},{10,8},{9,1... | collective-permute-start | bytes 98312 | tf_op jit(solution)/shard_map/ppermute | solution.py:49
  101.3 2.1 %collective-permute-start.27 = (f32[64,128]{1,0:T(8,128)S(1)}, f32[64,128]{1,0:T(8,128)S(1)}, u32[]{:S(2)}, u32[]{:S(2)}) collective-permute-start(f32[64,128]{1,0:T(8,128)S(1)} %constant_dynamic-update-slice_fusion.8.refs_4_), channel_id=1, source_target_pairs={{0,1},{1,0},{2,3},{3,2},{4,5},{5,4},{6,7},{7,6},{8,9},{9,8},{10,11... | collective-permute-start | bytes 98312 | tf_op jit(solution)/shard_map/ppermute | solution.py:49
  103.4 1.2 %collective-permute-start.29 = (f32[64,128]{1,0:T(8,128)S(1)}, f32[64,128]{1,0:T(8,128)S(1)}, u32[]{:S(2)}, u32[]{:S(2)}) collective-permute-start(f32[64,128]{1,0:T(8,128)S(1)} %collective-permute-done.28.refs_6_), channel_id=1, source_target_pairs={{0,1},{1,0},{2,3},{3,2},{4,5},{5,4},{6,7},{7,6},{8,9},{9,8},{10,11... | collective-permute-start | bytes 98312 | tf_op jit(solution)/shard_map/ppermute | solution.py:49

commit v2 on v1

--- a/solution.py
+++ b/solution.py
@@ -12,7 +12,7 @@
 SUPPORT = 0.3
 HALF_LOG2E = 0.7213475204444817
 DEPTH = 48
-UNROLL = 4
+UNROLL = 8
 ARRAYS = 4
 MIB = 1024 * 1024
 VMEM = pl.BlockSpec(memory_space=pltpu.VMEM)

time: 106 us -> 102 us (0.962)
  Pallas kernels: 46.6 us -> 40.9 us
  starting transfers between devices: 31.2 us -> 34.3 us
    pallas_call x6, Pallas kernels: 46.6 us -> 40.9 us  [call(): pl.pallas_call(kernel, in_specs=in_specs, out_shape=shapes, out_specs=out...]
    ppermute x30, starting transfers between devices: 31.2 us -> 34.3 us  [swap(): lax.ppermute(x, axis, [(i, i ^ code) for i in range(lax.axis_size(axis))])]
where the time goes in v2:
time: 102 us
  Pallas kernels  40.9 us (40%)
  starting transfers between devices  34.3 us (34%)
  waiting for transfers between devices  22.7 us (22%)
  other arithmetic  1.48 us (1%)
  between operations  1.43 us (1%)
    pallas_call x6, Pallas kernels, call(): pl.pallas_call(kernel, in_specs=in_specs, out_shape=shapes, out_specs=out...  40.9 us
    ppermute x30, starting transfers between devices, swap(): lax.ppermute(x, axis, [(i, i ^ code) for i in range(lax.axis_size(axis))])  34.3 us
    ppermute x30, waiting for transfers between devices, swap(): lax.ppermute(x, axis, [(i, i ^ code) for i in range(lax.axis_size(axis))])  22.7 us
  transfers between devices with their start and end apart: 30, of which 15 were waited for; matrix products, arithmetic and copies ran while one was open for 2% of the time, Pallas kernels for 3%

profile of v2, /device:TPU:0, one launch (start us, length us, event | category | flops | bytes accessed | tf_op | source)
XLA Modules:
  0.0 101.9 jit_solution(18096377788439503024)
XLA Ops:
  1.3 0.7 broadcast_select_fusion
  2.0 5.0 %collective-permute-start.2 = (s32[4,128]{1,0:T(4,128)S(1)}, s32[4,128]{1,0:T(4,128)S(1)}, u32[]{:S(2)}, u32[]{:S(2)}) collective-permute-start(s32[4,128]{1,0:T(4,128)S(1)} %reshape.28), channel_id=1, source_target_pairs={{0,12},{4,8},{8,4},{12,0},{1,13},{5,9},{9,5},{13,1},{2,14},{6,10},... | collective-permute-start | bytes 6152 | tf_op jit(solution)/shard_map/ppermute | solution.py:49
  7.0 0.0 collective-permute-start.1
  7.0 0.6 collective-permute-start
  7.7 1.0 copy.9
  8.6 0.8 fusion
  9.4 3.8 %collective-permute-start.8 = (f32[256,128]{1,0:T(8,128)S(1)}, f32[256,128]{1,0:T(8,128)S(1)}, u32[]{:S(2)}, u32[]{:S(2)}) collective-permute-start(f32[256,128]{1,0:T(8,128)S(1)} %bitcast.22), channel_id=1, source_target_pairs={{0,12},{4,8},{8,4},{12,0},{1,13},{5,9},{9,5},{13,1},{2,14},{6,10},... | collective-permute-start | bytes 393224 | tf_op jit(solution)/shard_map/ppermute | solution.py:49
  13.2 0.0 collective-permute-done.2
  13.2 0.6 collective-permute-start.6
  13.9 1.7 %collective-permute-start.4 = (s32[16,128]{1,0:T(8,128)S(1)}, s32[16,128]{1,0:T(8,128)S(1)}, u32[]{:S(2)}, u32[]{:S(2)}) collective-permute-start(s32[16,128]{1,0:T(8,128)S(1)} %pad_add_fusion.refs_0_), channel_id=1, source_target_pairs={{0,2},{2,0},{1,3},{3,1},{4,6},{6,4},{5,7},{7,5},{8,10},{10,8},{9,1... | collective-permute-start | bytes 24584 | tf_op jit(solution)/shard_map/ppermute | solution.py:49
  15.6 2.0 %collective-permute-done.4.refs_2_ = s32[16,128]{1,0:T(8,128)S(1)} collective-permute-done((s32[16,128]{1,0:T(8,128)S(1)}, s32[16,128]{1,0:T(8,128)S(1)}, u32[]{:S(2)}, u32[]{:S(2)}) %collective-permute-start.4) | collective-permute-done | bytes 8224 | tf_op jit(solution)/shard_map/ppermute | solution.py:49
  17.6 0.0 collective-permute-start.5
  17.6 0.4 shard_map.69.refs_2_
  18.0 0.0 collective-permute-done.3.refs_1_
  18.0 0.8 collective-permute-done.5.refs_3_
  18.8 2.8 %shard_map.68 = (s32[24,128]{1,0:T(8,128)S(1)}, s32[1]{0:T(128)}) custom-call(s32[16,128]{1,0:T(8,128)S(1)} %pad_add_fusion.refs_0_, s32[16,128]{1,0:T(8,128)S(1)} %collective-permute-done.3.refs_1_, s32[16,128]{1,0:T(8,128)S(1)} %collective-permute-done.4.refs_2_, s32[16,128]{1,0:T(8,128)S(1)} %collective-permute-done.5.refs_3_), custom_call_target="tpu_custom_call" | custom-call | flops 10000000 | bytes 1048576 | tf_op jit(solution)/shard_map/pallas_call | solution.py:468
  21.6 1.9 %collective-permute-done.7.refs_8_ = f32[256,128]{1,0:T(8,128)S(1)} collective-permute-done((f32[256,128]{1,0:T(8,128)S(1)}, f32[256,128]{1,0:T(8,128)S(1)}, u32[]{:S(2)}, u32[]{:S(2)}) %collective-permute-start.7) | collective-permute-done | bytes 131104 | tf_op jit(solution)/shard_map/ppermute | solution.py:49
  23.4 0.0 collective-permute-start.9
  23.4 0.5 collective-permute-start.10
  23.9 0.0 collective-permute-start.11
  23.9 0.8 collective-permute-done.9.refs_7_
  24.8 0.2 collective-permute-done.10.refs_9_
  25.0 0.3 collective-permute-done.11.refs_11_
  25.3 25.4 %shard_map.70 = (f32[14336,128]{1,0:T(8,128)S(1)}, f32[14336,128]{1,0:T(8,128)S(1)}, f32[14336,128]{1,0:T(8,128)S(1)}, f32[14336,128]{1,0:T(8,128)S(1)}, bf16[24...) custom-call(s32[3072]{0:T(1024)S(1)} %bitcast.16, ...), custom_call_target="tpu_custom_call" | custom-call | flops 100000000 | bytes 1048576 | tf_op jit(solution)/shard_map/pallas_call | solution.py:468
  50.7 0.1 collective-permute-start.14
  50.7 1.7 %collective-permute-start.13 = (f32[32,128]{1,0:T(8,128)S(1)}, f32[32,128]{1,0:T(8,128)S(1)}, u32[]{:S(2)}, u32[]{:S(2)}) collective-permute-start(f32[32,128]{1,0:T(8,128)S(1)} %get-tuple-element.42), channel_id=1, source_target_pairs={{0,8},{4,12},{8,0},{12,4},{1,9},{5,13},{9,1},{13,5},{2,10},{6,14},... | collective-permute-start | bytes 49160 | tf_op jit(solution)/shard_map/ppermute | solution.py:49
  52.5 2.6 %collective-permute-start.12 = (f32[32,128]{1,0:T(8,128)S(1)}, f32[32,128]{1,0:T(8,128)S(1)}, u32[]{:S(2)}, u32[]{:S(2)}) collective-permute-start(f32[32,128]{1,0:T(8,128)S(1)} %get-tuple-element.42), channel_id=1, source_target_pairs={{0,4},{4,0},{8,12},{12,8},{1,5},{5,1},{9,13},{13,9},{2,6},{6,2},{1... | collective-permute-start | bytes 49160 | tf_op jit(solution)/shard_map/ppermute | solution.py:49
  55.1 1.7 %collective-permute-done.12 = f32[32,128]{1,0:T(8,128)S(1)} collective-permute-done((f32[32,128]{1,0:T(8,128)S(1)}, f32[32,128]{1,0:T(8,128)S(1)}, u32[]{:S(2)}, u32[]{:S(2)}) %collective-permute-start.12) | collective-permute-done | bytes 16416 | tf_op jit(solution)/shard_map/ppermute | solution.py:49
  56.9 4.4 %collective-permute-start.16 = (f32[128,128]{1,0:T(8,128)S(1)}, f32[128,128]{1,0:T(8,128)S(1)}, u32[]{:S(2)}, u32[]{:S(2)}) collective-permute-start(f32[128,128]{1,0:T(8,128)S(1)} %constant_dynamic-update-slice_fusion.refs_9_), channel_id=1, source_target_pairs={{0,2},{2,0},{1,3},{3,1},{4,6},{6,4},{5,7},{7,5},{8,10},{10,8},{9,1... | collective-permute-start | bytes 196616 | tf_op jit(solution)/shard_map/ppermute | solution.py:49
  61.3 2.2 %collective-permute-done.16.refs_11_ = f32[128,128]{1,0:T(8,128)S(1)} collective-permute-done((f32[128,128]{1,0:T(8,128)S(1)}, f32[128,128]{1,0:T(8,128)S(1)}, u32[]{:S(2)}, u32[]{:S(2)}) %collective-permute-start.16) | collective-permute-done | bytes 65568 | tf_op jit(solution)/shard_map/ppermute | solution.py:49
  63.5 1.2 %collective-permute-done.17.refs_12_ = f32[128,128]{1,0:T(8,128)S(1)} collective-permute-done((f32[128,128]{1,0:T(8,128)S(1)}, f32[128,128]{1,0:T(8,128)S(1)}, u32[]{:S(2)}, u32[]{:S(2)}) %collective-permute-start.17) | collective-permute-done | bytes 65568 | tf_op jit(solution)/shard_map/ppermute | solution.py:49
  64.8 5.8 %shard_map.71 = (f32[32,128]{1,0:T(8,128)S(1)}, f32[8,128]{1,0:T(8,128)S(1)}, f32[128,128]{1,0:T(8,128)S(1)}, f32[512,128]{1,0:T(8,128)S(1)}, f32[512,128]{1,0:T(8,128)S(1)}) custom-call(s32[3072]{0:T(1024)S(1)} %bitcast.17, s32[1]{0:T(128)} %get-tuple-element.33.refs_1_, bf16[4224,128]{1,0:T(8,128)(2,1)S(1)} %shard_map.69.refs_2_, ...), custom_call_target="tpu_custom_call" | custom-call | flops 100000000 | bytes 1048576 | tf_op jit(solution)/shard_map/pallas_call | solution.py:468
  70.6 2.0 %collective-permute-start.20 = (f32[32,128]{1,0:T(8,128)S(1)}, f32[32,128]{1,0:T(8,128)S(1)}, u32[]{:S(2)}, u32[]{:S(2)}) collective-permute-start(f32[32,128]{1,0:T(8,128)S(1)} %get-tuple-element.51), channel_id=1, source_target_pairs={{0,12},{4,8},{8,4},{12,0},{1,13},{5,9},{9,5},{13,1},{2,14},{6,10},... | collective-permute-start | bytes 49160 | tf_op jit(solution)/shard_map/ppermute | solution.py:49
  72.6 1.6 %collective-permute-start.19 = (f32[32,128]{1,0:T(8,128)S(1)}, f32[32,128]{1,0:T(8,128)S(1)}, u32[]{:S(2)}, u32[]{:S(2)}) collective-permute-start(f32[32,128]{1,0:T(8,128)S(1)} %get-tuple-element.51), channel_id=1, source_target_pairs={{0,8},{4,12},{8,0},{12,4},{1,9},{5,13},{9,1},{13,5},{2,10},{6,14},... | collective-permute-start | bytes 49160 | tf_op jit(solution)/shard_map/ppermute | solution.py:49
  74.2 0.8 collective-permute-start.18
  75.1 2.9 %collective-permute-done.18 = f32[32,128]{1,0:T(8,128)S(1)} collective-permute-done((f32[32,128]{1,0:T(8,128)S(1)}, f32[32,128]{1,0:T(8,128)S(1)}, u32[]{:S(2)}, u32[]{:S(2)}) %collective-permute-start.18) | collective-permute-done | bytes 16416 | tf_op jit(solution)/shard_map/ppermute | solution.py:49
  78.0 2.1 %collective-permute-start.22 = (f32[128,128]{1,0:T(8,128)S(1)}, f32[128,128]{1,0:T(8,128)S(1)}, u32[]{:S(2)}, u32[]{:S(2)}) collective-permute-start(f32[128,128]{1,0:T(8,128)S(1)} %constant_dynamic-update-slice_fusion.4.refs_9_), channel_id=1, source_target_pairs={{0,2},{2,0},{1,3},{3,1},{4,6},{6,4},{5,7},{7,5},{8,10},{10,8},{9,1... | collective-permute-start | bytes 196616 | tf_op jit(solution)/shard_map/ppermute | solution.py:49
  80.1 2.2 %collective-permute-done.22.refs_11_ = f32[128,128]{1,0:T(8,128)S(1)} collective-permute-done((f32[128,128]{1,0:T(8,128)S(1)}, f32[128,128]{1,0:T(8,128)S(1)}, u32[]{:S(2)}, u32[]{:S(2)}) %collective-permute-start.22) | collective-permute-done | bytes 65568 | tf_op jit(solution)/shard_map/ppermute | solution.py:49
  82.4 1.2 %collective-permute-done.23.refs_12_ = f32[128,128]{1,0:T(8,128)S(1)} collective-permute-done((f32[128,128]{1,0:T(8,128)S(1)}, f32[128,128]{1,0:T(8,128)S(1)}, u32[]{:S(2)}, u32[]{:S(2)}) %collective-permute-start.23) | collective-permute-done | bytes 65568 | tf_op jit(solution)/shard_map/ppermute | solution.py:49
  83.6 5.9 %shard_map.72 = (f32[32,128]{1,0:T(8,128)S(1)}, f32[8,128]{1,0:T(8,128)S(1)}, f32[128,128]{1,0:T(8,128)S(1)}, f32[128,128]{1,0:T(8,128)S(1)}, f32[128,128]{1,0:T(8,128)S(1)}, /*index=5*/f32[8,128]{1,0:T(8,128)S(1)}) custom-call(s32[3072]{0:T(1024)S(1)} %bitcast.18, s32[1]{0:T(128)} %get-tuple-element.33.refs_1_, bf16[4224,128]{1,0:T(8,128)(2,1)S(1)} %shard_map.69.refs_2_, ...), custom_call_target="tpu_custom_call" | custom-call | flops 100000000 | bytes 1048576 | tf_op jit(solution)/shard_map/pallas_call | solution.py:468
  89.5 1.2 %collective-permute-start.26 = (f32[8,128]{1,0:T(8,128)S(1)}, f32[8,128]{1,0:T(8,128)S(1)}, u32[]{:S(2)}, u32[]{:S(2)}) collective-permute-start(f32[8,128]{1,0:T(8,128)S(1)} %get-tuple-element.57), channel_id=1, source_target_pairs={{0,12},{4,8},{8,4},{12,0},{1,13},{5,9},{9,5},{13,1},{2,14},{6,10},... | collective-permute-start | bytes 12296 | tf_op jit(solution)/shard_map/ppermute | solution.py:49
  90.8 1.6 %collective-permute-start.25 = (f32[8,128]{1,0:T(8,128)S(1)}, f32[8,128]{1,0:T(8,128)S(1)}, u32[]{:S(2)}, u32[]{:S(2)}) collective-permute-start(f32[8,128]{1,0:T(8,128)S(1)} %get-tuple-element.57), channel_id=1, source_target_pairs={{0,8},{4,12},{8,0},{12,4},{1,9},{5,13},{9,1},{13,5},{2,10},{6,14},... | collective-permute-start | bytes 12296 | tf_op jit(solution)/shard_map/ppermute | solution.py:49
  92.4 1.6 %collective-permute-start.24 = (f32[8,128]{1,0:T(8,128)S(1)}, f32[8,128]{1,0:T(8,128)S(1)}, u32[]{:S(2)}, u32[]{:S(2)}) collective-permute-start(f32[8,128]{1,0:T(8,128)S(1)} %get-tuple-element.57), channel_id=1, source_target_pairs={{0,4},{4,0},{8,12},{12,8},{1,5},{5,1},{9,13},{13,9},{2,6},{6,2},{1... | collective-permute-start | bytes 12296 | tf_op jit(solution)/shard_map/ppermute | solution.py:49
  94.0 2.0 %collective-permute-done.24 = f32[8,128]{1,0:T(8,128)S(1)} collective-permute-done((f32[8,128]{1,0:T(8,128)S(1)}, f32[8,128]{1,0:T(8,128)S(1)}, u32[]{:S(2)}, u32[]{:S(2)}) %collective-permute-start.24) | collective-permute-done | bytes 4128 | tf_op jit(solution)/shard_map/ppermute | solution.py:49
  96.0 2.1 %collective-permute-start.28 = (f32[64,128]{1,0:T(8,128)S(1)}, f32[64,128]{1,0:T(8,128)S(1)}, u32[]{:S(2)}, u32[]{:S(2)}) collective-permute-start(f32[64,128]{1,0:T(8,128)S(1)} %constant_dynamic-update-slice_fusion.8.refs_4_), channel_id=1, source_target_pairs={{0,2},{2,0},{1,3},{3,1},{4,6},{6,4},{5,7},{7,5},{8,10},{10,8},{9,1... | collective-permute-start | bytes 98312 | tf_op jit(solution)/shard_map/ppermute | solution.py:49
  98.1 1.9 %collective-permute-done.28.refs_6_ = f32[64,128]{1,0:T(8,128)S(1)} collective-permute-done((f32[64,128]{1,0:T(8,128)S(1)}, f32[64,128]{1,0:T(8,128)S(1)}, u32[]{:S(2)}, u32[]{:S(2)}) %collective-permute-start.28) | collective-permute-done | bytes 32800 | tf_op jit(solution)/shard_map/ppermute | solution.py:49
  100.0 1.2 %collective-permute-done.29.refs_7_ = f32[64,128]{1,0:T(8,128)S(1)} collective-permute-done((f32[64,128]{1,0:T(8,128)S(1)}, f32[64,128]{1,0:T(8,128)S(1)}, u32[]{:S(2)}, u32[]{:S(2)}) %collective-permute-start.29) | collective-permute-done | bytes 32800 | tf_op jit(solution)/shard_map/ppermute | solution.py:49
  101.2 0.7 shard_map.73
  (37 shorter events, 0.1 us)
Async XLA Ops:
  2.0 11.3 %collective-permute-start.2 = (s32[4,128]{1,0:T(4,128)S(1)}, s32[4,128]{1,0:T(4,128)S(1)}, u32[]{:S(2)}, u32[]{:S(2)}) collective-permute-start(s32[4,128]{1,0:T(4,128)S(1)} %reshape.28), channel_id=1, source_target_pairs={{0,12},{4,8},{8,4},{12,0},{1,13},{5,9},{9,5},{13,1},{2,14},{6,10},... | collective-permute-start | bytes 6152 | tf_op jit(solution)/shard_map/ppermute | solution.py:49
  7.0 6.8 %collective-permute-start.1 = (s32[4,128]{1,0:T(4,128)S(1)}, s32[4,128]{1,0:T(4,128)S(1)}, u32[]{:S(2)}, u32[]{:S(2)}) collective-permute-start(s32[4,128]{1,0:T(4,128)S(1)} %reshape.28), channel_id=1, source_target_pairs={{0,8},{4,12},{8,0},{12,4},{1,9},{5,13},{9,1},{13,5},{2,10},{6,14},... | collective-permute-start | bytes 6152 | tf_op jit(solution)/shard_map/ppermute | solution.py:49
  7.0 6.8 %collective-permute-start = (s32[4,128]{1,0:T(4,128)S(1)}, s32[4,128]{1,0:T(4,128)S(1)}, u32[]{:S(2)}, u32[]{:S(2)}) collective-permute-start(s32[4,128]{1,0:T(4,128)S(1)} %reshape.28), channel_id=1, source_target_pairs={{0,4},{4,0},{8,12},{12,8},{1,5},{5,1},{9,13},{13,9},{2,6},{6,2},{1... | collective-permute-start | bytes 6152 | tf_op jit(solution)/shard_map/ppermute | solution.py:49
  9.4 12.1 %collective-permute-start.8 = (f32[256,128]{1,0:T(8,128)S(1)}, f32[256,128]{1,0:T(8,128)S(1)}, u32[]{:S(2)}, u32[]{:S(2)}) collective-permute-start(f32[256,128]{1,0:T(8,128)S(1)} %bitcast.22), channel_id=1, source_target_pairs={{0,12},{4,8},{8,4},{12,0},{1,13},{5,9},{9,5},{13,1},{2,14},{6,10},... | collective-permute-start | bytes 393224 | tf_op jit(solution)/shard_map/ppermute | solution.py:49
  13.2 10.2 %collective-permute-start.7 = (f32[256,128]{1,0:T(8,128)S(1)}, f32[256,128]{1,0:T(8,128)S(1)}, u32[]{:S(2)}, u32[]{:S(2)}) collective-permute-start(f32[256,128]{1,0:T(8,128)S(1)} %bitcast.23), channel_id=1, source_target_pairs={{0,8},{4,12},{8,0},{12,4},{1,9},{5,13},{9,1},{13,5},{2,10},{6,14},... | collective-permute-start | bytes 393224 | tf_op jit(solution)/shard_map/ppermute | solution.py:49
  13.2 10.2 %collective-permute-start.6 = (f32[256,128]{1,0:T(8,128)S(1)}, f32[256,128]{1,0:T(8,128)S(1)}, u32[]{:S(2)}, u32[]{:S(2)}) collective-permute-start(f32[256,128]{1,0:T(8,128)S(1)} %bitcast.24), channel_id=1, source_target_pairs={{0,4},{4,0},{8,12},{12,8},{1,5},{5,1},{9,13},{13,9},{2,6},{6,2},{1... | collective-permute-start | bytes 393224 | tf_op jit(solution)/shard_map/ppermute | solution.py:49
  13.9 3.7 %collective-permute-start.4 = (s32[16,128]{1,0:T(8,128)S(1)}, s32[16,128]{1,0:T(8,128)S(1)}, u32[]{:S(2)}, u32[]{:S(2)}) collective-permute-start(s32[16,128]{1,0:T(8,128)S(1)} %pad_add_fusion.refs_0_), channel_id=1, source_target_pairs={{0,2},{2,0},{1,3},{3,1},{4,6},{6,4},{5,7},{7,5},{8,10},{10,8},{9,1... | collective-permute-start | bytes 24584 | tf_op jit(solution)/shard_map/ppermute | solution.py:49
  15.6 2.4 %collective-permute-start.3 = (s32[16,128]{1,0:T(8,128)S(1)}, s32[16,128]{1,0:T(8,128)S(1)}, u32[]{:S(2)}, u32[]{:S(2)}) collective-permute-start(s32[16,128]{1,0:T(8,128)S(1)} %pad_add_fusion.refs_0_), channel_id=1, source_target_pairs={{0,1},{1,0},{2,3},{3,2},{4,5},{5,4},{6,7},{7,6},{8,9},{9,8},{10,11... | collective-permute-start | bytes 24584 | tf_op jit(solution)/shard_map/ppermute | solution.py:49
  17.6 1.2 %collective-permute-start.5 = (s32[16,128]{1,0:T(8,128)S(1)}, s32[16,128]{1,0:T(8,128)S(1)}, u32[]{:S(2)}, u32[]{:S(2)}) collective-permute-start(s32[16,128]{1,0:T(8,128)S(1)} %collective-permute-done.4.refs_2_), channel_id=1, source_target_pairs={{0,1},{1,0},{2,3},{3,2},{4,5},{5,4},{6,7},{7,6},{8,9},{9,8},{10,11... | collective-permute-start | bytes 24584 | tf_op jit(solution)/shard_map/ppermute | solution.py:49
  23.4 1.3 %collective-permute-start.9 = (f32[256,128]{1,0:T(8,128)S(1)}, f32[256,128]{1,0:T(8,128)S(1)}, u32[]{:S(2)}, u32[]{:S(2)}) collective-permute-start(f32[256,128]{1,0:T(8,128)S(1)} %collective-permute-done.6.refs_6_), channel_id=1, source_target_pairs={{0,1},{1,0},{2,3},{3,2},{4,5},{5,4},{6,7},{7,6},{8,9},{9,8},{10,11... | collective-permute-start | bytes 393224 | tf_op jit(solution)/shard_map/ppermute | solution.py:49
  23.4 1.5 %collective-permute-start.10 = (f32[256,128]{1,0:T(8,128)S(1)}, f32[256,128]{1,0:T(8,128)S(1)}, u32[]{:S(2)}, u32[]{:S(2)}) collective-permute-start(f32[256,128]{1,0:T(8,128)S(1)} %collective-permute-done.7.refs_8_), channel_id=1, source_target_pairs={{0,1},{1,0},{2,3},{3,2},{4,5},{5,4},{6,7},{7,6},{8,9},{9,8},{10,11... | collective-permute-start | bytes 393224 | tf_op jit(solution)/shard_map/ppermute | solution.py:49
  23.9 1.3 %collective-permute-start.11 = (f32[256,128]{1,0:T(8,128)S(1)}, f32[256,128]{1,0:T(8,128)S(1)}, u32[]{:S(2)}, u32[]{:S(2)}) collective-permute-start(f32[256,128]{1,0:T(8,128)S(1)} %collective-permute-done.8.refs_10_), channel_id=1, source_target_pairs={{0,1},{1,0},{2,3},{3,2},{4,5},{5,4},{6,7},{7,6},{8,9},{9,8},{10,11... | collective-permute-start | bytes 393224 | tf_op jit(solution)/shard_map/ppermute | solution.py:49
  50.7 6.2 %collective-permute-start.14 = (f32[32,128]{1,0:T(8,128)S(1)}, f32[32,128]{1,0:T(8,128)S(1)}, u32[]{:S(2)}, u32[]{:S(2)}) collective-permute-start(f32[32,128]{1,0:T(8,128)S(1)} %get-tuple-element.42), channel_id=1, source_target_pairs={{0,12},{4,8},{8,4},{12,0},{1,13},{5,9},{9,5},{13,1},{2,14},{6,10},... | collective-permute-start | bytes 49160 | tf_op jit(solution)/shard_map/ppermute | solution.py:49
  50.7 6.1 %collective-permute-start.13 = (f32[32,128]{1,0:T(8,128)S(1)}, f32[32,128]{1,0:T(8,128)S(1)}, u32[]{:S(2)}, u32[]{:S(2)}) collective-permute-start(f32[32,128]{1,0:T(8,128)S(1)} %get-tuple-element.42), channel_id=1, source_target_pairs={{0,8},{4,12},{8,0},{12,4},{1,9},{5,13},{9,1},{13,5},{2,10},{6,14},... | collective-permute-start | bytes 49160 | tf_op jit(solution)/shard_map/ppermute | solution.py:49
  52.5 4.4 %collective-permute-start.12 = (f32[32,128]{1,0:T(8,128)S(1)}, f32[32,128]{1,0:T(8,128)S(1)}, u32[]{:S(2)}, u32[]{:S(2)}) collective-permute-start(f32[32,128]{1,0:T(8,128)S(1)} %get-tuple-element.42), channel_id=1, source_target_pairs={{0,4},{4,0},{8,12},{12,8},{1,5},{5,1},{9,13},{13,9},{2,6},{6,2},{1... | collective-permute-start | bytes 49160 | tf_op jit(solution)/shard_map/ppermute | solution.py:49
  56.9 6.7 %collective-permute-start.16 = (f32[128,128]{1,0:T(8,128)S(1)}, f32[128,128]{1,0:T(8,128)S(1)}, u32[]{:S(2)}, u32[]{:S(2)}) collective-permute-start(f32[128,128]{1,0:T(8,128)S(1)} %constant_dynamic-update-slice_fusion.refs_9_), channel_id=1, source_target_pairs={{0,2},{2,0},{1,3},{3,1},{4,6},{6,4},{5,7},{7,5},{8,10},{10,8},{9,1... | collective-permute-start | bytes 196616 | tf_op jit(solution)/shard_map/ppermute | solution.py:49
  61.3 2.3 %collective-permute-start.15 = (f32[128,128]{1,0:T(8,128)S(1)}, f32[128,128]{1,0:T(8,128)S(1)}, u32[]{:S(2)}, u32[]{:S(2)}) collective-permute-start(f32[128,128]{1,0:T(8,128)S(1)} %constant_dynamic-update-slice_fusion.refs_9_), channel_id=1, source_target_pairs={{0,1},{1,0},{2,3},{3,2},{4,5},{5,4},{6,7},{7,6},{8,9},{9,8},{10,11... | collective-permute-start | bytes 196616 | tf_op jit(solution)/shard_map/ppermute | solution.py:49
  63.5 1.3 %collective-permute-start.17 = (f32[128,128]{1,0:T(8,128)S(1)}, f32[128,128]{1,0:T(8,128)S(1)}, u32[]{:S(2)}, u32[]{:S(2)}) collective-permute-start(f32[128,128]{1,0:T(8,128)S(1)} %collective-permute-done.16.refs_11_), channel_id=1, source_target_pairs={{0,1},{1,0},{2,3},{3,2},{4,5},{5,4},{6,7},{7,6},{8,9},{9,8},{10,11... | collective-permute-start | bytes 196616 | tf_op jit(solution)/shard_map/ppermute | solution.py:49
  70.6 7.4 %collective-permute-start.20 = (f32[32,128]{1,0:T(8,128)S(1)}, f32[32,128]{1,0:T(8,128)S(1)}, u32[]{:S(2)}, u32[]{:S(2)}) collective-permute-start(f32[32,128]{1,0:T(8,128)S(1)} %get-tuple-element.51), channel_id=1, source_target_pairs={{0,12},{4,8},{8,4},{12,0},{1,13},{5,9},{9,5},{13,1},{2,14},{6,10},... | collective-permute-start | bytes 49160 | tf_op jit(solution)/shard_map/ppermute | solution.py:49
  72.6 5.4 %collective-permute-start.19 = (f32[32,128]{1,0:T(8,128)S(1)}, f32[32,128]{1,0:T(8,128)S(1)}, u32[]{:S(2)}, u32[]{:S(2)}) collective-permute-start(f32[32,128]{1,0:T(8,128)S(1)} %get-tuple-element.51), channel_id=1, source_target_pairs={{0,8},{4,12},{8,0},{12,4},{1,9},{5,13},{9,1},{13,5},{2,10},{6,14},... | collective-permute-start | bytes 49160 | tf_op jit(solution)/shard_map/ppermute | solution.py:49
  74.2 3.7 %collective-permute-start.18 = (f32[32,128]{1,0:T(8,128)S(1)}, f32[32,128]{1,0:T(8,128)S(1)}, u32[]{:S(2)}, u32[]{:S(2)}) collective-permute-start(f32[32,128]{1,0:T(8,128)S(1)} %get-tuple-element.51), channel_id=1, source_target_pairs={{0,4},{4,0},{8,12},{12,8},{1,5},{5,1},{9,13},{13,9},{2,6},{6,2},{1... | collective-permute-start | bytes 49160 | tf_op jit(solution)/shard_map/ppermute | solution.py:49
  78.0 4.3 %collective-permute-start.22 = (f32[128,128]{1,0:T(8,128)S(1)}, f32[128,128]{1,0:T(8,128)S(1)}, u32[]{:S(2)}, u32[]{:S(2)}) collective-permute-start(f32[128,128]{1,0:T(8,128)S(1)} %constant_dynamic-update-slice_fusion.4.refs_9_), channel_id=1, source_target_pairs={{0,2},{2,0},{1,3},{3,1},{4,6},{6,4},{5,7},{7,5},{8,10},{10,8},{9,1... | collective-permute-start | bytes 196616 | tf_op jit(solution)/shard_map/ppermute | solution.py:49
  80.1 2.3 %collective-permute-start.21 = (f32[128,128]{1,0:T(8,128)S(1)}, f32[128,128]{1,0:T(8,128)S(1)}, u32[]{:S(2)}, u32[]{:S(2)}) collective-permute-start(f32[128,128]{1,0:T(8,128)S(1)} %constant_dynamic-update-slice_fusion.4.refs_9_), channel_id=1, source_target_pairs={{0,1},{1,0},{2,3},{3,2},{4,5},{5,4},{6,7},{7,6},{8,9},{9,8},{10,11... | collective-permute-start | bytes 196616 | tf_op jit(solution)/shard_map/ppermute | solution.py:49
  82.4 1.3 %collective-permute-start.23 = (f32[128,128]{1,0:T(8,128)S(1)}, f32[128,128]{1,0:T(8,128)S(1)}, u32[]{:S(2)}, u32[]{:S(2)}) collective-permute-start(f32[128,128]{1,0:T(8,128)S(1)} %collective-permute-done.22.refs_11_), channel_id=1, source_target_pairs={{0,1},{1,0},{2,3},{3,2},{4,5},{5,4},{6,7},{7,6},{8,9},{9,8},{10,11... | collective-permute-start | bytes 196616 | tf_op jit(solution)/shard_map/ppermute | solution.py:49
  89.5 6.5 %collective-permute-start.26 = (f32[8,128]{1,0:T(8,128)S(1)}, f32[8,128]{1,0:T(8,128)S(1)}, u32[]{:S(2)}, u32[]{:S(2)}) collective-permute-start(f32[8,128]{1,0:T(8,128)S(1)} %get-tuple-element.57), channel_id=1, source_target_pairs={{0,12},{4,8},{8,4},{12,0},{1,13},{5,9},{9,5},{13,1},{2,14},{6,10},... | collective-permute-start | bytes 12296 | tf_op jit(solution)/shard_map/ppermute | solution.py:49
  90.8 5.3 %collective-permute-start.25 = (f32[8,128]{1,0:T(8,128)S(1)}, f32[8,128]{1,0:T(8,128)S(1)}, u32[]{:S(2)}, u32[]{:S(2)}) collective-permute-start(f32[8,128]{1,0:T(8,128)S(1)} %get-tuple-element.57), channel_id=1, source_target_pairs={{0,8},{4,12},{8,0},{12,4},{1,9},{5,13},{9,1},{13,5},{2,10},{6,14},... | collective-permute-start | bytes 12296 | tf_op jit(solution)/shard_map/ppermute | solution.py:49
  92.4 3.6 %collective-permute-start.24 = (f32[8,128]{1,0:T(8,128)S(1)}, f32[8,128]{1,0:T(8,128)S(1)}, u32[]{:S(2)}, u32[]{:S(2)}) collective-permute-start(f32[8,128]{1,0:T(8,128)S(1)} %get-tuple-element.57), channel_id=1, source_target_pairs={{0,4},{4,0},{8,12},{12,8},{1,5},{5,1},{9,13},{13,9},{2,6},{6,2},{1... | collective-permute-start | bytes 12296 | tf_op jit(solution)/shard_map/ppermute | solution.py:49
  96.0 4.0 %collective-permute-start.28 = (f32[64,128]{1,0:T(8,128)S(1)}, f32[64,128]{1,0:T(8,128)S(1)}, u32[]{:S(2)}, u32[]{:S(2)}) collective-permute-start(f32[64,128]{1,0:T(8,128)S(1)} %constant_dynamic-update-slice_fusion.8.refs_4_), channel_id=1, source_target_pairs={{0,2},{2,0},{1,3},{3,1},{4,6},{6,4},{5,7},{7,5},{8,10},{10,8},{9,1... | collective-permute-start | bytes 98312 | tf_op jit(solution)/shard_map/ppermute | solution.py:49
  98.1 1.9 %collective-permute-start.27 = (f32[64,128]{1,0:T(8,128)S(1)}, f32[64,128]{1,0:T(8,128)S(1)}, u32[]{:S(2)}, u32[]{:S(2)}) collective-permute-start(f32[64,128]{1,0:T(8,128)S(1)} %constant_dynamic-update-slice_fusion.8.refs_4_), channel_id=1, source_target_pairs={{0,1},{1,0},{2,3},{3,2},{4,5},{5,4},{6,7},{7,6},{8,9},{9,8},{10,11... | collective-permute-start | bytes 98312 | tf_op jit(solution)/shard_map/ppermute | solution.py:49
  100.0 1.2 %collective-permute-start.29 = (f32[64,128]{1,0:T(8,128)S(1)}, f32[64,128]{1,0:T(8,128)S(1)}, u32[]{:S(2)}, u32[]{:S(2)}) collective-permute-start(f32[64,128]{1,0:T(8,128)S(1)} %collective-permute-done.28.refs_6_), channel_id=1, source_target_pairs={{0,1},{1,0},{2,3},{3,2},{4,5},{5,4},{6,7},{7,6},{8,9},{9,8},{10,11... | collective-permute-start | bytes 98312 | tf_op jit(solution)/shard_map/ppermute | solution.py:49

commit v3 on v2

--- a/solution.py
+++ b/solution.py
@@ -12,7 +12,7 @@
 SUPPORT = 0.3
 HALF_LOG2E = 0.7213475204444817
 DEPTH = 48
-UNROLL = 8
+UNROLL = 16
 ARRAYS = 4
 MIB = 1024 * 1024
 VMEM = pl.BlockSpec(memory_space=pltpu.VMEM)
@@ -36,7 +36,7 @@
         self.capacity = 2 * self.plane * slots + 1024
         per_row = slots * self.devs // self.blocks
         self.first_mib = 6 + self.blocks * DEPTH * BS * 2 // MIB
-        self.kept = min(448, (48 - self.first_mib) * 16) // ARRAYS
+        self.kept = min(448, (48 - self.first_mib) * 16) // (ARRAYS * UNROLL) * UNROLL
         self.scale = 16.0 / (BS * per_row) / 256.0
 
     def me(self):
@@ -258,20 +258,24 @@
     top = jnp.maximum(lax.div(count + (UNROLL - 1), UNROLL) - 1, 0)
 
     def squared(g, u):
-        i, j = entry_of(list_ref, jnp.minimum(g, top) * UNROLL + u)
-        return squared_of(own_features(lhs_ref, i), other_features(rhs_ref, j))
-
-    for u in range(UNROLL):
-        squares[u * BS : (u + 1) * BS, :] = squared(0, u)
+        k = jnp.minimum(g, top) * UNROLL + u
+        i, j = entry_of(list_ref, k)
+        unused, twin = entry_of(list_ref, k + 1)
+        both = jnp.concatenate([other_features(rhs_ref, j), other_features(rhs_ref, twin)], axis=1)
+        return squared_of(own_features(lhs_ref, i), both)
+
+    for u in range(0, UNROLL, 2):
+        squares[u // 2 * BS : (u // 2 + 1) * BS, :] = squared(0, u)
     for at, tile_ref in enumerate(tile_refs):
 
         def group(g, unused, at=at, tile_ref=tile_ref):
-            for u in range(UNROLL):
+            for u in range(0, UNROLL, 2):
                 following = squared(g + 1, u)
                 start = pl.multiple_of((g * UNROLL + u - at * sz.kept) * BS, BS)
                 for r in range(0, BS, 8):
-                    here = slice(u * BS + r, u * BS + r + 8)
-                    tile_ref[pl.ds(start + r, 8), :] = taper_of(squares[here, :])
+                    here = slice(u // 2 * BS + r, u // 2 * BS + r + 8)
+                    tile_ref[pl.ds(start + r, 8), :] = taper_of(squares[here, :BS])
+                    tile_ref[pl.ds(start + BS + r, 8), :] = taper_of(squares[here, BS:])
                     squares[here, :] = following[r : r + 8, :]
             return unused
 
@@ -542,7 +546,7 @@
             tall,
             tall,
             pltpu.VMEM((own, BS), F32),
-            pltpu.VMEM((UNROLL * BS, BS), F32),
+            pltpu.VMEM((UNROLL // 2 * BS, 2 * BS), F32),
             pltpu.VMEM((home, BS), F32),
             pltpu.SemaphoreType.DMA,
             pltpu.SemaphoreType.DMA((2,)),
@@ -565,7 +569,7 @@
         outs = [array(own, BS), array(8, BS), array(home, BS), array(span, BS), array(span, BS)]
         mapped, norm, field, resid, dirn, *dot = call(
             functools.partial(step_kernel, sz, last),
-            5,
+            8,
             [SMEM, SMEM, ANY, ANY] + [VMEM] * (5 + sz.plane + ARRAYS),
             outs + [array(8, BS)] * last,
             [VMEM] * (len(outs) + last),

time: 102 us -> 103 us (level)
  Pallas kernels: 40.9 us -> 46.2 us
  starting transfers between devices: 34.3 us -> 30.5 us
    pallas_call x6, Pallas kernels: 40.9 us -> 46.2 us  [call(): pl.pallas_call(kernel, in_specs=in_specs, out_shape=shapes, out_specs=out...]
    ppermute x30, starting transfers between devices: 34.3 us -> 30.5 us  [swap(): lax.ppermute(x, axis, [(i, i ^ code) for i in range(lax.axis_size(axis))])]
  transfers between devices with their start and end apart: 30 -> 30, of which waited for: 15 -> 15; matrix products, arithmetic and copies ran while one was open for 2% -> 2% of each run, Pallas kernels for 3% -> 4%
where the time goes in v3:
time: 103 us
  Pallas kernels  46.2 us (45%)
  starting transfers between devices  30.5 us (30%)
  waiting for transfers between devices  22.9 us (22%)
  other arithmetic  1.48 us (1%)
  between operations  1.43 us (1%)
    pallas_call x6, Pallas kernels, call(): pl.pallas_call(kernel, in_specs=in_specs, out_shape=shapes, out_specs=out...  46.2 us
    ppermute x30, starting transfers between devices, swap(): lax.ppermute(x, axis, [(i, i ^ code) for i in range(lax.axis_size(axis))])  30.5 us
    ppermute x30, waiting for transfers between devices, swap(): lax.ppermute(x, axis, [(i, i ^ code) for i in range(lax.axis_size(axis))])  22.9 us
  transfers between devices with their start and end apart: 30, of which 15 were waited for; matrix products, arithmetic and copies ran while one was open for 2% of the time, Pallas kernels for 4%

profile of v3, /device:TPU:0, one launch (start us, length us, event | category | flops | bytes accessed | tf_op | source)
XLA Modules:
  0.0 103.5 jit_solution(9807091010111635901)
XLA Ops:
  1.3 0.7 broadcast_select_fusion
  2.0 5.0 %collective-permute-start.2 = (s32[4,128]{1,0:T(4,128)S(1)}, s32[4,128]{1,0:T(4,128)S(1)}, u32[]{:S(2)}, u32[]{:S(2)}) collective-permute-start(s32[4,128]{1,0:T(4,128)S(1)} %reshape.28), channel_id=1, source_target_pairs={{0,12},{4,8},{8,4},{12,0},{1,13},{5,9},{9,5},{13,1},{2,14},{6,10},... | collective-permute-start | bytes 6152 | tf_op jit(solution)/shard_map/ppermute | solution.py:49
  7.0 0.0 collective-permute-start.1
  7.0 0.6 collective-permute-start
  7.7 1.0 copy.9
  8.6 0.8 fusion
  9.4 3.8 %collective-permute-start.8 = (f32[256,128]{1,0:T(8,128)S(1)}, f32[256,128]{1,0:T(8,128)S(1)}, u32[]{:S(2)}, u32[]{:S(2)}) collective-permute-start(f32[256,128]{1,0:T(8,128)S(1)} %bitcast.22), channel_id=1, source_target_pairs={{0,12},{4,8},{8,4},{12,0},{1,13},{5,9},{9,5},{13,1},{2,14},{6,10},... | collective-permute-start | bytes 393224 | tf_op jit(solution)/shard_map/ppermute | solution.py:49
  13.2 0.0 collective-permute-done.2
  13.2 0.6 collective-permute-start.6
  13.9 1.7 %collective-permute-start.4 = (s32[16,128]{1,0:T(8,128)S(1)}, s32[16,128]{1,0:T(8,128)S(1)}, u32[]{:S(2)}, u32[]{:S(2)}) collective-permute-start(s32[16,128]{1,0:T(8,128)S(1)} %pad_add_fusion.refs_0_), channel_id=1, source_target_pairs={{0,2},{2,0},{1,3},{3,1},{4,6},{6,4},{5,7},{7,5},{8,10},{10,8},{9,1... | collective-permute-start | bytes 24584 | tf_op jit(solution)/shard_map/ppermute | solution.py:49
  15.6 2.0 %collective-permute-done.4.refs_2_ = s32[16,128]{1,0:T(8,128)S(1)} collective-permute-done((s32[16,128]{1,0:T(8,128)S(1)}, s32[16,128]{1,0:T(8,128)S(1)}, u32[]{:S(2)}, u32[]{:S(2)}) %collective-permute-start.4) | collective-permute-done | bytes 8224 | tf_op jit(solution)/shard_map/ppermute | solution.py:49
  17.6 0.0 collective-permute-start.5
  17.6 0.4 shard_map.69.refs_2_
  18.0 0.0 collective-permute-done.3.refs_1_
  18.0 0.8 collective-permute-done.5.refs_3_
  18.8 3.4 %shard_map.68 = (s32[24,128]{1,0:T(8,128)S(1)}, s32[1]{0:T(128)}) custom-call(s32[16,128]{1,0:T(8,128)S(1)} %pad_add_fusion.refs_0_, s32[16,128]{1,0:T(8,128)S(1)} %collective-permute-done.3.refs_1_, s32[16,128]{1,0:T(8,128)S(1)} %collective-permute-done.4.refs_2_, s32[16,128]{1,0:T(8,128)S(1)} %collective-permute-done.5.refs_3_), custom_call_target="tpu_custom_call" | custom-call | flops 10000000 | bytes 1048576 | tf_op jit(solution)/shard_map/pallas_call | solution.py:472
  22.2 0.0 collective-permute-done.8.refs_10_
  22.2 1.2 %collective-permute-done.7.refs_8_ = f32[256,128]{1,0:T(8,128)S(1)} collective-permute-done((f32[256,128]{1,0:T(8,128)S(1)}, f32[256,128]{1,0:T(8,128)S(1)}, u32[]{:S(2)}, u32[]{:S(2)}) %collective-permute-start.7) | collective-permute-done | bytes 131104 | tf_op jit(solution)/shard_map/ppermute | solution.py:49
  23.4 0.5 collective-permute-start.10
  23.9 0.0 collective-permute-start.11
  23.9 0.8 collective-permute-done.9.refs_7_
  24.8 0.2 collective-permute-done.10.refs_9_
  25.0 0.3 collective-permute-done.11.refs_11_
  25.3 28.6 %shard_map.70 = (f32[14336,128]{1,0:T(8,128)S(1)}, f32[14336,128]{1,0:T(8,128)S(1)}, f32[14336,128]{1,0:T(8,128)S(1)}, f32[14336,128]{1,0:T(8,128)S(1)}, bf16[24...) custom-call(s32[3072]{0:T(1024)S(1)} %bitcast.16, ...), custom_call_target="tpu_custom_call" | custom-call | flops 100000000 | bytes 1048576 | tf_op jit(solution)/shard_map/pallas_call | solution.py:472
  53.9 0.1 collective-permute-start.14
  54.1 0.0 collective-permute-start.13
  54.1 4.3 %collective-permute-start.12 = (f32[32,128]{1,0:T(8,128)S(1)}, f32[32,128]{1,0:T(8,128)S(1)}, u32[]{:S(2)}, u32[]{:S(2)}) collective-permute-start(f32[32,128]{1,0:T(8,128)S(1)} %get-tuple-element.42), channel_id=1, source_target_pairs={{0,4},{4,0},{8,12},{12,8},{1,5},{5,1},{9,13},{13,9},{2,6},{6,2},{1... | collective-permute-start | bytes 49160 | tf_op jit(solution)/shard_map/ppermute | solution.py:49
  58.4 1.7 %collective-permute-done.12 = f32[32,128]{1,0:T(8,128)S(1)} collective-permute-done((f32[32,128]{1,0:T(8,128)S(1)}, f32[32,128]{1,0:T(8,128)S(1)}, u32[]{:S(2)}, u32[]{:S(2)}) %collective-permute-start.12) | collective-permute-done | bytes 16416 | tf_op jit(solution)/shard_map/ppermute | solution.py:49
  60.1 1.6 %collective-permute-start.16 = (f32[128,128]{1,0:T(8,128)S(1)}, f32[128,128]{1,0:T(8,128)S(1)}, u32[]{:S(2)}, u32[]{:S(2)}) collective-permute-start(f32[128,128]{1,0:T(8,128)S(1)} %constant_dynamic-update-slice_fusion.refs_9_), channel_id=1, source_target_pairs={{0,2},{2,0},{1,3},{3,1},{4,6},{6,4},{5,7},{7,5},{8,10},{10,8},{9,1... | collective-permute-start | bytes 196616 | tf_op jit(solution)/shard_map/ppermute | solution.py:49
  61.7 2.8 %collective-permute-done.16.refs_11_ = f32[128,128]{1,0:T(8,128)S(1)} collective-permute-done((f32[128,128]{1,0:T(8,128)S(1)}, f32[128,128]{1,0:T(8,128)S(1)}, u32[]{:S(2)}, u32[]{:S(2)}) %collective-permute-start.16) | collective-permute-done | bytes 65568 | tf_op jit(solution)/shard_map/ppermute | solution.py:49
  64.5 1.2 %collective-permute-done.17.refs_12_ = f32[128,128]{1,0:T(8,128)S(1)} collective-permute-done((f32[128,128]{1,0:T(8,128)S(1)}, f32[128,128]{1,0:T(8,128)S(1)}, u32[]{:S(2)}, u32[]{:S(2)}) %collective-permute-start.17) | collective-permute-done | bytes 65568 | tf_op jit(solution)/shard_map/ppermute | solution.py:49
  65.7 6.5 %shard_map.71 = (f32[32,128]{1,0:T(8,128)S(1)}, f32[8,128]{1,0:T(8,128)S(1)}, f32[128,128]{1,0:T(8,128)S(1)}, f32[512,128]{1,0:T(8,128)S(1)}, f32[512,128]{1,0:T(8,128)S(1)}) custom-call(s32[3072]{0:T(1024)S(1)} %bitcast.17, s32[1]{0:T(128)} %get-tuple-element.33.refs_1_, bf16[4224,128]{1,0:T(8,128)(2,1)S(1)} %shard_map.69.refs_2_, ...), custom_call_target="tpu_custom_call" | custom-call | flops 100000000 | bytes 1048576 | tf_op jit(solution)/shard_map/pallas_call | solution.py:472
  72.2 2.0 %collective-permute-start.20 = (f32[32,128]{1,0:T(8,128)S(1)}, f32[32,128]{1,0:T(8,128)S(1)}, u32[]{:S(2)}, u32[]{:S(2)}) collective-permute-start(f32[32,128]{1,0:T(8,128)S(1)} %get-tuple-element.51), channel_id=1, source_target_pairs={{0,12},{4,8},{8,4},{12,0},{1,13},{5,9},{9,5},{13,1},{2,14},{6,10},... | collective-permute-start | bytes 49160 | tf_op jit(solution)/shard_map/ppermute | solution.py:49
  74.3 1.3 %collective-permute-start.19 = (f32[32,128]{1,0:T(8,128)S(1)}, f32[32,128]{1,0:T(8,128)S(1)}, u32[]{:S(2)}, u32[]{:S(2)}) collective-permute-start(f32[32,128]{1,0:T(8,128)S(1)} %get-tuple-element.51), channel_id=1, source_target_pairs={{0,8},{4,12},{8,0},{12,4},{1,9},{5,13},{9,1},{13,5},{2,10},{6,14},... | collective-permute-start | bytes 49160 | tf_op jit(solution)/shard_map/ppermute | solution.py:49
  75.5 1.1 %collective-permute-start.18 = (f32[32,128]{1,0:T(8,128)S(1)}, f32[32,128]{1,0:T(8,128)S(1)}, u32[]{:S(2)}, u32[]{:S(2)}) collective-permute-start(f32[32,128]{1,0:T(8,128)S(1)} %get-tuple-element.51), channel_id=1, source_target_pairs={{0,4},{4,0},{8,12},{12,8},{1,5},{5,1},{9,13},{13,9},{2,6},{6,2},{1... | collective-permute-start | bytes 49160 | tf_op jit(solution)/shard_map/ppermute | solution.py:49
  76.7 2.6 %collective-permute-done.18 = f32[32,128]{1,0:T(8,128)S(1)} collective-permute-done((f32[32,128]{1,0:T(8,128)S(1)}, f32[32,128]{1,0:T(8,128)S(1)}, u32[]{:S(2)}, u32[]{:S(2)}) %collective-permute-start.18) | collective-permute-done | bytes 16416 | tf_op jit(solution)/shard_map/ppermute | solution.py:49
  79.3 1.6 %collective-permute-start.22 = (f32[128,128]{1,0:T(8,128)S(1)}, f32[128,128]{1,0:T(8,128)S(1)}, u32[]{:S(2)}, u32[]{:S(2)}) collective-permute-start(f32[128,128]{1,0:T(8,128)S(1)} %constant_dynamic-update-slice_fusion.4.refs_9_), channel_id=1, source_target_pairs={{0,2},{2,0},{1,3},{3,1},{4,6},{6,4},{5,7},{7,5},{8,10},{10,8},{9,1... | collective-permute-start | bytes 196616 | tf_op jit(solution)/shard_map/ppermute | solution.py:49
  80.9 2.7 %collective-permute-done.22.refs_11_ = f32[128,128]{1,0:T(8,128)S(1)} collective-permute-done((f32[128,128]{1,0:T(8,128)S(1)}, f32[128,128]{1,0:T(8,128)S(1)}, u32[]{:S(2)}, u32[]{:S(2)}) %collective-permute-start.22) | collective-permute-done | bytes 65568 | tf_op jit(solution)/shard_map/ppermute | solution.py:49
  83.7 1.2 %collective-permute-done.23.refs_12_ = f32[128,128]{1,0:T(8,128)S(1)} collective-permute-done((f32[128,128]{1,0:T(8,128)S(1)}, f32[128,128]{1,0:T(8,128)S(1)}, u32[]{:S(2)}, u32[]{:S(2)}) %collective-permute-start.23) | collective-permute-done | bytes 65568 | tf_op jit(solution)/shard_map/ppermute | solution.py:49
  84.9 6.6 %shard_map.72 = (f32[32,128]{1,0:T(8,128)S(1)}, f32[8,128]{1,0:T(8,128)S(1)}, f32[128,128]{1,0:T(8,128)S(1)}, f32[128,128]{1,0:T(8,128)S(1)}, f32[128,128]{1,0:T(8,128)S(1)}, /*index=5*/f32[8,128]{1,0:T(8,128)S(1)}) custom-call(s32[3072]{0:T(1024)S(1)} %bitcast.18, s32[1]{0:T(128)} %get-tuple-element.33.refs_1_, bf16[4224,128]{1,0:T(8,128)(2,1)S(1)} %shard_map.69.refs_2_, ...), custom_call_target="tpu_custom_call" | custom-call | flops 100000000 | bytes 1048576 | tf_op jit(solution)/shard_map/pallas_call | solution.py:472
  91.5 1.1 %collective-permute-start.26 = (f32[8,128]{1,0:T(8,128)S(1)}, f32[8,128]{1,0:T(8,128)S(1)}, u32[]{:S(2)}, u32[]{:S(2)}) collective-permute-start(f32[8,128]{1,0:T(8,128)S(1)} %get-tuple-element.57), channel_id=1, source_target_pairs={{0,12},{4,8},{8,4},{12,0},{1,13},{5,9},{9,5},{13,1},{2,14},{6,10},... | collective-permute-start | bytes 12296 | tf_op jit(solution)/shard_map/ppermute | solution.py:49
  92.7 1.3 %collective-permute-start.25 = (f32[8,128]{1,0:T(8,128)S(1)}, f32[8,128]{1,0:T(8,128)S(1)}, u32[]{:S(2)}, u32[]{:S(2)}) collective-permute-start(f32[8,128]{1,0:T(8,128)S(1)} %get-tuple-element.57), channel_id=1, source_target_pairs={{0,8},{4,12},{8,0},{12,4},{1,9},{5,13},{9,1},{13,5},{2,10},{6,14},... | collective-permute-start | bytes 12296 | tf_op jit(solution)/shard_map/ppermute | solution.py:49
  93.9 2.0 %collective-permute-start.24 = (f32[8,128]{1,0:T(8,128)S(1)}, f32[8,128]{1,0:T(8,128)S(1)}, u32[]{:S(2)}, u32[]{:S(2)}) collective-permute-start(f32[8,128]{1,0:T(8,128)S(1)} %get-tuple-element.57), channel_id=1, source_target_pairs={{0,4},{4,0},{8,12},{12,8},{1,5},{5,1},{9,13},{13,9},{2,6},{6,2},{1... | collective-permute-start | bytes 12296 | tf_op jit(solution)/shard_map/ppermute | solution.py:49
  96.0 1.6 %collective-permute-done.24 = f32[8,128]{1,0:T(8,128)S(1)} collective-permute-done((f32[8,128]{1,0:T(8,128)S(1)}, f32[8,128]{1,0:T(8,128)S(1)}, u32[]{:S(2)}, u32[]{:S(2)}) %collective-permute-start.24) | collective-permute-done | bytes 4128 | tf_op jit(solution)/shard_map/ppermute | solution.py:49
  97.6 1.6 %collective-permute-start.28 = (f32[64,128]{1,0:T(8,128)S(1)}, f32[64,128]{1,0:T(8,128)S(1)}, u32[]{:S(2)}, u32[]{:S(2)}) collective-permute-start(f32[64,128]{1,0:T(8,128)S(1)} %constant_dynamic-update-slice_fusion.8.refs_4_), channel_id=1, source_target_pairs={{0,2},{2,0},{1,3},{3,1},{4,6},{6,4},{5,7},{7,5},{8,10},{10,8},{9,1... | collective-permute-start | bytes 98312 | tf_op jit(solution)/shard_map/ppermute | solution.py:49
  99.2 2.4 %collective-permute-done.28.refs_6_ = f32[64,128]{1,0:T(8,128)S(1)} collective-permute-done((f32[64,128]{1,0:T(8,128)S(1)}, f32[64,128]{1,0:T(8,128)S(1)}, u32[]{:S(2)}, u32[]{:S(2)}) %collective-permute-start.28) | collective-permute-done | bytes 32800 | tf_op jit(solution)/shard_map/ppermute | solution.py:49
  101.6 1.2 %collective-permute-done.29.refs_7_ = f32[64,128]{1,0:T(8,128)S(1)} collective-permute-done((f32[64,128]{1,0:T(8,128)S(1)}, f32[64,128]{1,0:T(8,128)S(1)}, u32[]{:S(2)}, u32[]{:S(2)}) %collective-permute-start.29) | collective-permute-done | bytes 32800 | tf_op jit(solution)/shard_map/ppermute | solution.py:49
  102.8 0.7 shard_map.73
  (37 shorter events, 0.1 us)
Async XLA Ops:
  2.0 11.3 %collective-permute-start.2 = (s32[4,128]{1,0:T(4,128)S(1)}, s32[4,128]{1,0:T(4,128)S(1)}, u32[]{:S(2)}, u32[]{:S(2)}) collective-permute-start(s32[4,128]{1,0:T(4,128)S(1)} %reshape.28), channel_id=1, source_target_pairs={{0,12},{4,8},{8,4},{12,0},{1,13},{5,9},{9,5},{13,1},{2,14},{6,10},... | collective-permute-start | bytes 6152 | tf_op jit(solution)/shard_map/ppermute | solution.py:49
  7.0 6.8 %collective-permute-start.1 = (s32[4,128]{1,0:T(4,128)S(1)}, s32[4,128]{1,0:T(4,128)S(1)}, u32[]{:S(2)}, u32[]{:S(2)}) collective-permute-start(s32[4,128]{1,0:T(4,128)S(1)} %reshape.28), channel_id=1, source_target_pairs={{0,8},{4,12},{8,0},{12,4},{1,9},{5,13},{9,1},{13,5},{2,10},{6,14},... | collective-permute-start | bytes 6152 | tf_op jit(solution)/shard_map/ppermute | solution.py:49
  7.0 6.8 %collective-permute-start = (s32[4,128]{1,0:T(4,128)S(1)}, s32[4,128]{1,0:T(4,128)S(1)}, u32[]{:S(2)}, u32[]{:S(2)}) collective-permute-start(s32[4,128]{1,0:T(4,128)S(1)} %reshape.28), channel_id=1, source_target_pairs={{0,4},{4,0},{8,12},{12,8},{1,5},{5,1},{9,13},{13,9},{2,6},{6,2},{1... | collective-permute-start | bytes 6152 | tf_op jit(solution)/shard_map/ppermute | solution.py:49
  9.4 12.8 %collective-permute-start.8 = (f32[256,128]{1,0:T(8,128)S(1)}, f32[256,128]{1,0:T(8,128)S(1)}, u32[]{:S(2)}, u32[]{:S(2)}) collective-permute-start(f32[256,128]{1,0:T(8,128)S(1)} %bitcast.22), channel_id=1, source_target_pairs={{0,12},{4,8},{8,4},{12,0},{1,13},{5,9},{9,5},{13,1},{2,14},{6,10},... | collective-permute-start | bytes 393224 | tf_op jit(solution)/shard_map/ppermute | solution.py:49
  13.2 10.2 %collective-permute-start.7 = (f32[256,128]{1,0:T(8,128)S(1)}, f32[256,128]{1,0:T(8,128)S(1)}, u32[]{:S(2)}, u32[]{:S(2)}) collective-permute-start(f32[256,128]{1,0:T(8,128)S(1)} %bitcast.23), channel_id=1, source_target_pairs={{0,8},{4,12},{8,0},{12,4},{1,9},{5,13},{9,1},{13,5},{2,10},{6,14},... | collective-permute-start | bytes 393224 | tf_op jit(solution)/shard_map/ppermute | solution.py:49
  13.2 10.2 %collective-permute-start.6 = (f32[256,128]{1,0:T(8,128)S(1)}, f32[256,128]{1,0:T(8,128)S(1)}, u32[]{:S(2)}, u32[]{:S(2)}) collective-permute-start(f32[256,128]{1,0:T(8,128)S(1)} %bitcast.24), channel_id=1, source_target_pairs={{0,4},{4,0},{8,12},{12,8},{1,5},{5,1},{9,13},{13,9},{2,6},{6,2},{1... | collective-permute-start | bytes 393224 | tf_op jit(solution)/shard_map/ppermute | solution.py:49
  13.9 3.7 %collective-permute-start.4 = (s32[16,128]{1,0:T(8,128)S(1)}, s32[16,128]{1,0:T(8,128)S(1)}, u32[]{:S(2)}, u32[]{:S(2)}) collective-permute-start(s32[16,128]{1,0:T(8,128)S(1)} %pad_add_fusion.refs_0_), channel_id=1, source_target_pairs={{0,2},{2,0},{1,3},{3,1},{4,6},{6,4},{5,7},{7,5},{8,10},{10,8},{9,1... | collective-permute-start | bytes 24584 | tf_op jit(solution)/shard_map/ppermute | solution.py:49
  15.6 2.4 %collective-permute-start.3 = (s32[16,128]{1,0:T(8,128)S(1)}, s32[16,128]{1,0:T(8,128)S(1)}, u32[]{:S(2)}, u32[]{:S(2)}) collective-permute-start(s32[16,128]{1,0:T(8,128)S(1)} %pad_add_fusion.refs_0_), channel_id=1, source_target_pairs={{0,1},{1,0},{2,3},{3,2},{4,5},{5,4},{6,7},{7,6},{8,9},{9,8},{10,11... | collective-permute-start | bytes 24584 | tf_op jit(solution)/shard_map/ppermute | solution.py:49
  17.6 1.2 %collective-permute-start.5 = (s32[16,128]{1,0:T(8,128)S(1)}, s32[16,128]{1,0:T(8,128)S(1)}, u32[]{:S(2)}, u32[]{:S(2)}) collective-permute-start(s32[16,128]{1,0:T(8,128)S(1)} %collective-permute-done.4.refs_2_), channel_id=1, source_target_pairs={{0,1},{1,0},{2,3},{3,2},{4,5},{5,4},{6,7},{7,6},{8,9},{9,8},{10,11... | collective-permute-start | bytes 24584 | tf_op jit(solution)/shard_map/ppermute | solution.py:49
  23.4 1.3 %collective-permute-start.9 = (f32[256,128]{1,0:T(8,128)S(1)}, f32[256,128]{1,0:T(8,128)S(1)}, u32[]{:S(2)}, u32[]{:S(2)}) collective-permute-start(f32[256,128]{1,0:T(8,128)S(1)} %collective-permute-done.6.refs_6_), channel_id=1, source_target_pairs={{0,1},{1,0},{2,3},{3,2},{4,5},{5,4},{6,7},{7,6},{8,9},{9,8},{10,11... | collective-permute-start | bytes 393224 | tf_op jit(solution)/shard_map/ppermute | solution.py:49
  23.4 1.5 %collective-permute-start.10 = (f32[256,128]{1,0:T(8,128)S(1)}, f32[256,128]{1,0:T(8,128)S(1)}, u32[]{:S(2)}, u32[]{:S(2)}) collective-permute-start(f32[256,128]{1,0:T(8,128)S(1)} %collective-permute-done.7.refs_8_), channel_id=1, source_target_pairs={{0,1},{1,0},{2,3},{3,2},{4,5},{5,4},{6,7},{7,6},{8,9},{9,8},{10,11... | collective-permute-start | bytes 393224 | tf_op jit(solution)/shard_map/ppermute | solution.py:49
  23.9 1.3 %collective-permute-start.11 = (f32[256,128]{1,0:T(8,128)S(1)}, f32[256,128]{1,0:T(8,128)S(1)}, u32[]{:S(2)}, u32[]{:S(2)}) collective-permute-start(f32[256,128]{1,0:T(8,128)S(1)} %collective-permute-done.8.refs_10_), channel_id=1, source_target_pairs={{0,1},{1,0},{2,3},{3,2},{4,5},{5,4},{6,7},{7,6},{8,9},{9,8},{10,11... | collective-permute-start | bytes 393224 | tf_op jit(solution)/shard_map/ppermute | solution.py:49
  53.9 6.2 %collective-permute-start.14 = (f32[32,128]{1,0:T(8,128)S(1)}, f32[32,128]{1,0:T(8,128)S(1)}, u32[]{:S(2)}, u32[]{:S(2)}) collective-permute-start(f32[32,128]{1,0:T(8,128)S(1)} %get-tuple-element.42), channel_id=1, source_target_pairs={{0,12},{4,8},{8,4},{12,0},{1,13},{5,9},{9,5},{13,1},{2,14},{6,10},... | collective-permute-start | bytes 49160 | tf_op jit(solution)/shard_map/ppermute | solution.py:49
  54.1 6.1 %collective-permute-start.13 = (f32[32,128]{1,0:T(8,128)S(1)}, f32[32,128]{1,0:T(8,128)S(1)}, u32[]{:S(2)}, u32[]{:S(2)}) collective-permute-start(f32[32,128]{1,0:T(8,128)S(1)} %get-tuple-element.42), channel_id=1, source_target_pairs={{0,8},{4,12},{8,0},{12,4},{1,9},{5,13},{9,1},{13,5},{2,10},{6,14},... | collective-permute-start | bytes 49160 | tf_op jit(solution)/shard_map/ppermute | solution.py:49
  54.1 6.0 %collective-permute-start.12 = (f32[32,128]{1,0:T(8,128)S(1)}, f32[32,128]{1,0:T(8,128)S(1)}, u32[]{:S(2)}, u32[]{:S(2)}) collective-permute-start(f32[32,128]{1,0:T(8,128)S(1)} %get-tuple-element.42), channel_id=1, source_target_pairs={{0,4},{4,0},{8,12},{12,8},{1,5},{5,1},{9,13},{13,9},{2,6},{6,2},{1... | collective-permute-start | bytes 49160 | tf_op jit(solution)/shard_map/ppermute | solution.py:49
  60.1 4.3 %collective-permute-start.16 = (f32[128,128]{1,0:T(8,128)S(1)}, f32[128,128]{1,0:T(8,128)S(1)}, u32[]{:S(2)}, u32[]{:S(2)}) collective-permute-start(f32[128,128]{1,0:T(8,128)S(1)} %constant_dynamic-update-slice_fusion.refs_9_), channel_id=1, source_target_pairs={{0,2},{2,0},{1,3},{3,1},{4,6},{6,4},{5,7},{7,5},{8,10},{10,8},{9,1... | collective-permute-start | bytes 196616 | tf_op jit(solution)/shard_map/ppermute | solution.py:49
  61.7 2.8 %collective-permute-start.15 = (f32[128,128]{1,0:T(8,128)S(1)}, f32[128,128]{1,0:T(8,128)S(1)}, u32[]{:S(2)}, u32[]{:S(2)}) collective-permute-start(f32[128,128]{1,0:T(8,128)S(1)} %constant_dynamic-update-slice_fusion.refs_9_), channel_id=1, source_target_pairs={{0,1},{1,0},{2,3},{3,2},{4,5},{5,4},{6,7},{7,6},{8,9},{9,8},{10,11... | collective-permute-start | bytes 196616 | tf_op jit(solution)/shard_map/ppermute | solution.py:49
  64.5 1.3 %collective-permute-start.17 = (f32[128,128]{1,0:T(8,128)S(1)}, f32[128,128]{1,0:T(8,128)S(1)}, u32[]{:S(2)}, u32[]{:S(2)}) collective-permute-start(f32[128,128]{1,0:T(8,128)S(1)} %collective-permute-done.16.refs_11_), channel_id=1, source_target_pairs={{0,1},{1,0},{2,3},{3,2},{4,5},{5,4},{6,7},{7,6},{8,9},{9,8},{10,11... | collective-permute-start | bytes 196616 | tf_op jit(solution)/shard_map/ppermute | solution.py:49
  72.2 7.1 %collective-permute-start.20 = (f32[32,128]{1,0:T(8,128)S(1)}, f32[32,128]{1,0:T(8,128)S(1)}, u32[]{:S(2)}, u32[]{:S(2)}) collective-permute-start(f32[32,128]{1,0:T(8,128)S(1)} %get-tuple-element.51), channel_id=1, source_target_pairs={{0,12},{4,8},{8,4},{12,0},{1,13},{5,9},{9,5},{13,1},{2,14},{6,10},... | collective-permute-start | bytes 49160 | tf_op jit(solution)/shard_map/ppermute | solution.py:49
  74.3 5.0 %collective-permute-start.19 = (f32[32,128]{1,0:T(8,128)S(1)}, f32[32,128]{1,0:T(8,128)S(1)}, u32[]{:S(2)}, u32[]{:S(2)}) collective-permute-start(f32[32,128]{1,0:T(8,128)S(1)} %get-tuple-element.51), channel_id=1, source_target_pairs={{0,8},{4,12},{8,0},{12,4},{1,9},{5,13},{9,1},{13,5},{2,10},{6,14},... | collective-permute-start | bytes 49160 | tf_op jit(solution)/shard_map/ppermute | solution.py:49
  75.5 3.7 %collective-permute-start.18 = (f32[32,128]{1,0:T(8,128)S(1)}, f32[32,128]{1,0:T(8,128)S(1)}, u32[]{:S(2)}, u32[]{:S(2)}) collective-permute-start(f32[32,128]{1,0:T(8,128)S(1)} %get-tuple-element.51), channel_id=1, source_target_pairs={{0,4},{4,0},{8,12},{12,8},{1,5},{5,1},{9,13},{13,9},{2,6},{6,2},{1... | collective-permute-start | bytes 49160 | tf_op jit(solution)/shard_map/ppermute | solution.py:49
  79.3 4.3 %collective-permute-start.22 = (f32[128,128]{1,0:T(8,128)S(1)}, f32[128,128]{1,0:T(8,128)S(1)}, u32[]{:S(2)}, u32[]{:S(2)}) collective-permute-start(f32[128,128]{1,0:T(8,128)S(1)} %constant_dynamic-update-slice_fusion.4.refs_9_), channel_id=1, source_target_pairs={{0,2},{2,0},{1,3},{3,1},{4,6},{6,4},{5,7},{7,5},{8,10},{10,8},{9,1... | collective-permute-start | bytes 196616 | tf_op jit(solution)/shard_map/ppermute | solution.py:49
  80.9 2.7 %collective-permute-start.21 = (f32[128,128]{1,0:T(8,128)S(1)}, f32[128,128]{1,0:T(8,128)S(1)}, u32[]{:S(2)}, u32[]{:S(2)}) collective-permute-start(f32[128,128]{1,0:T(8,128)S(1)} %constant_dynamic-update-slice_fusion.4.refs_9_), channel_id=1, source_target_pairs={{0,1},{1,0},{2,3},{3,2},{4,5},{5,4},{6,7},{7,6},{8,9},{9,8},{10,11... | collective-permute-start | bytes 196616 | tf_op jit(solution)/shard_map/ppermute | solution.py:49
  83.6 1.3 %collective-permute-start.23 = (f32[128,128]{1,0:T(8,128)S(1)}, f32[128,128]{1,0:T(8,128)S(1)}, u32[]{:S(2)}, u32[]{:S(2)}) collective-permute-start(f32[128,128]{1,0:T(8,128)S(1)} %collective-permute-done.22.refs_11_), channel_id=1, source_target_pairs={{0,1},{1,0},{2,3},{3,2},{4,5},{5,4},{6,7},{7,6},{8,9},{9,8},{10,11... | collective-permute-start | bytes 196616 | tf_op jit(solution)/shard_map/ppermute | solution.py:49
  91.5 6.0 %collective-permute-start.26 = (f32[8,128]{1,0:T(8,128)S(1)}, f32[8,128]{1,0:T(8,128)S(1)}, u32[]{:S(2)}, u32[]{:S(2)}) collective-permute-start(f32[8,128]{1,0:T(8,128)S(1)} %get-tuple-element.57), channel_id=1, source_target_pairs={{0,12},{4,8},{8,4},{12,0},{1,13},{5,9},{9,5},{13,1},{2,14},{6,10},... | collective-permute-start | bytes 12296 | tf_op jit(solution)/shard_map/ppermute | solution.py:49
  92.7 4.9 %collective-permute-start.25 = (f32[8,128]{1,0:T(8,128)S(1)}, f32[8,128]{1,0:T(8,128)S(1)}, u32[]{:S(2)}, u32[]{:S(2)}) collective-permute-start(f32[8,128]{1,0:T(8,128)S(1)} %get-tuple-element.57), channel_id=1, source_target_pairs={{0,8},{4,12},{8,0},{12,4},{1,9},{5,13},{9,1},{13,5},{2,10},{6,14},... | collective-permute-start | bytes 12296 | tf_op jit(solution)/shard_map/ppermute | solution.py:49
  93.9 3.6 %collective-permute-start.24 = (f32[8,128]{1,0:T(8,128)S(1)}, f32[8,128]{1,0:T(8,128)S(1)}, u32[]{:S(2)}, u32[]{:S(2)}) collective-permute-start(f32[8,128]{1,0:T(8,128)S(1)} %get-tuple-element.57), channel_id=1, source_target_pairs={{0,4},{4,0},{8,12},{12,8},{1,5},{5,1},{9,13},{13,9},{2,6},{6,2},{1... | collective-permute-start | bytes 12296 | tf_op jit(solution)/shard_map/ppermute | solution.py:49
  97.6 4.0 %collective-permute-start.28 = (f32[64,128]{1,0:T(8,128)S(1)}, f32[64,128]{1,0:T(8,128)S(1)}, u32[]{:S(2)}, u32[]{:S(2)}) collective-permute-start(f32[64,128]{1,0:T(8,128)S(1)} %constant_dynamic-update-slice_fusion.8.refs_4_), channel_id=1, source_target_pairs={{0,2},{2,0},{1,3},{3,1},{4,6},{6,4},{5,7},{7,5},{8,10},{10,8},{9,1... | collective-permute-start | bytes 98312 | tf_op jit(solution)/shard_map/ppermute | solution.py:49
  99.2 2.4 %collective-permute-start.27 = (f32[64,128]{1,0:T(8,128)S(1)}, f32[64,128]{1,0:T(8,128)S(1)}, u32[]{:S(2)}, u32[]{:S(2)}) collective-permute-start(f32[64,128]{1,0:T(8,128)S(1)} %constant_dynamic-update-slice_fusion.8.refs_4_), channel_id=1, source_target_pairs={{0,1},{1,0},{2,3},{3,2},{4,5},{5,4},{6,7},{7,6},{8,9},{9,8},{10,11... | collective-permute-start | bytes 98312 | tf_op jit(solution)/shard_map/ppermute | solution.py:49
  101.6 1.2 %collective-permute-start.29 = (f32[64,128]{1,0:T(8,128)S(1)}, f32[64,128]{1,0:T(8,128)S(1)}, u32[]{:S(2)}, u32[]{:S(2)}) collective-permute-start(f32[64,128]{1,0:T(8,128)S(1)} %collective-permute-done.28.refs_6_), channel_id=1, source_target_pairs={{0,1},{1,0},{2,3},{3,2},{4,5},{5,4},{6,7},{7,6},{8,9},{9,8},{10,11... | collective-permute-start | bytes 98312 | tf_op jit(solution)/shard_map/ppermute | solution.py:49

commit v4 on v3

--- a/solution.py
+++ b/solution.py
@@ -10,7 +10,6 @@
 BS = 128
 ITERS = 3
 SUPPORT = 0.3
-HALF_LOG2E = 0.7213475204444817
 DEPTH = 48
 UNROLL = 16
 ARRAYS = 4
@@ -176,14 +175,15 @@
     from_here, after = lax.fori_loop(0, chunks, tally, (zero, zero))
     from_here = jnp.sum(from_here, axis=0, keepdims=True)
     each = from_here - jnp.sum(after, axis=0, keepdims=True)
-    odd = jnp.where(lane < sz.own, each - 2.0 * jnp.floor(0.5 * each), 0.0)
-    wide_odd = jnp.broadcast_to(odd, (BS, BS))
-    odd_column = wide_odd.T
-    odd_before = jnp.dot(wide_odd.astype(BF16), ahead, preferred_element_type=F32)[0:1, :]
-    start = (chunks * BS).astype(F32) - from_here + odd_before
-    null_place = jnp.where(odd > 0.0, start + each, -1.0)
+    odd = each - 2.0 * jnp.floor(0.5 * each)
+    pad = jnp.where(lane < sz.own, jnp.where(each == 0.0, 2.0, odd), 0.0)
+    wide_pad = jnp.broadcast_to(pad, (BS, BS))
+    pad_column = wide_pad.T
+    pad_before = jnp.dot(wide_pad.astype(BF16), ahead, preferred_element_type=F32)[0:1, :]
+    start = (chunks * BS).astype(F32) - from_here + pad_before
+    null_places = (jnp.where(pad > 0.0, start + each, -1.0), jnp.where(pad > 1.0, start + 1.0, -1.0))
     null_entry = (lane + 256 * sz.blocks).astype(F32)
-    full = count + jnp.sum(odd).astype(jnp.int32)
+    full = count + jnp.sum(pad).astype(jnp.int32)
     count_ref[0] = full
 
     def rank(c, unused):
@@ -194,7 +194,7 @@
             return total + jnp.where(lower, 1.0, 0.0)
 
         past = (sub + 1).astype(F32) * 65536.0 <= keys
-        total = lax.fori_loop(0, chunks, below, jnp.where(past, odd_column, 0.0))
+        total = lax.fori_loop(0, chunks, below, jnp.where(past, pad_column, 0.0))
         place[pl.ds(c, 1), :] = jnp.sum(total, axis=0, keepdims=True)
         return unused
 
@@ -207,7 +207,8 @@
             hit = place[pl.ds(r, 1), :] == slot
             return total + jnp.where(hit, entry_row[pl.ds(r, 1), :], 0.0)
 
-        total = lax.fori_loop(0, chunks, line, jnp.where(null_place == slot, null_entry, 0.0))
+        nulls = jnp.logical_or(null_places[0] == slot, null_places[1] == slot)
+        total = lax.fori_loop(0, chunks, line, jnp.where(nulls, null_entry, 0.0))
         found = jnp.sum(total.T, axis=0, keepdims=True).astype(jnp.int32)
         out_ref[pl.ds(c, 1), :] = jnp.where(lane + c * BS < full, found, sz.own)
         return unused
@@ -226,7 +227,7 @@
 
 def taper_of(squared):
     squared = jnp.maximum(squared, 1e-20)
-    remain = jnp.maximum(4.0 - jnp.exp2(jnp.log(squared) * HALF_LOG2E), 0.0)
+    remain = jnp.maximum(4.0 - squared * lax.rsqrt(squared), 0.0)
     twice = remain * remain
     return twice * twice * (5.0 - remain)
 
@@ -247,11 +248,6 @@
 
 def other_features(rhs_ref, j):
     return rhs_ref[pl.ds(pl.multiple_of(j * DEPTH, DEPTH), DEPTH), :]
-
-
-def clear(*accs):
-    for acc in accs:
-        acc[...] = jnp.zeros_like(acc)
 
 
 def generate(sz, list_ref, count, lhs_ref, rhs_ref, tile_refs, squares):
@@ -284,7 +280,12 @@
 
 def sweep(sz, list_ref, count, tile_refs, vec_ref, acc, acc_ones=None):
     accs = [acc] if acc_ones is None else [acc, acc_ones]
-    clear(*accs)
+
+    @pl.when(count > sz.kept * len(tile_refs))
+    def some_targets_are_extra():
+        for ref in accs:
+            ref[...] = jnp.zeros_like(ref)
+
     zero = jnp.zeros((8, BS), F32)
     carry = (jnp.int32(-1),) + ((zero,) * (BS // 8),) * len(accs)
     for at, tile_ref in enumerate(tile_refs):

time: 103 us -> 99.6 us (0.967); the launches traced: 103 us -> 98.3 us
  Pallas kernels: 46.2 us -> 37.6 us
  starting transfers between devices: 30.5 us -> 32.8 us
  waiting for transfers between devices: 22.9 us -> 24 us
    pallas_call x6, Pallas kernels: 46.2 us -> 37.6 us  [call(): pl.pallas_call(kernel, in_specs=in_specs, out_shape=shapes, out_specs=out...]
    ppermute x30, starting transfers between devices: 30.5 us -> 32.8 us  [swap(): lax.ppermute(x, axis, [(i, i ^ code) for i in range(lax.axis_size(axis))])]
    ppermute x30, waiting for transfers between devices: 22.9 us -> 24 us  [swap(): lax.ppermute(x, axis, [(i, i ^ code) for i in range(lax.axis_size(axis))])]
  transfers between devices with their start and end apart: 30 -> 30, of which waited for: 15 -> 17; matrix products, arithmetic and copies ran while one was open for 2% -> 2% of each run, Pallas kernels for 4% -> 3%
where the time goes in v4:
time: 99.6 us; the launch traced here: 98.3 us
  Pallas kernels  37.6 us (38%)
  starting transfers between devices  32.8 us (33%)
  waiting for transfers between devices  24 us (24%)
  other arithmetic  1.48 us (1%)
  between operations  1.4 us (1%)
  local copies, waits for them, and re-layouts  1.01 us (1%)
    pallas_call x6, Pallas kernels, call(): pl.pallas_call(kernel, in_specs=in_specs, out_shape=shapes, out_specs=out...  37.6 us
    ppermute x30, starting transfers between devices, swap(): lax.ppermute(x, axis, [(i, i ^ code) for i in range(lax.axis_size(axis))])  32.8 us
    ppermute x30, waiting for transfers between devices, swap(): lax.ppermute(x, axis, [(i, i ^ code) for i in range(lax.axis_size(axis))])  24 us
  transfers between devices with their start and end apart: 30, of which 17 were waited for; matrix products, arithmetic and copies ran while one was open for 2% of the time, Pallas kernels for 3%

profile of v4, /device:TPU:0, one launch (start us, length us, event | category | flops | bytes accessed | tf_op | source)
XLA Modules:
  0.0 98.3 jit_solution(11941191519281860902)
XLA Ops:
  1.3 0.7 broadcast_select_fusion
  2.0 5.0 %collective-permute-start.2 = (s32[4,128]{1,0:T(4,128)S(1)}, s32[4,128]{1,0:T(4,128)S(1)}, u32[]{:S(2)}, u32[]{:S(2)}) collective-permute-start(s32[4,128]{1,0:T(4,128)S(1)} %reshape.28), channel_id=1, source_target_pairs={{0,12},{4,8},{8,4},{12,0},{1,13},{5,9},{9,5},{13,1},{2,14},{6,10},... | collective-permute-start | bytes 6152 | tf_op jit(solution)/shard_map/ppermute | solution.py:48
  7.0 0.0 collective-permute-start.1
  7.0 0.6 collective-permute-start
  7.7 1.0 copy.9
  8.6 0.8 fusion
  9.4 3.8 %collective-permute-start.8 = (f32[256,128]{1,0:T(8,128)S(1)}, f32[256,128]{1,0:T(8,128)S(1)}, u32[]{:S(2)}, u32[]{:S(2)}) collective-permute-start(f32[256,128]{1,0:T(8,128)S(1)} %bitcast.22), channel_id=1, source_target_pairs={{0,12},{4,8},{8,4},{12,0},{1,13},{5,9},{9,5},{13,1},{2,14},{6,10},... | collective-permute-start | bytes 393224 | tf_op jit(solution)/shard_map/ppermute | solution.py:48
  13.2 0.6 collective-permute-start.6
  13.9 1.7 %collective-permute-start.4 = (s32[16,128]{1,0:T(8,128)S(1)}, s32[16,128]{1,0:T(8,128)S(1)}, u32[]{:S(2)}, u32[]{:S(2)}) collective-permute-start(s32[16,128]{1,0:T(8,128)S(1)} %pad_add_fusion.refs_0_), channel_id=1, source_target_pairs={{0,2},{2,0},{1,3},{3,1},{4,6},{6,4},{5,7},{7,5},{8,10},{10,8},{9,1... | collective-permute-start | bytes 24584 | tf_op jit(solution)/shard_map/ppermute | solution.py:48
  15.6 2.0 %collective-permute-done.4.refs_2_ = s32[16,128]{1,0:T(8,128)S(1)} collective-permute-done((s32[16,128]{1,0:T(8,128)S(1)}, s32[16,128]{1,0:T(8,128)S(1)}, u32[]{:S(2)}, u32[]{:S(2)}) %collective-permute-start.4) | collective-permute-done | bytes 8224 | tf_op jit(solution)/shard_map/ppermute | solution.py:48
  17.6 0.0 collective-permute-start.5
  17.6 0.4 shard_map.69.refs_2_
  18.0 0.0 collective-permute-done.3.refs_1_
  18.0 0.8 collective-permute-done.5.refs_3_
  18.8 2.8 %shard_map.68 = (s32[24,128]{1,0:T(8,128)S(1)}, s32[1]{0:T(128)}) custom-call(s32[16,128]{1,0:T(8,128)S(1)} %pad_add_fusion.refs_0_, s32[16,128]{1,0:T(8,128)S(1)} %collective-permute-done.3.refs_1_, s32[16,128]{1,0:T(8,128)S(1)} %collective-permute-done.4.refs_2_, s32[16,128]{1,0:T(8,128)S(1)} %collective-permute-done.5.refs_3_), custom_call_target="tpu_custom_call" | custom-call | flops 10000000 | bytes 1048576 | tf_op jit(solution)/shard_map/pallas_call | solution.py:473
  21.6 1.8 %collective-permute-done.7.refs_8_ = f32[256,128]{1,0:T(8,128)S(1)} collective-permute-done((f32[256,128]{1,0:T(8,128)S(1)}, f32[256,128]{1,0:T(8,128)S(1)}, u32[]{:S(2)}, u32[]{:S(2)}) %collective-permute-start.7) | collective-permute-done | bytes 131104 | tf_op jit(solution)/shard_map/ppermute | solution.py:48
  23.4 0.5 collective-permute-start.10
  23.9 0.0 collective-permute-start.11
  23.9 0.8 collective-permute-done.9.refs_7_
  24.8 0.2 collective-permute-done.10.refs_9_
  25.0 0.3 collective-permute-done.11.refs_11_
  25.3 22.0 %shard_map.70 = (f32[14336,128]{1,0:T(8,128)S(1)}, f32[14336,128]{1,0:T(8,128)S(1)}, f32[14336,128]{1,0:T(8,128)S(1)}, f32[14336,128]{1,0:T(8,128)S(1)}, bf16[24...) custom-call(s32[3072]{0:T(1024)S(1)} %bitcast.16, ...), custom_call_target="tpu_custom_call" | custom-call | flops 100000000 | bytes 1048576 | tf_op jit(solution)/shard_map/pallas_call | solution.py:473
  47.3 3.1 %collective-permute-start.14 = (f32[32,128]{1,0:T(8,128)S(1)}, f32[32,128]{1,0:T(8,128)S(1)}, u32[]{:S(2)}, u32[]{:S(2)}) collective-permute-start(f32[32,128]{1,0:T(8,128)S(1)} %get-tuple-element.42), channel_id=1, source_target_pairs={{0,12},{4,8},{8,4},{12,0},{1,13},{5,9},{9,5},{13,1},{2,14},{6,10},... | collective-permute-start | bytes 49160 | tf_op jit(solution)/shard_map/ppermute | solution.py:48
  50.3 0.0 collective-permute-start.13
  50.3 1.4 %collective-permute-start.12 = (f32[32,128]{1,0:T(8,128)S(1)}, f32[32,128]{1,0:T(8,128)S(1)}, u32[]{:S(2)}, u32[]{:S(2)}) collective-permute-start(f32[32,128]{1,0:T(8,128)S(1)} %get-tuple-element.42), channel_id=1, source_target_pairs={{0,4},{4,0},{8,12},{12,8},{1,5},{5,1},{9,13},{13,9},{2,6},{6,2},{1... | collective-permute-start | bytes 49160 | tf_op jit(solution)/shard_map/ppermute | solution.py:48
  51.7 2.3 %collective-permute-done.12 = f32[32,128]{1,0:T(8,128)S(1)} collective-permute-done((f32[32,128]{1,0:T(8,128)S(1)}, f32[32,128]{1,0:T(8,128)S(1)}, u32[]{:S(2)}, u32[]{:S(2)}) %collective-permute-start.12) | collective-permute-done | bytes 16416 | tf_op jit(solution)/shard_map/ppermute | solution.py:48
  54.1 0.9 collective-permute-done.13
  55.0 2.9 %collective-permute-start.16 = (f32[128,128]{1,0:T(8,128)S(1)}, f32[128,128]{1,0:T(8,128)S(1)}, u32[]{:S(2)}, u32[]{:S(2)}) collective-permute-start(f32[128,128]{1,0:T(8,128)S(1)} %constant_dynamic-update-slice_fusion.refs_9_), channel_id=1, source_target_pairs={{0,2},{2,0},{1,3},{3,1},{4,6},{6,4},{5,7},{7,5},{8,10},{10,8},{9,1... | collective-permute-start | bytes 196616 | tf_op jit(solution)/shard_map/ppermute | solution.py:48
  57.8 2.2 %collective-permute-done.16.refs_11_ = f32[128,128]{1,0:T(8,128)S(1)} collective-permute-done((f32[128,128]{1,0:T(8,128)S(1)}, f32[128,128]{1,0:T(8,128)S(1)}, u32[]{:S(2)}, u32[]{:S(2)}) %collective-permute-start.16) | collective-permute-done | bytes 65568 | tf_op jit(solution)/shard_map/ppermute | solution.py:48
  60.1 1.2 %collective-permute-done.17.refs_12_ = f32[128,128]{1,0:T(8,128)S(1)} collective-permute-done((f32[128,128]{1,0:T(8,128)S(1)}, f32[128,128]{1,0:T(8,128)S(1)}, u32[]{:S(2)}, u32[]{:S(2)}) %collective-permute-start.17) | collective-permute-done | bytes 65568 | tf_op jit(solution)/shard_map/ppermute | solution.py:48
  61.3 5.9 %shard_map.71 = (f32[32,128]{1,0:T(8,128)S(1)}, f32[8,128]{1,0:T(8,128)S(1)}, f32[128,128]{1,0:T(8,128)S(1)}, f32[512,128]{1,0:T(8,128)S(1)}, f32[512,128]{1,0:T(8,128)S(1)}) custom-call(s32[3072]{0:T(1024)S(1)} %bitcast.17, s32[1]{0:T(128)} %get-tuple-element.33.refs_1_, bf16[4224,128]{1,0:T(8,128)(2,1)S(1)} %shard_map.69.refs_2_, ...), custom_call_target="tpu_custom_call" | custom-call | flops 100000000 | bytes 1048576 | tf_op jit(solution)/shard_map/pallas_call | solution.py:473
  67.2 1.7 %collective-permute-start.20 = (f32[32,128]{1,0:T(8,128)S(1)}, f32[32,128]{1,0:T(8,128)S(1)}, u32[]{:S(2)}, u32[]{:S(2)}) collective-permute-start(f32[32,128]{1,0:T(8,128)S(1)} %get-tuple-element.51), channel_id=1, source_target_pairs={{0,12},{4,8},{8,4},{12,0},{1,13},{5,9},{9,5},{13,1},{2,14},{6,10},... | collective-permute-start | bytes 49160 | tf_op jit(solution)/shard_map/ppermute | solution.py:48
  68.9 0.3 collective-permute-start.19
  69.2 2.5 %collective-permute-start.18 = (f32[32,128]{1,0:T(8,128)S(1)}, f32[32,128]{1,0:T(8,128)S(1)}, u32[]{:S(2)}, u32[]{:S(2)}) collective-permute-start(f32[32,128]{1,0:T(8,128)S(1)} %get-tuple-element.51), channel_id=1, source_target_pairs={{0,4},{4,0},{8,12},{12,8},{1,5},{5,1},{9,13},{13,9},{2,6},{6,2},{1... | collective-permute-start | bytes 49160 | tf_op jit(solution)/shard_map/ppermute | solution.py:48
  71.7 1.7 %collective-permute-done.18 = f32[32,128]{1,0:T(8,128)S(1)} collective-permute-done((f32[32,128]{1,0:T(8,128)S(1)}, f32[32,128]{1,0:T(8,128)S(1)}, u32[]{:S(2)}, u32[]{:S(2)}) %collective-permute-start.18) | collective-permute-done | bytes 16416 | tf_op jit(solution)/shard_map/ppermute | solution.py:48
  73.4 0.2 collective-permute-done.19
  73.6 2.4 %collective-permute-start.22 = (f32[128,128]{1,0:T(8,128)S(1)}, f32[128,128]{1,0:T(8,128)S(1)}, u32[]{:S(2)}, u32[]{:S(2)}) collective-permute-start(f32[128,128]{1,0:T(8,128)S(1)} %constant_dynamic-update-slice_fusion.4.refs_9_), channel_id=1, source_target_pairs={{0,2},{2,0},{1,3},{3,1},{4,6},{6,4},{5,7},{7,5},{8,10},{10,8},{9,1... | collective-permute-start | bytes 196616 | tf_op jit(solution)/shard_map/ppermute | solution.py:48
  76.0 2.2 %collective-permute-done.22.refs_11_ = f32[128,128]{1,0:T(8,128)S(1)} collective-permute-done((f32[128,128]{1,0:T(8,128)S(1)}, f32[128,128]{1,0:T(8,128)S(1)}, u32[]{:S(2)}, u32[]{:S(2)}) %collective-permute-start.22) | collective-permute-done | bytes 65568 | tf_op jit(solution)/shard_map/ppermute | solution.py:48
  78.2 1.2 %collective-permute-done.23.refs_12_ = f32[128,128]{1,0:T(8,128)S(1)} collective-permute-done((f32[128,128]{1,0:T(8,128)S(1)}, f32[128,128]{1,0:T(8,128)S(1)}, u32[]{:S(2)}, u32[]{:S(2)}) %collective-permute-start.23) | collective-permute-done | bytes 65568 | tf_op jit(solution)/shard_map/ppermute | solution.py:48
  79.5 5.9 %shard_map.72 = (f32[32,128]{1,0:T(8,128)S(1)}, f32[8,128]{1,0:T(8,128)S(1)}, f32[128,128]{1,0:T(8,128)S(1)}, f32[128,128]{1,0:T(8,128)S(1)}, f32[128,128]{1,0:T(8,128)S(1)}, /*index=5*/f32[8,128]{1,0:T(8,128)S(1)}) custom-call(s32[3072]{0:T(1024)S(1)} %bitcast.18, s32[1]{0:T(128)} %get-tuple-element.33.refs_1_, bf16[4224,128]{1,0:T(8,128)(2,1)S(1)} %shard_map.69.refs_2_, ...), custom_call_target="tpu_custom_call" | custom-call | flops 100000000 | bytes 1048576 | tf_op jit(solution)/shard_map/pallas_call | solution.py:473
  85.4 2.3 %collective-permute-start.26 = (f32[8,128]{1,0:T(8,128)S(1)}, f32[8,128]{1,0:T(8,128)S(1)}, u32[]{:S(2)}, u32[]{:S(2)}) collective-permute-start(f32[8,128]{1,0:T(8,128)S(1)} %get-tuple-element.57), channel_id=1, source_target_pairs={{0,12},{4,8},{8,4},{12,0},{1,13},{5,9},{9,5},{13,1},{2,14},{6,10},... | collective-permute-start | bytes 12296 | tf_op jit(solution)/shard_map/ppermute | solution.py:48
  87.7 1.1 %collective-permute-start.25 = (f32[8,128]{1,0:T(8,128)S(1)}, f32[8,128]{1,0:T(8,128)S(1)}, u32[]{:S(2)}, u32[]{:S(2)}) collective-permute-start(f32[8,128]{1,0:T(8,128)S(1)} %get-tuple-element.57), channel_id=1, source_target_pairs={{0,8},{4,12},{8,0},{12,4},{1,9},{5,13},{9,1},{13,5},{2,10},{6,14},... | collective-permute-start | bytes 12296 | tf_op jit(solution)/shard_map/ppermute | solution.py:48
  88.8 1.1 %collective-permute-start.24 = (f32[8,128]{1,0:T(8,128)S(1)}, f32[8,128]{1,0:T(8,128)S(1)}, u32[]{:S(2)}, u32[]{:S(2)}) collective-permute-start(f32[8,128]{1,0:T(8,128)S(1)} %get-tuple-element.57), channel_id=1, source_target_pairs={{0,4},{4,0},{8,12},{12,8},{1,5},{5,1},{9,13},{13,9},{2,6},{6,2},{1... | collective-permute-start | bytes 12296 | tf_op jit(solution)/shard_map/ppermute | solution.py:48
  89.9 2.5 %collective-permute-done.24 = f32[8,128]{1,0:T(8,128)S(1)} collective-permute-done((f32[8,128]{1,0:T(8,128)S(1)}, f32[8,128]{1,0:T(8,128)S(1)}, u32[]{:S(2)}, u32[]{:S(2)}) %collective-permute-start.24) | collective-permute-done | bytes 4128 | tf_op jit(solution)/shard_map/ppermute | solution.py:48
  92.4 1.8 %collective-permute-start.28 = (f32[64,128]{1,0:T(8,128)S(1)}, f32[64,128]{1,0:T(8,128)S(1)}, u32[]{:S(2)}, u32[]{:S(2)}) collective-permute-start(f32[64,128]{1,0:T(8,128)S(1)} %constant_dynamic-update-slice_fusion.8.refs_4_), channel_id=1, source_target_pairs={{0,2},{2,0},{1,3},{3,1},{4,6},{6,4},{5,7},{7,5},{8,10},{10,8},{9,1... | collective-permute-start | bytes 98312 | tf_op jit(solution)/shard_map/ppermute | solution.py:48
  94.2 2.1 %collective-permute-done.28.refs_6_ = f32[64,128]{1,0:T(8,128)S(1)} collective-permute-done((f32[64,128]{1,0:T(8,128)S(1)}, f32[64,128]{1,0:T(8,128)S(1)}, u32[]{:S(2)}, u32[]{:S(2)}) %collective-permute-start.28) | collective-permute-done | bytes 32800 | tf_op jit(solution)/shard_map/ppermute | solution.py:48
  96.4 1.2 %collective-permute-done.29.refs_7_ = f32[64,128]{1,0:T(8,128)S(1)} collective-permute-done((f32[64,128]{1,0:T(8,128)S(1)}, f32[64,128]{1,0:T(8,128)S(1)}, u32[]{:S(2)}, u32[]{:S(2)}) %collective-permute-start.29) | collective-permute-done | bytes 32800 | tf_op jit(solution)/shard_map/ppermute | solution.py:48
  97.6 0.7 shard_map.73
  (37 shorter events, 0.1 us)
Async XLA Ops:
  2.0 11.3 %collective-permute-start.2 = (s32[4,128]{1,0:T(4,128)S(1)}, s32[4,128]{1,0:T(4,128)S(1)}, u32[]{:S(2)}, u32[]{:S(2)}) collective-permute-start(s32[4,128]{1,0:T(4,128)S(1)} %reshape.28), channel_id=1, source_target_pairs={{0,12},{4,8},{8,4},{12,0},{1,13},{5,9},{9,5},{13,1},{2,14},{6,10},... | collective-permute-start | bytes 6152 | tf_op jit(solution)/shard_map/ppermute | solution.py:48
  7.0 6.8 %collective-permute-start.1 = (s32[4,128]{1,0:T(4,128)S(1)}, s32[4,128]{1,0:T(4,128)S(1)}, u32[]{:S(2)}, u32[]{:S(2)}) collective-permute-start(s32[4,128]{1,0:T(4,128)S(1)} %reshape.28), channel_id=1, source_target_pairs={{0,8},{4,12},{8,0},{12,4},{1,9},{5,13},{9,1},{13,5},{2,10},{6,14},... | collective-permute-start | bytes 6152 | tf_op jit(solution)/shard_map/ppermute | solution.py:48
  7.0 6.8 %collective-permute-start = (s32[4,128]{1,0:T(4,128)S(1)}, s32[4,128]{1,0:T(4,128)S(1)}, u32[]{:S(2)}, u32[]{:S(2)}) collective-permute-start(s32[4,128]{1,0:T(4,128)S(1)} %reshape.28), channel_id=1, source_target_pairs={{0,4},{4,0},{8,12},{12,8},{1,5},{5,1},{9,13},{13,9},{2,6},{6,2},{1... | collective-permute-start | bytes 6152 | tf_op jit(solution)/shard_map/ppermute | solution.py:48
  9.4 12.2 %collective-permute-start.8 = (f32[256,128]{1,0:T(8,128)S(1)}, f32[256,128]{1,0:T(8,128)S(1)}, u32[]{:S(2)}, u32[]{:S(2)}) collective-permute-start(f32[256,128]{1,0:T(8,128)S(1)} %bitcast.22), channel_id=1, source_target_pairs={{0,12},{4,8},{8,4},{12,0},{1,13},{5,9},{9,5},{13,1},{2,14},{6,10},... | collective-permute-start | bytes 393224 | tf_op jit(solution)/shard_map/ppermute | solution.py:48
  13.2 10.2 %collective-permute-start.7 = (f32[256,128]{1,0:T(8,128)S(1)}, f32[256,128]{1,0:T(8,128)S(1)}, u32[]{:S(2)}, u32[]{:S(2)}) collective-permute-start(f32[256,128]{1,0:T(8,128)S(1)} %bitcast.23), channel_id=1, source_target_pairs={{0,8},{4,12},{8,0},{12,4},{1,9},{5,13},{9,1},{13,5},{2,10},{6,14},... | collective-permute-start | bytes 393224 | tf_op jit(solution)/shard_map/ppermute | solution.py:48
  13.2 10.2 %collective-permute-start.6 = (f32[256,128]{1,0:T(8,128)S(1)}, f32[256,128]{1,0:T(8,128)S(1)}, u32[]{:S(2)}, u32[]{:S(2)}) collective-permute-start(f32[256,128]{1,0:T(8,128)S(1)} %bitcast.24), channel_id=1, source_target_pairs={{0,4},{4,0},{8,12},{12,8},{1,5},{5,1},{9,13},{13,9},{2,6},{6,2},{1... | collective-permute-start | bytes 393224 | tf_op jit(solution)/shard_map/ppermute | solution.py:48
  13.9 3.7 %collective-permute-start.4 = (s32[16,128]{1,0:T(8,128)S(1)}, s32[16,128]{1,0:T(8,128)S(1)}, u32[]{:S(2)}, u32[]{:S(2)}) collective-permute-start(s32[16,128]{1,0:T(8,128)S(1)} %pad_add_fusion.refs_0_), channel_id=1, source_target_pairs={{0,2},{2,0},{1,3},{3,1},{4,6},{6,4},{5,7},{7,5},{8,10},{10,8},{9,1... | collective-permute-start | bytes 24584 | tf_op jit(solution)/shard_map/ppermute | solution.py:48
  15.6 2.4 %collective-permute-start.3 = (s32[16,128]{1,0:T(8,128)S(1)}, s32[16,128]{1,0:T(8,128)S(1)}, u32[]{:S(2)}, u32[]{:S(2)}) collective-permute-start(s32[16,128]{1,0:T(8,128)S(1)} %pad_add_fusion.refs_0_), channel_id=1, source_target_pairs={{0,1},{1,0},{2,3},{3,2},{4,5},{5,4},{6,7},{7,6},{8,9},{9,8},{10,11... | collective-permute-start | bytes 24584 | tf_op jit(solution)/shard_map/ppermute | solution.py:48
  17.6 1.2 %collective-permute-start.5 = (s32[16,128]{1,0:T(8,128)S(1)}, s32[16,128]{1,0:T(8,128)S(1)}, u32[]{:S(2)}, u32[]{:S(2)}) collective-permute-start(s32[16,128]{1,0:T(8,128)S(1)} %collective-permute-done.4.refs_2_), channel_id=1, source_target_pairs={{0,1},{1,0},{2,3},{3,2},{4,5},{5,4},{6,7},{7,6},{8,9},{9,8},{10,11... | collective-permute-start | bytes 24584 | tf_op jit(solution)/shard_map/ppermute | solution.py:48
  23.4 1.3 %collective-permute-start.9 = (f32[256,128]{1,0:T(8,128)S(1)}, f32[256,128]{1,0:T(8,128)S(1)}, u32[]{:S(2)}, u32[]{:S(2)}) collective-permute-start(f32[256,128]{1,0:T(8,128)S(1)} %collective-permute-done.6.refs_6_), channel_id=1, source_target_pairs={{0,1},{1,0},{2,3},{3,2},{4,5},{5,4},{6,7},{7,6},{8,9},{9,8},{10,11... | collective-permute-start | bytes 393224 | tf_op jit(solution)/shard_map/ppermute | solution.py:48
  23.4 1.5 %collective-permute-start.10 = (f32[256,128]{1,0:T(8,128)S(1)}, f32[256,128]{1,0:T(8,128)S(1)}, u32[]{:S(2)}, u32[]{:S(2)}) collective-permute-start(f32[256,128]{1,0:T(8,128)S(1)} %collective-permute-done.7.refs_8_), channel_id=1, source_target_pairs={{0,1},{1,0},{2,3},{3,2},{4,5},{5,4},{6,7},{7,6},{8,9},{9,8},{10,11... | collective-permute-start | bytes 393224 | tf_op jit(solution)/shard_map/ppermute | solution.py:48
  23.9 1.3 %collective-permute-start.11 = (f32[256,128]{1,0:T(8,128)S(1)}, f32[256,128]{1,0:T(8,128)S(1)}, u32[]{:S(2)}, u32[]{:S(2)}) collective-permute-start(f32[256,128]{1,0:T(8,128)S(1)} %collective-permute-done.8.refs_10_), channel_id=1, source_target_pairs={{0,1},{1,0},{2,3},{3,2},{4,5},{5,4},{6,7},{7,6},{8,9},{9,8},{10,11... | collective-permute-start | bytes 393224 | tf_op jit(solution)/shard_map/ppermute | solution.py:48
  47.3 7.7 %collective-permute-start.14 = (f32[32,128]{1,0:T(8,128)S(1)}, f32[32,128]{1,0:T(8,128)S(1)}, u32[]{:S(2)}, u32[]{:S(2)}) collective-permute-start(f32[32,128]{1,0:T(8,128)S(1)} %get-tuple-element.42), channel_id=1, source_target_pairs={{0,12},{4,8},{8,4},{12,0},{1,13},{5,9},{9,5},{13,1},{2,14},{6,10},... | collective-permute-start | bytes 49160 | tf_op jit(solution)/shard_map/ppermute | solution.py:48
  50.3 4.6 %collective-permute-start.13 = (f32[32,128]{1,0:T(8,128)S(1)}, f32[32,128]{1,0:T(8,128)S(1)}, u32[]{:S(2)}, u32[]{:S(2)}) collective-permute-start(f32[32,128]{1,0:T(8,128)S(1)} %get-tuple-element.42), channel_id=1, source_target_pairs={{0,8},{4,12},{8,0},{12,4},{1,9},{5,13},{9,1},{13,5},{2,10},{6,14},... | collective-permute-start | bytes 49160 | tf_op jit(solution)/shard_map/ppermute | solution.py:48
  50.3 3.7 %collective-permute-start.12 = (f32[32,128]{1,0:T(8,128)S(1)}, f32[32,128]{1,0:T(8,128)S(1)}, u32[]{:S(2)}, u32[]{:S(2)}) collective-permute-start(f32[32,128]{1,0:T(8,128)S(1)} %get-tuple-element.42), channel_id=1, source_target_pairs={{0,4},{4,0},{8,12},{12,8},{1,5},{5,1},{9,13},{13,9},{2,6},{6,2},{1... | collective-permute-start | bytes 49160 | tf_op jit(solution)/shard_map/ppermute | solution.py:48
  55.0 5.1 %collective-permute-start.16 = (f32[128,128]{1,0:T(8,128)S(1)}, f32[128,128]{1,0:T(8,128)S(1)}, u32[]{:S(2)}, u32[]{:S(2)}) collective-permute-start(f32[128,128]{1,0:T(8,128)S(1)} %constant_dynamic-update-slice_fusion.refs_9_), channel_id=1, source_target_pairs={{0,2},{2,0},{1,3},{3,1},{4,6},{6,4},{5,7},{7,5},{8,10},{10,8},{9,1... | collective-permute-start | bytes 196616 | tf_op jit(solution)/shard_map/ppermute | solution.py:48
  57.8 2.3 %collective-permute-start.15 = (f32[128,128]{1,0:T(8,128)S(1)}, f32[128,128]{1,0:T(8,128)S(1)}, u32[]{:S(2)}, u32[]{:S(2)}) collective-permute-start(f32[128,128]{1,0:T(8,128)S(1)} %constant_dynamic-update-slice_fusion.refs_9_), channel_id=1, source_target_pairs={{0,1},{1,0},{2,3},{3,2},{4,5},{5,4},{6,7},{7,6},{8,9},{9,8},{10,11... | collective-permute-start | bytes 196616 | tf_op jit(solution)/shard_map/ppermute | solution.py:48
  60.1 1.3 %collective-permute-start.17 = (f32[128,128]{1,0:T(8,128)S(1)}, f32[128,128]{1,0:T(8,128)S(1)}, u32[]{:S(2)}, u32[]{:S(2)}) collective-permute-start(f32[128,128]{1,0:T(8,128)S(1)} %collective-permute-done.16.refs_11_), channel_id=1, source_target_pairs={{0,1},{1,0},{2,3},{3,2},{4,5},{5,4},{6,7},{7,6},{8,9},{9,8},{10,11... | collective-permute-start | bytes 196616 | tf_op jit(solution)/shard_map/ppermute | solution.py:48
  67.2 6.4 %collective-permute-start.20 = (f32[32,128]{1,0:T(8,128)S(1)}, f32[32,128]{1,0:T(8,128)S(1)}, u32[]{:S(2)}, u32[]{:S(2)}) collective-permute-start(f32[32,128]{1,0:T(8,128)S(1)} %get-tuple-element.51), channel_id=1, source_target_pairs={{0,12},{4,8},{8,4},{12,0},{1,13},{5,9},{9,5},{13,1},{2,14},{6,10},... | collective-permute-start | bytes 49160 | tf_op jit(solution)/shard_map/ppermute | solution.py:48
  68.9 4.7 %collective-permute-start.19 = (f32[32,128]{1,0:T(8,128)S(1)}, f32[32,128]{1,0:T(8,128)S(1)}, u32[]{:S(2)}, u32[]{:S(2)}) collective-permute-start(f32[32,128]{1,0:T(8,128)S(1)} %get-tuple-element.51), channel_id=1, source_target_pairs={{0,8},{4,12},{8,0},{12,4},{1,9},{5,13},{9,1},{13,5},{2,10},{6,14},... | collective-permute-start | bytes 49160 | tf_op jit(solution)/shard_map/ppermute | solution.py:48
  69.2 4.2 %collective-permute-start.18 = (f32[32,128]{1,0:T(8,128)S(1)}, f32[32,128]{1,0:T(8,128)S(1)}, u32[]{:S(2)}, u32[]{:S(2)}) collective-permute-start(f32[32,128]{1,0:T(8,128)S(1)} %get-tuple-element.51), channel_id=1, source_target_pairs={{0,4},{4,0},{8,12},{12,8},{1,5},{5,1},{9,13},{13,9},{2,6},{6,2},{1... | collective-permute-start | bytes 49160 | tf_op jit(solution)/shard_map/ppermute | solution.py:48
  73.6 4.6 %collective-permute-start.22 = (f32[128,128]{1,0:T(8,128)S(1)}, f32[128,128]{1,0:T(8,128)S(1)}, u32[]{:S(2)}, u32[]{:S(2)}) collective-permute-start(f32[128,128]{1,0:T(8,128)S(1)} %constant_dynamic-update-slice_fusion.4.refs_9_), channel_id=1, source_target_pairs={{0,2},{2,0},{1,3},{3,1},{4,6},{6,4},{5,7},{7,5},{8,10},{10,8},{9,1... | collective-permute-start | bytes 196616 | tf_op jit(solution)/shard_map/ppermute | solution.py:48
  76.0 2.3 %collective-permute-start.21 = (f32[128,128]{1,0:T(8,128)S(1)}, f32[128,128]{1,0:T(8,128)S(1)}, u32[]{:S(2)}, u32[]{:S(2)}) collective-permute-start(f32[128,128]{1,0:T(8,128)S(1)} %constant_dynamic-update-slice_fusion.4.refs_9_), channel_id=1, source_target_pairs={{0,1},{1,0},{2,3},{3,2},{4,5},{5,4},{6,7},{7,6},{8,9},{9,8},{10,11... | collective-permute-start | bytes 196616 | tf_op jit(solution)/shard_map/ppermute | solution.py:48
  78.2 1.3 %collective-permute-start.23 = (f32[128,128]{1,0:T(8,128)S(1)}, f32[128,128]{1,0:T(8,128)S(1)}, u32[]{:S(2)}, u32[]{:S(2)}) collective-permute-start(f32[128,128]{1,0:T(8,128)S(1)} %collective-permute-done.22.refs_11_), channel_id=1, source_target_pairs={{0,1},{1,0},{2,3},{3,2},{4,5},{5,4},{6,7},{7,6},{8,9},{9,8},{10,11... | collective-permute-start | bytes 196616 | tf_op jit(solution)/shard_map/ppermute | solution.py:48
  85.4 7.0 %collective-permute-start.26 = (f32[8,128]{1,0:T(8,128)S(1)}, f32[8,128]{1,0:T(8,128)S(1)}, u32[]{:S(2)}, u32[]{:S(2)}) collective-permute-start(f32[8,128]{1,0:T(8,128)S(1)} %get-tuple-element.57), channel_id=1, source_target_pairs={{0,12},{4,8},{8,4},{12,0},{1,13},{5,9},{9,5},{13,1},{2,14},{6,10},... | collective-permute-start | bytes 12296 | tf_op jit(solution)/shard_map/ppermute | solution.py:48
  87.7 4.7 %collective-permute-start.25 = (f32[8,128]{1,0:T(8,128)S(1)}, f32[8,128]{1,0:T(8,128)S(1)}, u32[]{:S(2)}, u32[]{:S(2)}) collective-permute-start(f32[8,128]{1,0:T(8,128)S(1)} %get-tuple-element.57), channel_id=1, source_target_pairs={{0,8},{4,12},{8,0},{12,4},{1,9},{5,13},{9,1},{13,5},{2,10},{6,14},... | collective-permute-start | bytes 12296 | tf_op jit(solution)/shard_map/ppermute | solution.py:48
  88.8 3.6 %collective-permute-start.24 = (f32[8,128]{1,0:T(8,128)S(1)}, f32[8,128]{1,0:T(8,128)S(1)}, u32[]{:S(2)}, u32[]{:S(2)}) collective-permute-start(f32[8,128]{1,0:T(8,128)S(1)} %get-tuple-element.57), channel_id=1, source_target_pairs={{0,4},{4,0},{8,12},{12,8},{1,5},{5,1},{9,13},{13,9},{2,6},{6,2},{1... | collective-permute-start | bytes 12296 | tf_op jit(solution)/shard_map/ppermute | solution.py:48
  92.4 4.0 %collective-permute-start.28 = (f32[64,128]{1,0:T(8,128)S(1)}, f32[64,128]{1,0:T(8,128)S(1)}, u32[]{:S(2)}, u32[]{:S(2)}) collective-permute-start(f32[64,128]{1,0:T(8,128)S(1)} %constant_dynamic-update-slice_fusion.8.refs_4_), channel_id=1, source_target_pairs={{0,2},{2,0},{1,3},{3,1},{4,6},{6,4},{5,7},{7,5},{8,10},{10,8},{9,1... | collective-permute-start | bytes 98312 | tf_op jit(solution)/shard_map/ppermute | solution.py:48
  94.2 2.1 %collective-permute-start.27 = (f32[64,128]{1,0:T(8,128)S(1)}, f32[64,128]{1,0:T(8,128)S(1)}, u32[]{:S(2)}, u32[]{:S(2)}) collective-permute-start(f32[64,128]{1,0:T(8,128)S(1)} %constant_dynamic-update-slice_fusion.8.refs_4_), channel_id=1, source_target_pairs={{0,1},{1,0},{2,3},{3,2},{4,5},{5,4},{6,7},{7,6},{8,9},{9,8},{10,11... | collective-permute-start | bytes 98312 | tf_op jit(solution)/shard_map/ppermute | solution.py:48
  96.4 1.2 %collective-permute-start.29 = (f32[64,128]{1,0:T(8,128)S(1)}, f32[64,128]{1,0:T(8,128)S(1)}, u32[]{:S(2)}, u32[]{:S(2)}) collective-permute-start(f32[64,128]{1,0:T(8,128)S(1)} %collective-permute-done.28.refs_6_), channel_id=1, source_target_pairs={{0,1},{1,0},{2,3},{3,2},{4,5},{5,4},{6,7},{7,6},{8,9},{9,8},{10,11... | collective-permute-start | bytes 98312 | tf_op jit(solution)/shard_map/ppermute | solution.py:48

commit v5 on v4

--- a/solution.py
+++ b/solution.py
@@ -250,7 +250,15 @@
     return rhs_ref[pl.ds(pl.multiple_of(j * DEPTH, DEPTH), DEPTH), :]
 
 
-def generate(sz, list_ref, count, lhs_ref, rhs_ref, tile_refs, squares):
+def clear_if_extra(sz, count, accs):
+    @pl.when(count > sz.kept * ARRAYS)
+    def clear():
+        for ref in accs:
+            ref[...] = jnp.zeros_like(ref)
+
+
+def generate(sz, list_ref, count, lhs_ref, rhs_ref, tile_refs, squares, vec_ref, acc, acc_ones):
+    clear_if_extra(sz, count, (acc, acc_ones))
     top = jnp.maximum(lax.div(count + (UNROLL - 1), UNROLL) - 1, 0)
 
     def squared(g, u):
@@ -262,41 +270,54 @@
 
     for u in range(0, UNROLL, 2):
         squares[u // 2 * BS : (u // 2 + 1) * BS, :] = squared(0, u)
+    zero = jnp.zeros((8, BS), F32)
+    carry = (jnp.int32(-1), (zero,) * (BS // 8), (zero,) * (BS // 8))
     for at, tile_ref in enumerate(tile_refs):
 
-        def group(g, unused, at=at, tile_ref=tile_ref):
+        def group(g, carry, at=at, tile_ref=tile_ref):
+            before, totals, ones = carry
+            totals, ones = list(totals), list(ones)
             for u in range(0, UNROLL, 2):
                 following = squared(g + 1, u)
+                i, j = entry_of(list_ref, g * UNROLL + u)
+                unused, twin = entry_of(list_ref, g * UNROLL + u + 1)
+                keep = jnp.where(i == before, 1.0, 0.0)
+                before = i
                 start = pl.multiple_of((g * UNROLL + u - at * sz.kept) * BS, BS)
-                for r in range(0, BS, 8):
+                base = pl.multiple_of(i * BS, BS)
+                row = jnp.broadcast_to(vector_row(vec_ref, j), (8, BS))
+                twin_row = jnp.broadcast_to(vector_row(vec_ref, twin), (8, BS))
+                for k in range(BS // 8):
+                    r = 8 * k
                     here = slice(u // 2 * BS + r, u // 2 * BS + r + 8)
-                    tile_ref[pl.ds(start + r, 8), :] = taper_of(squares[here, :BS])
-                    tile_ref[pl.ds(start + BS + r, 8), :] = taper_of(squares[here, BS:])
+                    tile = taper_of(squares[here, :BS])
+                    twin_tile = taper_of(squares[here, BS:])
+                    tile_ref[pl.ds(start + r, 8), :] = tile
+                    tile_ref[pl.ds(start + BS + r, 8), :] = twin_tile
                     squares[here, :] = following[r : r + 8, :]
-            return unused
-
-        lax.fori_loop(*kept_groups(sz, count, at), group, 0)
-
-
-def sweep(sz, list_ref, count, tile_refs, vec_ref, acc, acc_ones=None):
-    accs = [acc] if acc_ones is None else [acc, acc_ones]
-
-    @pl.when(count > sz.kept * len(tile_refs))
-    def some_targets_are_extra():
-        for ref in accs:
-            ref[...] = jnp.zeros_like(ref)
-
+                    totals[k] = totals[k] * keep + (tile * row + twin_tile * twin_row)
+                    ones[k] = ones[k] * keep + (tile + twin_tile)
+                    acc[pl.ds(base + r, 8), :] = totals[k]
+                    acc_ones[pl.ds(base + r, 8), :] = ones[k]
+            return before, tuple(totals), tuple(ones)
+
+        carry = lax.fori_loop(*kept_groups(sz, count, at), group, carry)
+
+
+def sweep(sz, list_ref, count, tile_refs, vec_ref, acc):
+    clear_if_extra(sz, count, (acc,))
     zero = jnp.zeros((8, BS), F32)
-    carry = (jnp.int32(-1),) + ((zero,) * (BS // 8),) * len(accs)
+    carry = (jnp.int32(-1), (zero,) * (BS // 8))
     for at, tile_ref in enumerate(tile_refs):
 
         def group(g, carry, at=at, tile_ref=tile_ref):
-            before, *totals = carry
-            totals = [list(total) for total in totals]
+            before, totals = carry
+            totals = list(totals)
             for u in range(0, UNROLL, 2):
                 i, j = entry_of(list_ref, g * UNROLL + u)
                 unused, twin = entry_of(list_ref, g * UNROLL + u + 1)
                 keep = jnp.where(i == before, 1.0, 0.0)
+                before = i
                 start = pl.multiple_of((g * UNROLL + u - at * sz.kept) * BS, BS)
                 base = pl.multiple_of(i * BS, BS)
                 row = jnp.broadcast_to(vector_row(vec_ref, j), (8, BS))
@@ -304,11 +325,9 @@
                 for k in range(BS // 8):
                     tile = tile_ref[pl.ds(start + 8 * k, 8), :]
                     twin_tile = tile_ref[pl.ds(start + BS + 8 * k, 8), :]
-                    for ref, total, term in zip(accs, totals, (tile * row + twin_tile * twin_row, tile + twin_tile)):
-                        total[k] = total[k] * keep + term
-                        ref[pl.ds(base + 8 * k, 8), :] = total[k]
-                before = i
-            return (before, *(tuple(total) for total in totals))
+                    totals[k] = totals[k] * keep + (tile * row + twin_tile * twin_row)
+                    acc[pl.ds(base + 8 * k, 8), :] = totals[k]
+            return before, tuple(totals)
 
         carry = lax.fori_loop(*kept_groups(sz, count, at), group, carry)
 
@@ -377,9 +396,8 @@
     far = lax.broadcasted_iota(jnp.int32, (DEPTH, BS), 0) == 3
     rhs_ref[sz.blocks * DEPTH :, :] = jnp.where(far, 1e6, 0.0).astype(BF16)
     count = count_ref[0]
-    generate(sz, list_ref, count, lhs_ref, rhs_ref, tile_refs, squares)
     fetch_obs.wait()
-    sweep(sz, list_ref, count, tile_refs, obs_ref, acc, acc_ones)
+    generate(sz, list_ref, count, lhs_ref, rhs_ref, tile_refs, squares, obs_ref, acc, acc_ones)
     extras(
         sz,
         list_ref,

time: 99.6 us -> 96.9 us (0.973); the launches traced: 98.3 us -> 97.1 us
  starting transfers between devices: 32.8 us -> 27.6 us
  waiting for transfers between devices: 24 us -> 27.1 us
    ppermute x30, starting transfers between devices: 32.8 us -> 27.6 us  [swap(): lax.ppermute(x, axis, [(i, i ^ code) for i in range(lax.axis_size(axis))])]
    ppermute x30, waiting for transfers between devices: 24 us -> 27.1 us  [swap(): lax.ppermute(x, axis, [(i, i ^ code) for i in range(lax.axis_size(axis))])]
  transfers between devices with their start and end apart: 30 -> 30, of which waited for: 17 -> 15; matrix products, arithmetic and copies ran while one was open for 2% -> 2% of each run, Pallas kernels for 3% -> 3%
where the time goes in v5:
time: 96.9 us; the launch traced here: 97.1 us
  Pallas kernels  38.5 us (40%)
  starting transfers between devices  27.6 us (28%)
  waiting for transfers between devices  27.1 us (28%)
  other arithmetic  1.48 us (2%)
  between operations  1.45 us (1%)
  local copies, waits for them, and re-layouts  1.01 us (1%)
    pallas_call x6, Pallas kernels, call(): pl.pallas_call(kernel, in_specs=in_specs, out_shape=shapes, out_specs=out...  38.5 us
    ppermute x30, starting transfers between devices, swap(): lax.ppermute(x, axis, [(i, i ^ code) for i in range(lax.axis_size(axis))])  27.6 us
    ppermute x30, waiting for transfers between devices, swap(): lax.ppermute(x, axis, [(i, i ^ code) for i in range(lax.axis_size(axis))])  27.1 us
  transfers between devices with their start and end apart: 30, of which 15 were waited for; matrix products, arithmetic and copies ran while one was open for 2% of the time, Pallas kernels for 3%

profile of v5, /device:TPU:0, one launch (start us, length us, event | category | flops | bytes accessed | tf_op | source)
XLA Modules:
  0.0 97.1 jit_solution(16123072145535215668)
XLA Ops:
  1.3 0.7 broadcast_select_fusion
  2.0 5.0 %collective-permute-start.2 = (s32[4,128]{1,0:T(4,128)S(1)}, s32[4,128]{1,0:T(4,128)S(1)}, u32[]{:S(2)}, u32[]{:S(2)}) collective-permute-start(s32[4,128]{1,0:T(4,128)S(1)} %reshape.28), channel_id=1, source_target_pairs={{0,12},{4,8},{8,4},{12,0},{1,13},{5,9},{9,5},{13,1},{2,14},{6,10},... | collective-permute-start | bytes 6152 | tf_op jit(solution)/shard_map/ppermute | solution.py:48
  7.0 0.6 collective-permute-start
  7.7 1.0 copy.9
  8.6 0.8 fusion
  9.4 3.8 %collective-permute-start.8 = (f32[256,128]{1,0:T(8,128)S(1)}, f32[256,128]{1,0:T(8,128)S(1)}, u32[]{:S(2)}, u32[]{:S(2)}) collective-permute-start(f32[256,128]{1,0:T(8,128)S(1)} %bitcast.22), channel_id=1, source_target_pairs={{0,12},{4,8},{8,4},{12,0},{1,13},{5,9},{9,5},{13,1},{2,14},{6,10},... | collective-permute-start | bytes 393224 | tf_op jit(solution)/shard_map/ppermute | solution.py:48
  13.2 0.0 collective-permute-start.7
  13.2 0.0 collective-permute-done.2
  13.2 0.6 collective-permute-start.6
  13.9 0.0 collective-permute-done.1
  13.9 0.0 collective-permute-done
  13.9 1.7 %collective-permute-start.4 = (s32[16,128]{1,0:T(8,128)S(1)}, s32[16,128]{1,0:T(8,128)S(1)}, u32[]{:S(2)}, u32[]{:S(2)}) collective-permute-start(s32[16,128]{1,0:T(8,128)S(1)} %pad_add_fusion.refs_0_), channel_id=1, source_target_pairs={{0,2},{2,0},{1,3},{3,1},{4,6},{6,4},{5,7},{7,5},{8,10},{10,8},{9,1... | collective-permute-start | bytes 24584 | tf_op jit(solution)/shard_map/ppermute | solution.py:48
  15.6 2.0 %collective-permute-done.4.refs_2_ = s32[16,128]{1,0:T(8,128)S(1)} collective-permute-done((s32[16,128]{1,0:T(8,128)S(1)}, s32[16,128]{1,0:T(8,128)S(1)}, u32[]{:S(2)}, u32[]{:S(2)}) %collective-permute-start.4) | collective-permute-done | bytes 8224 | tf_op jit(solution)/shard_map/ppermute | solution.py:48
  17.6 0.4 shard_map.69.refs_2_
  18.0 0.8 collective-permute-done.5.refs_3_
  18.8 2.8 %shard_map.68 = (s32[24,128]{1,0:T(8,128)S(1)}, s32[1]{0:T(128)}) custom-call(s32[16,128]{1,0:T(8,128)S(1)} %pad_add_fusion.refs_0_, s32[16,128]{1,0:T(8,128)S(1)} %collective-permute-done.3.refs_1_, s32[16,128]{1,0:T(8,128)S(1)} %collective-permute-done.4.refs_2_, s32[16,128]{1,0:T(8,128)S(1)} %collective-permute-done.5.refs_3_), custom_call_target="tpu_custom_call" | custom-call | flops 10000000 | bytes 1048576 | tf_op jit(solution)/shard_map/pallas_call | solution.py:491
  21.6 1.8 %collective-permute-done.7.refs_8_ = f32[256,128]{1,0:T(8,128)S(1)} collective-permute-done((f32[256,128]{1,0:T(8,128)S(1)}, f32[256,128]{1,0:T(8,128)S(1)}, u32[]{:S(2)}, u32[]{:S(2)}) %collective-permute-start.7) | collective-permute-done | bytes 131104 | tf_op jit(solution)/shard_map/ppermute | solution.py:48
  23.4 0.5 collective-permute-start.10
  23.9 0.0 collective-permute-start.11
  23.9 0.8 collective-permute-done.9.refs_7_
  24.8 0.2 collective-permute-done.10.refs_9_
  25.0 0.3 collective-permute-done.11.refs_11_
  25.3 22.4 %shard_map.70 = (f32[14336,128]{1,0:T(8,128)S(1)}, f32[14336,128]{1,0:T(8,128)S(1)}, f32[14336,128]{1,0:T(8,128)S(1)}, f32[14336,128]{1,0:T(8,128)S(1)}, bf16[24...) custom-call(s32[3072]{0:T(1024)S(1)} %bitcast.16, ...), custom_call_target="tpu_custom_call" | custom-call | flops 100000000 | bytes 1048576 | tf_op jit(solution)/shard_map/pallas_call | solution.py:491
  47.7 0.1 collective-permute-start.14
  47.8 2.6 %collective-permute-start.13 = (f32[32,128]{1,0:T(8,128)S(1)}, f32[32,128]{1,0:T(8,128)S(1)}, u32[]{:S(2)}, u32[]{:S(2)}) collective-permute-start(f32[32,128]{1,0:T(8,128)S(1)} %get-tuple-element.42), channel_id=1, source_target_pairs={{0,8},{4,12},{8,0},{12,4},{1,9},{5,13},{9,1},{13,5},{2,10},{6,14},... | collective-permute-start | bytes 49160 | tf_op jit(solution)/shard_map/ppermute | solution.py:48
  50.4 1.8 %collective-permute-start.12 = (f32[32,128]{1,0:T(8,128)S(1)}, f32[32,128]{1,0:T(8,128)S(1)}, u32[]{:S(2)}, u32[]{:S(2)}) collective-permute-start(f32[32,128]{1,0:T(8,128)S(1)} %get-tuple-element.42), channel_id=1, source_target_pairs={{0,4},{4,0},{8,12},{12,8},{1,5},{5,1},{9,13},{13,9},{2,6},{6,2},{1... | collective-permute-start | bytes 49160 | tf_op jit(solution)/shard_map/ppermute | solution.py:48
  52.1 2.0 %collective-permute-done.12 = f32[32,128]{1,0:T(8,128)S(1)} collective-permute-done((f32[32,128]{1,0:T(8,128)S(1)}, f32[32,128]{1,0:T(8,128)S(1)}, u32[]{:S(2)}, u32[]{:S(2)}) %collective-permute-start.12) | collective-permute-done | bytes 16416 | tf_op jit(solution)/shard_map/ppermute | solution.py:48
  54.1 1.1 %collective-permute-start.16 = (f32[128,128]{1,0:T(8,128)S(1)}, f32[128,128]{1,0:T(8,128)S(1)}, u32[]{:S(2)}, u32[]{:S(2)}) collective-permute-start(f32[128,128]{1,0:T(8,128)S(1)} %constant_dynamic-update-slice_fusion.refs_9_), channel_id=1, source_target_pairs={{0,2},{2,0},{1,3},{3,1},{4,6},{6,4},{5,7},{7,5},{8,10},{10,8},{9,1... | collective-permute-start | bytes 196616 | tf_op jit(solution)/shard_map/ppermute | solution.py:48
  55.2 3.2 %collective-permute-done.16.refs_11_ = f32[128,128]{1,0:T(8,128)S(1)} collective-permute-done((f32[128,128]{1,0:T(8,128)S(1)}, f32[128,128]{1,0:T(8,128)S(1)}, u32[]{:S(2)}, u32[]{:S(2)}) %collective-permute-start.16) | collective-permute-done | bytes 65568 | tf_op jit(solution)/shard_map/ppermute | solution.py:48
  58.5 1.2 %collective-permute-done.17.refs_12_ = f32[128,128]{1,0:T(8,128)S(1)} collective-permute-done((f32[128,128]{1,0:T(8,128)S(1)}, f32[128,128]{1,0:T(8,128)S(1)}, u32[]{:S(2)}, u32[]{:S(2)}) %collective-permute-start.17) | collective-permute-done | bytes 65568 | tf_op jit(solution)/shard_map/ppermute | solution.py:48
  59.7 6.1 %shard_map.71 = (f32[32,128]{1,0:T(8,128)S(1)}, f32[8,128]{1,0:T(8,128)S(1)}, f32[128,128]{1,0:T(8,128)S(1)}, f32[512,128]{1,0:T(8,128)S(1)}, f32[512,128]{1,0:T(8,128)S(1)}) custom-call(s32[3072]{0:T(1024)S(1)} %bitcast.17, s32[1]{0:T(128)} %get-tuple-element.33.refs_1_, bf16[4224,128]{1,0:T(8,128)(2,1)S(1)} %shard_map.69.refs_2_, ...), custom_call_target="tpu_custom_call" | custom-call | flops 100000000 | bytes 1048576 | tf_op jit(solution)/shard_map/pallas_call | solution.py:491
  65.8 1.7 %collective-permute-start.20 = (f32[32,128]{1,0:T(8,128)S(1)}, f32[32,128]{1,0:T(8,128)S(1)}, u32[]{:S(2)}, u32[]{:S(2)}) collective-permute-start(f32[32,128]{1,0:T(8,128)S(1)} %get-tuple-element.51), channel_id=1, source_target_pairs={{0,12},{4,8},{8,4},{12,0},{1,13},{5,9},{9,5},{13,1},{2,14},{6,10},... | collective-permute-start | bytes 49160 | tf_op jit(solution)/shard_map/ppermute | solution.py:48
  67.5 1.9 %collective-permute-start.19 = (f32[32,128]{1,0:T(8,128)S(1)}, f32[32,128]{1,0:T(8,128)S(1)}, u32[]{:S(2)}, u32[]{:S(2)}) collective-permute-start(f32[32,128]{1,0:T(8,128)S(1)} %get-tuple-element.51), channel_id=1, source_target_pairs={{0,8},{4,12},{8,0},{12,4},{1,9},{5,13},{9,1},{13,5},{2,10},{6,14},... | collective-permute-start | bytes 49160 | tf_op jit(solution)/shard_map/ppermute | solution.py:48
  69.4 0.9 collective-permute-start.18
  70.3 2.8 %collective-permute-done.18 = f32[32,128]{1,0:T(8,128)S(1)} collective-permute-done((f32[32,128]{1,0:T(8,128)S(1)}, f32[32,128]{1,0:T(8,128)S(1)}, u32[]{:S(2)}, u32[]{:S(2)}) %collective-permute-start.18) | collective-permute-done | bytes 16416 | tf_op jit(solution)/shard_map/ppermute | solution.py:48
  73.2 0.1 collective-permute-start.22
  73.2 0.1 collective-permute-start.21
  73.3 4.2 %collective-permute-done.22.refs_11_ = f32[128,128]{1,0:T(8,128)S(1)} collective-permute-done((f32[128,128]{1,0:T(8,128)S(1)}, f32[128,128]{1,0:T(8,128)S(1)}, u32[]{:S(2)}, u32[]{:S(2)}) %collective-permute-start.22) | collective-permute-done | bytes 65568 | tf_op jit(solution)/shard_map/ppermute | solution.py:48
  77.5 1.2 %collective-permute-done.23.refs_12_ = f32[128,128]{1,0:T(8,128)S(1)} collective-permute-done((f32[128,128]{1,0:T(8,128)S(1)}, f32[128,128]{1,0:T(8,128)S(1)}, u32[]{:S(2)}, u32[]{:S(2)}) %collective-permute-start.23) | collective-permute-done | bytes 65568 | tf_op jit(solution)/shard_map/ppermute | solution.py:48
  78.7 6.2 %shard_map.72 = (f32[32,128]{1,0:T(8,128)S(1)}, f32[8,128]{1,0:T(8,128)S(1)}, f32[128,128]{1,0:T(8,128)S(1)}, f32[128,128]{1,0:T(8,128)S(1)}, f32[128,128]{1,0:T(8,128)S(1)}, /*index=5*/f32[8,128]{1,0:T(8,128)S(1)}) custom-call(s32[3072]{0:T(1024)S(1)} %bitcast.18, s32[1]{0:T(128)} %get-tuple-element.33.refs_1_, bf16[4224,128]{1,0:T(8,128)(2,1)S(1)} %shard_map.69.refs_2_, ...), custom_call_target="tpu_custom_call" | custom-call | flops 100000000 | bytes 1048576 | tf_op jit(solution)/shard_map/pallas_call | solution.py:491
  85.0 0.8 collective-permute-start.26
  85.7 1.9 %collective-permute-start.25 = (f32[8,128]{1,0:T(8,128)S(1)}, f32[8,128]{1,0:T(8,128)S(1)}, u32[]{:S(2)}, u32[]{:S(2)}) collective-permute-start(f32[8,128]{1,0:T(8,128)S(1)} %get-tuple-element.57), channel_id=1, source_target_pairs={{0,8},{4,12},{8,0},{12,4},{1,9},{5,13},{9,1},{13,5},{2,10},{6,14},... | collective-permute-start | bytes 12296 | tf_op jit(solution)/shard_map/ppermute | solution.py:48
  87.6 1.8 %collective-permute-start.24 = (f32[8,128]{1,0:T(8,128)S(1)}, f32[8,128]{1,0:T(8,128)S(1)}, u32[]{:S(2)}, u32[]{:S(2)}) collective-permute-start(f32[8,128]{1,0:T(8,128)S(1)} %get-tuple-element.57), channel_id=1, source_target_pairs={{0,4},{4,0},{8,12},{12,8},{1,5},{5,1},{9,13},{13,9},{2,6},{6,2},{1... | collective-permute-start | bytes 12296 | tf_op jit(solution)/shard_map/ppermute | solution.py:48
  89.4 1.8 %collective-permute-done.24 = f32[8,128]{1,0:T(8,128)S(1)} collective-permute-done((f32[8,128]{1,0:T(8,128)S(1)}, f32[8,128]{1,0:T(8,128)S(1)}, u32[]{:S(2)}, u32[]{:S(2)}) %collective-permute-start.24) | collective-permute-done | bytes 4128 | tf_op jit(solution)/shard_map/ppermute | solution.py:48
  91.3 0.6 collective-permute-start.28
  91.9 3.4 %collective-permute-done.28.refs_6_ = f32[64,128]{1,0:T(8,128)S(1)} collective-permute-done((f32[64,128]{1,0:T(8,128)S(1)}, f32[64,128]{1,0:T(8,128)S(1)}, u32[]{:S(2)}, u32[]{:S(2)}) %collective-permute-start.28) | collective-permute-done | bytes 32800 | tf_op jit(solution)/shard_map/ppermute | solution.py:48
  95.2 1.2 %collective-permute-done.29.refs_7_ = f32[64,128]{1,0:T(8,128)S(1)} collective-permute-done((f32[64,128]{1,0:T(8,128)S(1)}, f32[64,128]{1,0:T(8,128)S(1)}, u32[]{:S(2)}, u32[]{:S(2)}) %collective-permute-start.29) | collective-permute-done | bytes 32800 | tf_op jit(solution)/shard_map/ppermute | solution.py:48
  96.4 0.7 shard_map.73
  (37 shorter events, 0.1 us)
Async XLA Ops:
  2.0 11.3 %collective-permute-start.2 = (s32[4,128]{1,0:T(4,128)S(1)}, s32[4,128]{1,0:T(4,128)S(1)}, u32[]{:S(2)}, u32[]{:S(2)}) collective-permute-start(s32[4,128]{1,0:T(4,128)S(1)} %reshape.28), channel_id=1, source_target_pairs={{0,12},{4,8},{8,4},{12,0},{1,13},{5,9},{9,5},{13,1},{2,14},{6,10},... | collective-permute-start | bytes 6152 | tf_op jit(solution)/shard_map/ppermute | solution.py:48
  7.0 6.8 %collective-permute-start.1 = (s32[4,128]{1,0:T(4,128)S(1)}, s32[4,128]{1,0:T(4,128)S(1)}, u32[]{:S(2)}, u32[]{:S(2)}) collective-permute-start(s32[4,128]{1,0:T(4,128)S(1)} %reshape.28), channel_id=1, source_target_pairs={{0,8},{4,12},{8,0},{12,4},{1,9},{5,13},{9,1},{13,5},{2,10},{6,14},... | collective-permute-start | bytes 6152 | tf_op jit(solution)/shard_map/ppermute | solution.py:48
  7.0 6.8 %collective-permute-start = (s32[4,128]{1,0:T(4,128)S(1)}, s32[4,128]{1,0:T(4,128)S(1)}, u32[]{:S(2)}, u32[]{:S(2)}) collective-permute-start(s32[4,128]{1,0:T(4,128)S(1)} %reshape.28), channel_id=1, source_target_pairs={{0,4},{4,0},{8,12},{12,8},{1,5},{5,1},{9,13},{13,9},{2,6},{6,2},{1... | collective-permute-start | bytes 6152 | tf_op jit(solution)/shard_map/ppermute | solution.py:48
  9.4 12.2 %collective-permute-start.8 = (f32[256,128]{1,0:T(8,128)S(1)}, f32[256,128]{1,0:T(8,128)S(1)}, u32[]{:S(2)}, u32[]{:S(2)}) collective-permute-start(f32[256,128]{1,0:T(8,128)S(1)} %bitcast.22), channel_id=1, source_target_pairs={{0,12},{4,8},{8,4},{12,0},{1,13},{5,9},{9,5},{13,1},{2,14},{6,10},... | collective-permute-start | bytes 393224 | tf_op jit(solution)/shard_map/ppermute | solution.py:48
  13.2 10.2 %collective-permute-start.7 = (f32[256,128]{1,0:T(8,128)S(1)}, f32[256,128]{1,0:T(8,128)S(1)}, u32[]{:S(2)}, u32[]{:S(2)}) collective-permute-start(f32[256,128]{1,0:T(8,128)S(1)} %bitcast.23), channel_id=1, source_target_pairs={{0,8},{4,12},{8,0},{12,4},{1,9},{5,13},{9,1},{13,5},{2,10},{6,14},... | collective-permute-start | bytes 393224 | tf_op jit(solution)/shard_map/ppermute | solution.py:48
  13.2 10.2 %collective-permute-start.6 = (f32[256,128]{1,0:T(8,128)S(1)}, f32[256,128]{1,0:T(8,128)S(1)}, u32[]{:S(2)}, u32[]{:S(2)}) collective-permute-start(f32[256,128]{1,0:T(8,128)S(1)} %bitcast.24), channel_id=1, source_target_pairs={{0,4},{4,0},{8,12},{12,8},{1,5},{5,1},{9,13},{13,9},{2,6},{6,2},{1... | collective-permute-start | bytes 393224 | tf_op jit(solution)/shard_map/ppermute | solution.py:48
  13.9 3.7 %collective-permute-start.4 = (s32[16,128]{1,0:T(8,128)S(1)}, s32[16,128]{1,0:T(8,128)S(1)}, u32[]{:S(2)}, u32[]{:S(2)}) collective-permute-start(s32[16,128]{1,0:T(8,128)S(1)} %pad_add_fusion.refs_0_), channel_id=1, source_target_pairs={{0,2},{2,0},{1,3},{3,1},{4,6},{6,4},{5,7},{7,5},{8,10},{10,8},{9,1... | collective-permute-start | bytes 24584 | tf_op jit(solution)/shard_map/ppermute | solution.py:48
  15.6 2.4 %collective-permute-start.3 = (s32[16,128]{1,0:T(8,128)S(1)}, s32[16,128]{1,0:T(8,128)S(1)}, u32[]{:S(2)}, u32[]{:S(2)}) collective-permute-start(s32[16,128]{1,0:T(8,128)S(1)} %pad_add_fusion.refs_0_), channel_id=1, source_target_pairs={{0,1},{1,0},{2,3},{3,2},{4,5},{5,4},{6,7},{7,6},{8,9},{9,8},{10,11... | collective-permute-start | bytes 24584 | tf_op jit(solution)/shard_map/ppermute | solution.py:48
  17.6 1.2 %collective-permute-start.5 = (s32[16,128]{1,0:T(8,128)S(1)}, s32[16,128]{1,0:T(8,128)S(1)}, u32[]{:S(2)}, u32[]{:S(2)}) collective-permute-start(s32[16,128]{1,0:T(8,128)S(1)} %collective-permute-done.4.refs_2_), channel_id=1, source_target_pairs={{0,1},{1,0},{2,3},{3,2},{4,5},{5,4},{6,7},{7,6},{8,9},{9,8},{10,11... | collective-permute-start | bytes 24584 | tf_op jit(solution)/shard_map/ppermute | solution.py:48
  23.4 1.3 %collective-permute-start.9 = (f32[256,128]{1,0:T(8,128)S(1)}, f32[256,128]{1,0:T(8,128)S(1)}, u32[]{:S(2)}, u32[]{:S(2)}) collective-permute-start(f32[256,128]{1,0:T(8,128)S(1)} %collective-permute-done.6.refs_6_), channel_id=1, source_target_pairs={{0,1},{1,0},{2,3},{3,2},{4,5},{5,4},{6,7},{7,6},{8,9},{9,8},{10,11... | collective-permute-start | bytes 393224 | tf_op jit(solution)/shard_map/ppermute | solution.py:48
  23.4 1.5 %collective-permute-start.10 = (f32[256,128]{1,0:T(8,128)S(1)}, f32[256,128]{1,0:T(8,128)S(1)}, u32[]{:S(2)}, u32[]{:S(2)}) collective-permute-start(f32[256,128]{1,0:T(8,128)S(1)} %collective-permute-done.7.refs_8_), channel_id=1, source_target_pairs={{0,1},{1,0},{2,3},{3,2},{4,5},{5,4},{6,7},{7,6},{8,9},{9,8},{10,11... | collective-permute-start | bytes 393224 | tf_op jit(solution)/shard_map/ppermute | solution.py:48
  23.9 1.3 %collective-permute-start.11 = (f32[256,128]{1,0:T(8,128)S(1)}, f32[256,128]{1,0:T(8,128)S(1)}, u32[]{:S(2)}, u32[]{:S(2)}) collective-permute-start(f32[256,128]{1,0:T(8,128)S(1)} %collective-permute-done.8.refs_10_), channel_id=1, source_target_pairs={{0,1},{1,0},{2,3},{3,2},{4,5},{5,4},{6,7},{7,6},{8,9},{9,8},{10,11... | collective-permute-start | bytes 393224 | tf_op jit(solution)/shard_map/ppermute | solution.py:48
  47.7 6.4 %collective-permute-start.14 = (f32[32,128]{1,0:T(8,128)S(1)}, f32[32,128]{1,0:T(8,128)S(1)}, u32[]{:S(2)}, u32[]{:S(2)}) collective-permute-start(f32[32,128]{1,0:T(8,128)S(1)} %get-tuple-element.42), channel_id=1, source_target_pairs={{0,12},{4,8},{8,4},{12,0},{1,13},{5,9},{9,5},{13,1},{2,14},{6,10},... | collective-permute-start | bytes 49160 | tf_op jit(solution)/shard_map/ppermute | solution.py:48
  47.8 6.3 %collective-permute-start.13 = (f32[32,128]{1,0:T(8,128)S(1)}, f32[32,128]{1,0:T(8,128)S(1)}, u32[]{:S(2)}, u32[]{:S(2)}) collective-permute-start(f32[32,128]{1,0:T(8,128)S(1)} %get-tuple-element.42), channel_id=1, source_target_pairs={{0,8},{4,12},{8,0},{12,4},{1,9},{5,13},{9,1},{13,5},{2,10},{6,14},... | collective-permute-start | bytes 49160 | tf_op jit(solution)/shard_map/ppermute | solution.py:48
  50.4 3.7 %collective-permute-start.12 = (f32[32,128]{1,0:T(8,128)S(1)}, f32[32,128]{1,0:T(8,128)S(1)}, u32[]{:S(2)}, u32[]{:S(2)}) collective-permute-start(f32[32,128]{1,0:T(8,128)S(1)} %get-tuple-element.42), channel_id=1, source_target_pairs={{0,4},{4,0},{8,12},{12,8},{1,5},{5,1},{9,13},{13,9},{2,6},{6,2},{1... | collective-permute-start | bytes 49160 | tf_op jit(solution)/shard_map/ppermute | solution.py:48
  54.1 4.3 %collective-permute-start.16 = (f32[128,128]{1,0:T(8,128)S(1)}, f32[128,128]{1,0:T(8,128)S(1)}, u32[]{:S(2)}, u32[]{:S(2)}) collective-permute-start(f32[128,128]{1,0:T(8,128)S(1)} %constant_dynamic-update-slice_fusion.refs_9_), channel_id=1, source_target_pairs={{0,2},{2,0},{1,3},{3,1},{4,6},{6,4},{5,7},{7,5},{8,10},{10,8},{9,1... | collective-permute-start | bytes 196616 | tf_op jit(solution)/shard_map/ppermute | solution.py:48
  55.2 3.2 %collective-permute-start.15 = (f32[128,128]{1,0:T(8,128)S(1)}, f32[128,128]{1,0:T(8,128)S(1)}, u32[]{:S(2)}, u32[]{:S(2)}) collective-permute-start(f32[128,128]{1,0:T(8,128)S(1)} %constant_dynamic-update-slice_fusion.refs_9_), channel_id=1, source_target_pairs={{0,1},{1,0},{2,3},{3,2},{4,5},{5,4},{6,7},{7,6},{8,9},{9,8},{10,11... | collective-permute-start | bytes 196616 | tf_op jit(solution)/shard_map/ppermute | solution.py:48
  58.5 1.3 %collective-permute-start.17 = (f32[128,128]{1,0:T(8,128)S(1)}, f32[128,128]{1,0:T(8,128)S(1)}, u32[]{:S(2)}, u32[]{:S(2)}) collective-permute-start(f32[128,128]{1,0:T(8,128)S(1)} %collective-permute-done.16.refs_11_), channel_id=1, source_target_pairs={{0,1},{1,0},{2,3},{3,2},{4,5},{5,4},{6,7},{7,6},{8,9},{9,8},{10,11... | collective-permute-start | bytes 196616 | tf_op jit(solution)/shard_map/ppermute | solution.py:48
  65.8 7.3 %collective-permute-start.20 = (f32[32,128]{1,0:T(8,128)S(1)}, f32[32,128]{1,0:T(8,128)S(1)}, u32[]{:S(2)}, u32[]{:S(2)}) collective-permute-start(f32[32,128]{1,0:T(8,128)S(1)} %get-tuple-element.51), channel_id=1, source_target_pairs={{0,12},{4,8},{8,4},{12,0},{1,13},{5,9},{9,5},{13,1},{2,14},{6,10},... | collective-permute-start | bytes 49160 | tf_op jit(solution)/shard_map/ppermute | solution.py:48
  67.5 5.6 %collective-permute-start.19 = (f32[32,128]{1,0:T(8,128)S(1)}, f32[32,128]{1,0:T(8,128)S(1)}, u32[]{:S(2)}, u32[]{:S(2)}) collective-permute-start(f32[32,128]{1,0:T(8,128)S(1)} %get-tuple-element.51), channel_id=1, source_target_pairs={{0,8},{4,12},{8,0},{12,4},{1,9},{5,13},{9,1},{13,5},{2,10},{6,14},... | collective-permute-start | bytes 49160 | tf_op jit(solution)/shard_map/ppermute | solution.py:48
  69.4 3.7 %collective-permute-start.18 = (f32[32,128]{1,0:T(8,128)S(1)}, f32[32,128]{1,0:T(8,128)S(1)}, u32[]{:S(2)}, u32[]{:S(2)}) collective-permute-start(f32[32,128]{1,0:T(8,128)S(1)} %get-tuple-element.51), channel_id=1, source_target_pairs={{0,4},{4,0},{8,12},{12,8},{1,5},{5,1},{9,13},{13,9},{2,6},{6,2},{1... | collective-permute-start | bytes 49160 | tf_op jit(solution)/shard_map/ppermute | solution.py:48
  73.2 4.3 %collective-permute-start.22 = (f32[128,128]{1,0:T(8,128)S(1)}, f32[128,128]{1,0:T(8,128)S(1)}, u32[]{:S(2)}, u32[]{:S(2)}) collective-permute-start(f32[128,128]{1,0:T(8,128)S(1)} %constant_dynamic-update-slice_fusion.4.refs_9_), channel_id=1, source_target_pairs={{0,2},{2,0},{1,3},{3,1},{4,6},{6,4},{5,7},{7,5},{8,10},{10,8},{9,1... | collective-permute-start | bytes 196616 | tf_op jit(solution)/shard_map/ppermute | solution.py:48
  73.2 4.3 %collective-permute-start.21 = (f32[128,128]{1,0:T(8,128)S(1)}, f32[128,128]{1,0:T(8,128)S(1)}, u32[]{:S(2)}, u32[]{:S(2)}) collective-permute-start(f32[128,128]{1,0:T(8,128)S(1)} %constant_dynamic-update-slice_fusion.4.refs_9_), channel_id=1, source_target_pairs={{0,1},{1,0},{2,3},{3,2},{4,5},{5,4},{6,7},{7,6},{8,9},{9,8},{10,11... | collective-permute-start | bytes 196616 | tf_op jit(solution)/shard_map/ppermute | solution.py:48
  77.5 1.3 %collective-permute-start.23 = (f32[128,128]{1,0:T(8,128)S(1)}, f32[128,128]{1,0:T(8,128)S(1)}, u32[]{:S(2)}, u32[]{:S(2)}) collective-permute-start(f32[128,128]{1,0:T(8,128)S(1)} %collective-permute-done.22.refs_11_), channel_id=1, source_target_pairs={{0,1},{1,0},{2,3},{3,2},{4,5},{5,4},{6,7},{7,6},{8,9},{9,8},{10,11... | collective-permute-start | bytes 196616 | tf_op jit(solution)/shard_map/ppermute | solution.py:48
  85.0 6.3 %collective-permute-start.26 = (f32[8,128]{1,0:T(8,128)S(1)}, f32[8,128]{1,0:T(8,128)S(1)}, u32[]{:S(2)}, u32[]{:S(2)}) collective-permute-start(f32[8,128]{1,0:T(8,128)S(1)} %get-tuple-element.57), channel_id=1, source_target_pairs={{0,12},{4,8},{8,4},{12,0},{1,13},{5,9},{9,5},{13,1},{2,14},{6,10},... | collective-permute-start | bytes 12296 | tf_op jit(solution)/shard_map/ppermute | solution.py:48
  85.7 5.5 %collective-permute-start.25 = (f32[8,128]{1,0:T(8,128)S(1)}, f32[8,128]{1,0:T(8,128)S(1)}, u32[]{:S(2)}, u32[]{:S(2)}) collective-permute-start(f32[8,128]{1,0:T(8,128)S(1)} %get-tuple-element.57), channel_id=1, source_target_pairs={{0,8},{4,12},{8,0},{12,4},{1,9},{5,13},{9,1},{13,5},{2,10},{6,14},... | collective-permute-start | bytes 12296 | tf_op jit(solution)/shard_map/ppermute | solution.py:48
  87.6 3.6 %collective-permute-start.24 = (f32[8,128]{1,0:T(8,128)S(1)}, f32[8,128]{1,0:T(8,128)S(1)}, u32[]{:S(2)}, u32[]{:S(2)}) collective-permute-start(f32[8,128]{1,0:T(8,128)S(1)} %get-tuple-element.57), channel_id=1, source_target_pairs={{0,4},{4,0},{8,12},{12,8},{1,5},{5,1},{9,13},{13,9},{2,6},{6,2},{1... | collective-permute-start | bytes 12296 | tf_op jit(solution)/shard_map/ppermute | solution.py:48
  91.3 4.0 %collective-permute-start.28 = (f32[64,128]{1,0:T(8,128)S(1)}, f32[64,128]{1,0:T(8,128)S(1)}, u32[]{:S(2)}, u32[]{:S(2)}) collective-permute-start(f32[64,128]{1,0:T(8,128)S(1)} %constant_dynamic-update-slice_fusion.8.refs_4_), channel_id=1, source_target_pairs={{0,2},{2,0},{1,3},{3,1},{4,6},{6,4},{5,7},{7,5},{8,10},{10,8},{9,1... | collective-permute-start | bytes 98312 | tf_op jit(solution)/shard_map/ppermute | solution.py:48
  91.9 3.4 %collective-permute-start.27 = (f32[64,128]{1,0:T(8,128)S(1)}, f32[64,128]{1,0:T(8,128)S(1)}, u32[]{:S(2)}, u32[]{:S(2)}) collective-permute-start(f32[64,128]{1,0:T(8,128)S(1)} %constant_dynamic-update-slice_fusion.8.refs_4_), channel_id=1, source_target_pairs={{0,1},{1,0},{2,3},{3,2},{4,5},{5,4},{6,7},{7,6},{8,9},{9,8},{10,11... | collective-permute-start | bytes 98312 | tf_op jit(solution)/shard_map/ppermute | solution.py:48
  95.2 1.2 %collective-permute-start.29 = (f32[64,128]{1,0:T(8,128)S(1)}, f32[64,128]{1,0:T(8,128)S(1)}, u32[]{:S(2)}, u32[]{:S(2)}) collective-permute-start(f32[64,128]{1,0:T(8,128)S(1)} %collective-permute-done.28.refs_6_), channel_id=1, source_target_pairs={{0,1},{1,0},{2,3},{3,2},{4,5},{5,4},{6,7},{7,6},{8,9},{9,8},{10,11... | collective-permute-start | bytes 98312 | tf_op jit(solution)/shard_map/ppermute | solution.py:48

commit v6 on v5

--- a/solution.py
+++ b/solution.py
@@ -142,10 +142,10 @@
     def compact(c, unused):
         slot = (sub + c * BS).astype(F32)
         base = (c * BS).astype(F32)
-        first = jnp.sum(jnp.where(ends <= base, 1.0, 0.0)).astype(jnp.int32)
-        last = jnp.sum(jnp.where(starts < base + BS, 1.0, 0.0)).astype(jnp.int32)
-        first = jnp.minimum(lax.shift_right_logical(first, 2), at // 4)
-        last = lax.shift_right_logical(last + 3, 2)
+        bounds = jnp.where(ends <= base, 1.0, 0.0) + jnp.where(starts < base + BS, 1024.0, 0.0)
+        bounds = jnp.sum(bounds).astype(jnp.int32)
+        first = jnp.minimum(lax.shift_right_logical(jnp.bitwise_and(bounds, 1023), 2), at // 4)
+        last = lax.shift_right_logical(lax.shift_right_logical(bounds, 10) + 3, 2)
 
         def lines(g, total):
             for u in range(4):
@@ -347,14 +347,13 @@
 
 
 def finish(sz, acc, out_ref):
-    unit = jnp.ones((8, BS), BF16)
+    unit = jnp.ones((8, 2 * BS), BF16)
     across = (((1,), (1,)), ((), ()))
     for i in range(sz.own):
         whole = acc[i * BS : (i + 1) * BS, :]
         high = whole.astype(BF16)
         low = (whole - high.astype(F32)).astype(BF16)
-        y = lax.dot_general(unit, high, across, preferred_element_type=F32)
-        y = y + lax.dot_general(unit, low, across, preferred_element_type=F32)
+        y = lax.dot_general(unit, jnp.concatenate([high, low], axis=1), across, preferred_element_type=F32)
         out_ref[i : i + 1, :] = y[0:1, :] * sz.scale
 
 

time: 96.9 us -> 96.4 us (level); the launches traced: 97.1 us -> 95 us
  waiting for transfers between devices: 27.1 us -> 23.3 us
  starting transfers between devices: 27.6 us -> 31.3 us
  Pallas kernels: 38.5 us -> 36.4 us
    ppermute x30, waiting for transfers between devices: 27.1 us -> 23.3 us  [swap(): lax.ppermute(x, axis, [(i, i ^ code) for i in range(lax.axis_size(axis))])]
    ppermute x30, starting transfers between devices: 27.6 us -> 31.3 us  [swap(): lax.ppermute(x, axis, [(i, i ^ code) for i in range(lax.axis_size(axis))])]
    pallas_call x6, Pallas kernels: 38.5 us -> 36.4 us  [call(): pl.pallas_call(kernel, in_specs=in_specs, out_shape=shapes, out_specs=out...]
  transfers between devices with their start and end apart: 30 -> 30, of which waited for: 15 -> 16; matrix products, arithmetic and copies ran while one was open for 2% -> 2% of each run, Pallas kernels for 3% -> 3%
where the time goes in v6:
time: 96.4 us; the launch traced here: 95 us
  Pallas kernels  36.4 us (38%)
  starting transfers between devices  31.3 us (32%)
  waiting for transfers between devices  23.3 us (24%)
  other arithmetic  1.48 us (2%)
  between operations  1.41 us (1%)
  local copies, waits for them, and re-layouts  1.01 us (1%)
    pallas_call x6, Pallas kernels, call(): pl.pallas_call(kernel, in_specs=in_specs, out_shape=shapes, out_specs=out...  36.4 us
    ppermute x30, starting transfers between devices, swap(): lax.ppermute(x, axis, [(i, i ^ code) for i in range(lax.axis_size(axis))])  31.3 us
    ppermute x30, waiting for transfers between devices, swap(): lax.ppermute(x, axis, [(i, i ^ code) for i in range(lax.axis_size(axis))])  23.3 us
  transfers between devices with their start and end apart: 30, of which 16 were waited for; matrix products, arithmetic and copies ran while one was open for 2% of the time, Pallas kernels for 3%

profile of v6, /device:TPU:0, one launch (start us, length us, event | category | flops | bytes accessed | tf_op | source)
XLA Modules:
  0.0 95.0 jit_solution(16336492940670742726)
XLA Ops:
  1.3 0.7 broadcast_select_fusion
  2.0 5.0 %collective-permute-start.2 = (s32[4,128]{1,0:T(4,128)S(1)}, s32[4,128]{1,0:T(4,128)S(1)}, u32[]{:S(2)}, u32[]{:S(2)}) collective-permute-start(s32[4,128]{1,0:T(4,128)S(1)} %reshape.28), channel_id=1, source_target_pairs={{0,12},{4,8},{8,4},{12,0},{1,13},{5,9},{9,5},{13,1},{2,14},{6,10},... | collective-permute-start | bytes 6152 | tf_op jit(solution)/shard_map/ppermute | solution.py:48
  7.0 0.6 collective-permute-start
  7.7 1.0 %copy.9 = f32[1,3,128,128]{3,2,1,0:T(8,128)S(1)} copy(f32[1,3,128,128]{3,1,2,0:T(4,128)} %bitcast.19) | data formatting | bytes 393216
  8.6 0.8 fusion
  9.4 3.8 %collective-permute-start.8 = (f32[256,128]{1,0:T(8,128)S(1)}, f32[256,128]{1,0:T(8,128)S(1)}, u32[]{:S(2)}, u32[]{:S(2)}) collective-permute-start(f32[256,128]{1,0:T(8,128)S(1)} %bitcast.22), channel_id=1, source_target_pairs={{0,12},{4,8},{8,4},{12,0},{1,13},{5,9},{9,5},{13,1},{2,14},{6,10},... | collective-permute-start | bytes 393224 | tf_op jit(solution)/shard_map/ppermute | solution.py:48
  13.2 0.0 collective-permute-start.7
  13.2 0.0 collective-permute-done.2
  13.2 0.6 collective-permute-start.6
  13.9 0.0 collective-permute-done.1
  13.9 0.0 collective-permute-done
  13.9 1.7 %collective-permute-start.4 = (s32[16,128]{1,0:T(8,128)S(1)}, s32[16,128]{1,0:T(8,128)S(1)}, u32[]{:S(2)}, u32[]{:S(2)}) collective-permute-start(s32[16,128]{1,0:T(8,128)S(1)} %pad_add_fusion.refs_0_), channel_id=1, source_target_pairs={{0,2},{2,0},{1,3},{3,1},{4,6},{6,4},{5,7},{7,5},{8,10},{10,8},{9,1... | collective-permute-start | bytes 24584 | tf_op jit(solution)/shard_map/ppermute | solution.py:48
  15.6 2.0 %collective-permute-done.4.refs_2_ = s32[16,128]{1,0:T(8,128)S(1)} collective-permute-done((s32[16,128]{1,0:T(8,128)S(1)}, s32[16,128]{1,0:T(8,128)S(1)}, u32[]{:S(2)}, u32[]{:S(2)}) %collective-permute-start.4) | collective-permute-done | bytes 8224 | tf_op jit(solution)/shard_map/ppermute | solution.py:48
  17.6 0.4 shard_map.69.refs_2_
  18.0 0.8 collective-permute-done.5.refs_3_
  18.8 2.8 %shard_map.68 = (s32[24,128]{1,0:T(8,128)S(1)}, s32[1]{0:T(128)}) custom-call(s32[16,128]{1,0:T(8,128)S(1)} %pad_add_fusion.refs_0_, s32[16,128]{1,0:T(8,128)S(1)} %collective-permute-done.3.refs_1_, s32[16,128]{1,0:T(8,128)S(1)} %collective-permute-done.4.refs_2_, s32[16,128]{1,0:T(8,128)S(1)} %collective-permute-done.5.refs_3_), custom_call_target="tpu_custom_call" | custom-call | flops 10000000 | bytes 1048576 | tf_op jit(solution)/shard_map/pallas_call | solution.py:490
  21.6 1.8 %collective-permute-done.7.refs_8_ = f32[256,128]{1,0:T(8,128)S(1)} collective-permute-done((f32[256,128]{1,0:T(8,128)S(1)}, f32[256,128]{1,0:T(8,128)S(1)}, u32[]{:S(2)}, u32[]{:S(2)}) %collective-permute-start.7) | collective-permute-done | bytes 131104 | tf_op jit(solution)/shard_map/ppermute | solution.py:48
  23.4 0.5 collective-permute-start.10
  23.9 0.0 collective-permute-start.11
  23.9 0.8 collective-permute-done.9.refs_7_
  24.8 0.2 collective-permute-done.10.refs_9_
  25.0 0.3 collective-permute-done.11.refs_11_
  25.3 21.4 %shard_map.70 = (f32[14336,128]{1,0:T(8,128)S(1)}, f32[14336,128]{1,0:T(8,128)S(1)}, f32[14336,128]{1,0:T(8,128)S(1)}, f32[14336,128]{1,0:T(8,128)S(1)}, bf16[24...) custom-call(s32[3072]{0:T(1024)S(1)} %bitcast.16, ...), custom_call_target="tpu_custom_call" | custom-call | flops 100000000 | bytes 1048576 | tf_op jit(solution)/shard_map/pallas_call | solution.py:490
  46.7 1.8 %collective-permute-start.14 = (f32[32,128]{1,0:T(8,128)S(1)}, f32[32,128]{1,0:T(8,128)S(1)}, u32[]{:S(2)}, u32[]{:S(2)}) collective-permute-start(f32[32,128]{1,0:T(8,128)S(1)} %get-tuple-element.42), channel_id=1, source_target_pairs={{0,12},{4,8},{8,4},{12,0},{1,13},{5,9},{9,5},{13,1},{2,14},{6,10},... | collective-permute-start | bytes 49160 | tf_op jit(solution)/shard_map/ppermute | solution.py:48
  48.5 0.2 collective-permute-start.13
  48.6 2.5 %collective-permute-start.12 = (f32[32,128]{1,0:T(8,128)S(1)}, f32[32,128]{1,0:T(8,128)S(1)}, u32[]{:S(2)}, u32[]{:S(2)}) collective-permute-start(f32[32,128]{1,0:T(8,128)S(1)} %get-tuple-element.42), channel_id=1, source_target_pairs={{0,4},{4,0},{8,12},{12,8},{1,5},{5,1},{9,13},{13,9},{2,6},{6,2},{1... | collective-permute-start | bytes 49160 | tf_op jit(solution)/shard_map/ppermute | solution.py:48
  51.1 1.7 %collective-permute-done.12 = f32[32,128]{1,0:T(8,128)S(1)} collective-permute-done((f32[32,128]{1,0:T(8,128)S(1)}, f32[32,128]{1,0:T(8,128)S(1)}, u32[]{:S(2)}, u32[]{:S(2)}) %collective-permute-start.12) | collective-permute-done | bytes 16416 | tf_op jit(solution)/shard_map/ppermute | solution.py:48
  52.8 0.3 collective-permute-done.13
  53.1 2.1 %collective-permute-start.16 = (f32[128,128]{1,0:T(8,128)S(1)}, f32[128,128]{1,0:T(8,128)S(1)}, u32[]{:S(2)}, u32[]{:S(2)}) collective-permute-start(f32[128,128]{1,0:T(8,128)S(1)} %constant_dynamic-update-slice_fusion.refs_9_), channel_id=1, source_target_pairs={{0,2},{2,0},{1,3},{3,1},{4,6},{6,4},{5,7},{7,5},{8,10},{10,8},{9,1... | collective-permute-start | bytes 196616 | tf_op jit(solution)/shard_map/ppermute | solution.py:48
  55.3 2.2 %collective-permute-done.16.refs_11_ = f32[128,128]{1,0:T(8,128)S(1)} collective-permute-done((f32[128,128]{1,0:T(8,128)S(1)}, f32[128,128]{1,0:T(8,128)S(1)}, u32[]{:S(2)}, u32[]{:S(2)}) %collective-permute-start.16) | collective-permute-done | bytes 65568 | tf_op jit(solution)/shard_map/ppermute | solution.py:48
  57.5 1.2 %collective-permute-done.17.refs_12_ = f32[128,128]{1,0:T(8,128)S(1)} collective-permute-done((f32[128,128]{1,0:T(8,128)S(1)}, f32[128,128]{1,0:T(8,128)S(1)}, u32[]{:S(2)}, u32[]{:S(2)}) %collective-permute-start.17) | collective-permute-done | bytes 65568 | tf_op jit(solution)/shard_map/ppermute | solution.py:48
  58.8 5.6 %shard_map.71 = (f32[32,128]{1,0:T(8,128)S(1)}, f32[8,128]{1,0:T(8,128)S(1)}, f32[128,128]{1,0:T(8,128)S(1)}, f32[512,128]{1,0:T(8,128)S(1)}, f32[512,128]{1,0:T(8,128)S(1)}) custom-call(s32[3072]{0:T(1024)S(1)} %bitcast.17, s32[1]{0:T(128)} %get-tuple-element.33.refs_1_, bf16[4224,128]{1,0:T(8,128)(2,1)S(1)} %shard_map.69.refs_2_, ...), custom_call_target="tpu_custom_call" | custom-call | flops 100000000 | bytes 1048576 | tf_op jit(solution)/shard_map/pallas_call | solution.py:490
  64.3 2.0 %collective-permute-start.20 = (f32[32,128]{1,0:T(8,128)S(1)}, f32[32,128]{1,0:T(8,128)S(1)}, u32[]{:S(2)}, u32[]{:S(2)}) collective-permute-start(f32[32,128]{1,0:T(8,128)S(1)} %get-tuple-element.51), channel_id=1, source_target_pairs={{0,12},{4,8},{8,4},{12,0},{1,13},{5,9},{9,5},{13,1},{2,14},{6,10},... | collective-permute-start | bytes 49160 | tf_op jit(solution)/shard_map/ppermute | solution.py:48
  66.3 1.4 %collective-permute-start.19 = (f32[32,128]{1,0:T(8,128)S(1)}, f32[32,128]{1,0:T(8,128)S(1)}, u32[]{:S(2)}, u32[]{:S(2)}) collective-permute-start(f32[32,128]{1,0:T(8,128)S(1)} %get-tuple-element.51), channel_id=1, source_target_pairs={{0,8},{4,12},{8,0},{12,4},{1,9},{5,13},{9,1},{13,5},{2,10},{6,14},... | collective-permute-start | bytes 49160 | tf_op jit(solution)/shard_map/ppermute | solution.py:48
  67.7 1.1 %collective-permute-start.18 = (f32[32,128]{1,0:T(8,128)S(1)}, f32[32,128]{1,0:T(8,128)S(1)}, u32[]{:S(2)}, u32[]{:S(2)}) collective-permute-start(f32[32,128]{1,0:T(8,128)S(1)} %get-tuple-element.51), channel_id=1, source_target_pairs={{0,4},{4,0},{8,12},{12,8},{1,5},{5,1},{9,13},{13,9},{2,6},{6,2},{1... | collective-permute-start | bytes 49160 | tf_op jit(solution)/shard_map/ppermute | solution.py:48
  68.8 2.7 %collective-permute-done.18 = f32[32,128]{1,0:T(8,128)S(1)} collective-permute-done((f32[32,128]{1,0:T(8,128)S(1)}, f32[32,128]{1,0:T(8,128)S(1)}, u32[]{:S(2)}, u32[]{:S(2)}) %collective-permute-start.18) | collective-permute-done | bytes 16416 | tf_op jit(solution)/shard_map/ppermute | solution.py:48
  71.5 1.5 %collective-permute-start.22 = (f32[128,128]{1,0:T(8,128)S(1)}, f32[128,128]{1,0:T(8,128)S(1)}, u32[]{:S(2)}, u32[]{:S(2)}) collective-permute-start(f32[128,128]{1,0:T(8,128)S(1)} %constant_dynamic-update-slice_fusion.4.refs_9_), channel_id=1, source_target_pairs={{0,2},{2,0},{1,3},{3,1},{4,6},{6,4},{5,7},{7,5},{8,10},{10,8},{9,1... | collective-permute-start | bytes 196616 | tf_op jit(solution)/shard_map/ppermute | solution.py:48
  73.0 2.8 %collective-permute-done.22.refs_11_ = f32[128,128]{1,0:T(8,128)S(1)} collective-permute-done((f32[128,128]{1,0:T(8,128)S(1)}, f32[128,128]{1,0:T(8,128)S(1)}, u32[]{:S(2)}, u32[]{:S(2)}) %collective-permute-start.22) | collective-permute-done | bytes 65568 | tf_op jit(solution)/shard_map/ppermute | solution.py:48
  75.8 1.2 %collective-permute-done.23.refs_12_ = f32[128,128]{1,0:T(8,128)S(1)} collective-permute-done((f32[128,128]{1,0:T(8,128)S(1)}, f32[128,128]{1,0:T(8,128)S(1)}, u32[]{:S(2)}, u32[]{:S(2)}) %collective-permute-start.23) | collective-permute-done | bytes 65568 | tf_op jit(solution)/shard_map/ppermute | solution.py:48
  77.1 5.7 %shard_map.72 = (f32[32,128]{1,0:T(8,128)S(1)}, f32[8,128]{1,0:T(8,128)S(1)}, f32[128,128]{1,0:T(8,128)S(1)}, f32[128,128]{1,0:T(8,128)S(1)}, f32[128,128]{1,0:T(8,128)S(1)}, /*index=5*/f32[8,128]{1,0:T(8,128)S(1)}) custom-call(s32[3072]{0:T(1024)S(1)} %bitcast.18, s32[1]{0:T(128)} %get-tuple-element.33.refs_1_, bf16[4224,128]{1,0:T(8,128)(2,1)S(1)} %shard_map.69.refs_2_, ...), custom_call_target="tpu_custom_call" | custom-call | flops 100000000 | bytes 1048576 | tf_op jit(solution)/shard_map/pallas_call | solution.py:490
  82.7 1.6 %collective-permute-start.26 = (f32[8,128]{1,0:T(8,128)S(1)}, f32[8,128]{1,0:T(8,128)S(1)}, u32[]{:S(2)}, u32[]{:S(2)}) collective-permute-start(f32[8,128]{1,0:T(8,128)S(1)} %get-tuple-element.57), channel_id=1, source_target_pairs={{0,12},{4,8},{8,4},{12,0},{1,13},{5,9},{9,5},{13,1},{2,14},{6,10},... | collective-permute-start | bytes 12296 | tf_op jit(solution)/shard_map/ppermute | solution.py:48
  84.4 1.1 %collective-permute-start.25 = (f32[8,128]{1,0:T(8,128)S(1)}, f32[8,128]{1,0:T(8,128)S(1)}, u32[]{:S(2)}, u32[]{:S(2)}) collective-permute-start(f32[8,128]{1,0:T(8,128)S(1)} %get-tuple-element.57), channel_id=1, source_target_pairs={{0,8},{4,12},{8,0},{12,4},{1,9},{5,13},{9,1},{13,5},{2,10},{6,14},... | collective-permute-start | bytes 12296 | tf_op jit(solution)/shard_map/ppermute | solution.py:48
  85.5 1.7 %collective-permute-start.24 = (f32[8,128]{1,0:T(8,128)S(1)}, f32[8,128]{1,0:T(8,128)S(1)}, u32[]{:S(2)}, u32[]{:S(2)}) collective-permute-start(f32[8,128]{1,0:T(8,128)S(1)} %get-tuple-element.57), channel_id=1, source_target_pairs={{0,4},{4,0},{8,12},{12,8},{1,5},{5,1},{9,13},{13,9},{2,6},{6,2},{1... | collective-permute-start | bytes 12296 | tf_op jit(solution)/shard_map/ppermute | solution.py:48
  87.2 1.9 %collective-permute-done.24 = f32[8,128]{1,0:T(8,128)S(1)} collective-permute-done((f32[8,128]{1,0:T(8,128)S(1)}, f32[8,128]{1,0:T(8,128)S(1)}, u32[]{:S(2)}, u32[]{:S(2)}) %collective-permute-start.24) | collective-permute-done | bytes 4128 | tf_op jit(solution)/shard_map/ppermute | solution.py:48
  89.1 2.0 %collective-permute-start.28 = (f32[64,128]{1,0:T(8,128)S(1)}, f32[64,128]{1,0:T(8,128)S(1)}, u32[]{:S(2)}, u32[]{:S(2)}) collective-permute-start(f32[64,128]{1,0:T(8,128)S(1)} %constant_dynamic-update-slice_fusion.8.refs_4_), channel_id=1, source_target_pairs={{0,2},{2,0},{1,3},{3,1},{4,6},{6,4},{5,7},{7,5},{8,10},{10,8},{9,1... | collective-permute-start | bytes 98312 | tf_op jit(solution)/shard_map/ppermute | solution.py:48
  91.1 2.0 %collective-permute-done.28.refs_6_ = f32[64,128]{1,0:T(8,128)S(1)} collective-permute-done((f32[64,128]{1,0:T(8,128)S(1)}, f32[64,128]{1,0:T(8,128)S(1)}, u32[]{:S(2)}, u32[]{:S(2)}) %collective-permute-start.28) | collective-permute-done | bytes 32800 | tf_op jit(solution)/shard_map/ppermute | solution.py:48
  93.1 1.2 %collective-permute-done.29.refs_7_ = f32[64,128]{1,0:T(8,128)S(1)} collective-permute-done((f32[64,128]{1,0:T(8,128)S(1)}, f32[64,128]{1,0:T(8,128)S(1)}, u32[]{:S(2)}, u32[]{:S(2)}) %collective-permute-start.29) | collective-permute-done | bytes 32800 | tf_op jit(solution)/shard_map/ppermute | solution.py:48
  94.3 0.7 shard_map.73
  (37 shorter events, 0.1 us)
Async XLA Ops:
  2.0 11.3 %collective-permute-start.2 = (s32[4,128]{1,0:T(4,128)S(1)}, s32[4,128]{1,0:T(4,128)S(1)}, u32[]{:S(2)}, u32[]{:S(2)}) collective-permute-start(s32[4,128]{1,0:T(4,128)S(1)} %reshape.28), channel_id=1, source_target_pairs={{0,12},{4,8},{8,4},{12,0},{1,13},{5,9},{9,5},{13,1},{2,14},{6,10},... | collective-permute-start | bytes 6152 | tf_op jit(solution)/shard_map/ppermute | solution.py:48
  7.0 6.8 %collective-permute-start.1 = (s32[4,128]{1,0:T(4,128)S(1)}, s32[4,128]{1,0:T(4,128)S(1)}, u32[]{:S(2)}, u32[]{:S(2)}) collective-permute-start(s32[4,128]{1,0:T(4,128)S(1)} %reshape.28), channel_id=1, source_target_pairs={{0,8},{4,12},{8,0},{12,4},{1,9},{5,13},{9,1},{13,5},{2,10},{6,14},... | collective-permute-start | bytes 6152 | tf_op jit(solution)/shard_map/ppermute | solution.py:48
  7.0 6.8 %collective-permute-start = (s32[4,128]{1,0:T(4,128)S(1)}, s32[4,128]{1,0:T(4,128)S(1)}, u32[]{:S(2)}, u32[]{:S(2)}) collective-permute-start(s32[4,128]{1,0:T(4,128)S(1)} %reshape.28), channel_id=1, source_target_pairs={{0,4},{4,0},{8,12},{12,8},{1,5},{5,1},{9,13},{13,9},{2,6},{6,2},{1... | collective-permute-start | bytes 6152 | tf_op jit(solution)/shard_map/ppermute | solution.py:48
  9.4 12.2 %collective-permute-start.8 = (f32[256,128]{1,0:T(8,128)S(1)}, f32[256,128]{1,0:T(8,128)S(1)}, u32[]{:S(2)}, u32[]{:S(2)}) collective-permute-start(f32[256,128]{1,0:T(8,128)S(1)} %bitcast.22), channel_id=1, source_target_pairs={{0,12},{4,8},{8,4},{12,0},{1,13},{5,9},{9,5},{13,1},{2,14},{6,10},... | collective-permute-start | bytes 393224 | tf_op jit(solution)/shard_map/ppermute | solution.py:48
  13.2 10.2 %collective-permute-start.7 = (f32[256,128]{1,0:T(8,128)S(1)}, f32[256,128]{1,0:T(8,128)S(1)}, u32[]{:S(2)}, u32[]{:S(2)}) collective-permute-start(f32[256,128]{1,0:T(8,128)S(1)} %bitcast.23), channel_id=1, source_target_pairs={{0,8},{4,12},{8,0},{12,4},{1,9},{5,13},{9,1},{13,5},{2,10},{6,14},... | collective-permute-start | bytes 393224 | tf_op jit(solution)/shard_map/ppermute | solution.py:48
  13.2 10.2 %collective-permute-start.6 = (f32[256,128]{1,0:T(8,128)S(1)}, f32[256,128]{1,0:T(8,128)S(1)}, u32[]{:S(2)}, u32[]{:S(2)}) collective-permute-start(f32[256,128]{1,0:T(8,128)S(1)} %bitcast.24), channel_id=1, source_target_pairs={{0,4},{4,0},{8,12},{12,8},{1,5},{5,1},{9,13},{13,9},{2,6},{6,2},{1... | collective-permute-start | bytes 393224 | tf_op jit(solution)/shard_map/ppermute | solution.py:48
  13.9 3.7 %collective-permute-start.4 = (s32[16,128]{1,0:T(8,128)S(1)}, s32[16,128]{1,0:T(8,128)S(1)}, u32[]{:S(2)}, u32[]{:S(2)}) collective-permute-start(s32[16,128]{1,0:T(8,128)S(1)} %pad_add_fusion.refs_0_), channel_id=1, source_target_pairs={{0,2},{2,0},{1,3},{3,1},{4,6},{6,4},{5,7},{7,5},{8,10},{10,8},{9,1... | collective-permute-start | bytes 24584 | tf_op jit(solution)/shard_map/ppermute | solution.py:48
  15.6 2.4 %collective-permute-start.3 = (s32[16,128]{1,0:T(8,128)S(1)}, s32[16,128]{1,0:T(8,128)S(1)}, u32[]{:S(2)}, u32[]{:S(2)}) collective-permute-start(s32[16,128]{1,0:T(8,128)S(1)} %pad_add_fusion.refs_0_), channel_id=1, source_target_pairs={{0,1},{1,0},{2,3},{3,2},{4,5},{5,4},{6,7},{7,6},{8,9},{9,8},{10,11... | collective-permute-start | bytes 24584 | tf_op jit(solution)/shard_map/ppermute | solution.py:48
  17.6 1.2 %collective-permute-start.5 = (s32[16,128]{1,0:T(8,128)S(1)}, s32[16,128]{1,0:T(8,128)S(1)}, u32[]{:S(2)}, u32[]{:S(2)}) collective-permute-start(s32[16,128]{1,0:T(8,128)S(1)} %collective-permute-done.4.refs_2_), channel_id=1, source_target_pairs={{0,1},{1,0},{2,3},{3,2},{4,5},{5,4},{6,7},{7,6},{8,9},{9,8},{10,11... | collective-permute-start | bytes 24584 | tf_op jit(solution)/shard_map/ppermute | solution.py:48
  23.4 1.3 %collective-permute-start.9 = (f32[256,128]{1,0:T(8,128)S(1)}, f32[256,128]{1,0:T(8,128)S(1)}, u32[]{:S(2)}, u32[]{:S(2)}) collective-permute-start(f32[256,128]{1,0:T(8,128)S(1)} %collective-permute-done.6.refs_6_), channel_id=1, source_target_pairs={{0,1},{1,0},{2,3},{3,2},{4,5},{5,4},{6,7},{7,6},{8,9},{9,8},{10,11... | collective-permute-start | bytes 393224 | tf_op jit(solution)/shard_map/ppermute | solution.py:48
  23.4 1.5 %collective-permute-start.10 = (f32[256,128]{1,0:T(8,128)S(1)}, f32[256,128]{1,0:T(8,128)S(1)}, u32[]{:S(2)}, u32[]{:S(2)}) collective-permute-start(f32[256,128]{1,0:T(8,128)S(1)} %collective-permute-done.7.refs_8_), channel_id=1, source_target_pairs={{0,1},{1,0},{2,3},{3,2},{4,5},{5,4},{6,7},{7,6},{8,9},{9,8},{10,11... | collective-permute-start | bytes 393224 | tf_op jit(solution)/shard_map/ppermute | solution.py:48
  23.9 1.3 %collective-permute-start.11 = (f32[256,128]{1,0:T(8,128)S(1)}, f32[256,128]{1,0:T(8,128)S(1)}, u32[]{:S(2)}, u32[]{:S(2)}) collective-permute-start(f32[256,128]{1,0:T(8,128)S(1)} %collective-permute-done.8.refs_10_), channel_id=1, source_target_pairs={{0,1},{1,0},{2,3},{3,2},{4,5},{5,4},{6,7},{7,6},{8,9},{9,8},{10,11... | collective-permute-start | bytes 393224 | tf_op jit(solution)/shard_map/ppermute | solution.py:48
  46.7 6.4 %collective-permute-start.14 = (f32[32,128]{1,0:T(8,128)S(1)}, f32[32,128]{1,0:T(8,128)S(1)}, u32[]{:S(2)}, u32[]{:S(2)}) collective-permute-start(f32[32,128]{1,0:T(8,128)S(1)} %get-tuple-element.42), channel_id=1, source_target_pairs={{0,12},{4,8},{8,4},{12,0},{1,13},{5,9},{9,5},{13,1},{2,14},{6,10},... | collective-permute-start | bytes 49160 | tf_op jit(solution)/shard_map/ppermute | solution.py:48
  48.5 4.6 %collective-permute-start.13 = (f32[32,128]{1,0:T(8,128)S(1)}, f32[32,128]{1,0:T(8,128)S(1)}, u32[]{:S(2)}, u32[]{:S(2)}) collective-permute-start(f32[32,128]{1,0:T(8,128)S(1)} %get-tuple-element.42), channel_id=1, source_target_pairs={{0,8},{4,12},{8,0},{12,4},{1,9},{5,13},{9,1},{13,5},{2,10},{6,14},... | collective-permute-start | bytes 49160 | tf_op jit(solution)/shard_map/ppermute | solution.py:48
  48.6 4.2 %collective-permute-start.12 = (f32[32,128]{1,0:T(8,128)S(1)}, f32[32,128]{1,0:T(8,128)S(1)}, u32[]{:S(2)}, u32[]{:S(2)}) collective-permute-start(f32[32,128]{1,0:T(8,128)S(1)} %get-tuple-element.42), channel_id=1, source_target_pairs={{0,4},{4,0},{8,12},{12,8},{1,5},{5,1},{9,13},{13,9},{2,6},{6,2},{1... | collective-permute-start | bytes 49160 | tf_op jit(solution)/shard_map/ppermute | solution.py:48
  53.1 4.4 %collective-permute-start.16 = (f32[128,128]{1,0:T(8,128)S(1)}, f32[128,128]{1,0:T(8,128)S(1)}, u32[]{:S(2)}, u32[]{:S(2)}) collective-permute-start(f32[128,128]{1,0:T(8,128)S(1)} %constant_dynamic-update-slice_fusion.refs_9_), channel_id=1, source_target_pairs={{0,2},{2,0},{1,3},{3,1},{4,6},{6,4},{5,7},{7,5},{8,10},{10,8},{9,1... | collective-permute-start | bytes 196616 | tf_op jit(solution)/shard_map/ppermute | solution.py:48
  55.3 2.3 %collective-permute-start.15 = (f32[128,128]{1,0:T(8,128)S(1)}, f32[128,128]{1,0:T(8,128)S(1)}, u32[]{:S(2)}, u32[]{:S(2)}) collective-permute-start(f32[128,128]{1,0:T(8,128)S(1)} %constant_dynamic-update-slice_fusion.refs_9_), channel_id=1, source_target_pairs={{0,1},{1,0},{2,3},{3,2},{4,5},{5,4},{6,7},{7,6},{8,9},{9,8},{10,11... | collective-permute-start | bytes 196616 | tf_op jit(solution)/shard_map/ppermute | solution.py:48
  57.5 1.3 %collective-permute-start.17 = (f32[128,128]{1,0:T(8,128)S(1)}, f32[128,128]{1,0:T(8,128)S(1)}, u32[]{:S(2)}, u32[]{:S(2)}) collective-permute-start(f32[128,128]{1,0:T(8,128)S(1)} %collective-permute-done.16.refs_11_), channel_id=1, source_target_pairs={{0,1},{1,0},{2,3},{3,2},{4,5},{5,4},{6,7},{7,6},{8,9},{9,8},{10,11... | collective-permute-start | bytes 196616 | tf_op jit(solution)/shard_map/ppermute | solution.py:48
  64.3 7.1 %collective-permute-start.20 = (f32[32,128]{1,0:T(8,128)S(1)}, f32[32,128]{1,0:T(8,128)S(1)}, u32[]{:S(2)}, u32[]{:S(2)}) collective-permute-start(f32[32,128]{1,0:T(8,128)S(1)} %get-tuple-element.51), channel_id=1, source_target_pairs={{0,12},{4,8},{8,4},{12,0},{1,13},{5,9},{9,5},{13,1},{2,14},{6,10},... | collective-permute-start | bytes 49160 | tf_op jit(solution)/shard_map/ppermute | solution.py:48
  66.3 5.1 %collective-permute-start.19 = (f32[32,128]{1,0:T(8,128)S(1)}, f32[32,128]{1,0:T(8,128)S(1)}, u32[]{:S(2)}, u32[]{:S(2)}) collective-permute-start(f32[32,128]{1,0:T(8,128)S(1)} %get-tuple-element.51), channel_id=1, source_target_pairs={{0,8},{4,12},{8,0},{12,4},{1,9},{5,13},{9,1},{13,5},{2,10},{6,14},... | collective-permute-start | bytes 49160 | tf_op jit(solution)/shard_map/ppermute | solution.py:48
  67.7 3.7 %collective-permute-start.18 = (f32[32,128]{1,0:T(8,128)S(1)}, f32[32,128]{1,0:T(8,128)S(1)}, u32[]{:S(2)}, u32[]{:S(2)}) collective-permute-start(f32[32,128]{1,0:T(8,128)S(1)} %get-tuple-element.51), channel_id=1, source_target_pairs={{0,4},{4,0},{8,12},{12,8},{1,5},{5,1},{9,13},{13,9},{2,6},{6,2},{1... | collective-permute-start | bytes 49160 | tf_op jit(solution)/shard_map/ppermute | solution.py:48
  71.5 4.3 %collective-permute-start.22 = (f32[128,128]{1,0:T(8,128)S(1)}, f32[128,128]{1,0:T(8,128)S(1)}, u32[]{:S(2)}, u32[]{:S(2)}) collective-permute-start(f32[128,128]{1,0:T(8,128)S(1)} %constant_dynamic-update-slice_fusion.4.refs_9_), channel_id=1, source_target_pairs={{0,2},{2,0},{1,3},{3,1},{4,6},{6,4},{5,7},{7,5},{8,10},{10,8},{9,1... | collective-permute-start | bytes 196616 | tf_op jit(solution)/shard_map/ppermute | solution.py:48
  73.0 2.8 %collective-permute-start.21 = (f32[128,128]{1,0:T(8,128)S(1)}, f32[128,128]{1,0:T(8,128)S(1)}, u32[]{:S(2)}, u32[]{:S(2)}) collective-permute-start(f32[128,128]{1,0:T(8,128)S(1)} %constant_dynamic-update-slice_fusion.4.refs_9_), channel_id=1, source_target_pairs={{0,1},{1,0},{2,3},{3,2},{4,5},{5,4},{6,7},{7,6},{8,9},{9,8},{10,11... | collective-permute-start | bytes 196616 | tf_op jit(solution)/shard_map/ppermute | solution.py:48
  75.8 1.3 %collective-permute-start.23 = (f32[128,128]{1,0:T(8,128)S(1)}, f32[128,128]{1,0:T(8,128)S(1)}, u32[]{:S(2)}, u32[]{:S(2)}) collective-permute-start(f32[128,128]{1,0:T(8,128)S(1)} %collective-permute-done.22.refs_11_), channel_id=1, source_target_pairs={{0,1},{1,0},{2,3},{3,2},{4,5},{5,4},{6,7},{7,6},{8,9},{9,8},{10,11... | collective-permute-start | bytes 196616 | tf_op jit(solution)/shard_map/ppermute | solution.py:48
  82.7 6.4 %collective-permute-start.26 = (f32[8,128]{1,0:T(8,128)S(1)}, f32[8,128]{1,0:T(8,128)S(1)}, u32[]{:S(2)}, u32[]{:S(2)}) collective-permute-start(f32[8,128]{1,0:T(8,128)S(1)} %get-tuple-element.57), channel_id=1, source_target_pairs={{0,12},{4,8},{8,4},{12,0},{1,13},{5,9},{9,5},{13,1},{2,14},{6,10},... | collective-permute-start | bytes 12296 | tf_op jit(solution)/shard_map/ppermute | solution.py:48
  84.4 4.7 %collective-permute-start.25 = (f32[8,128]{1,0:T(8,128)S(1)}, f32[8,128]{1,0:T(8,128)S(1)}, u32[]{:S(2)}, u32[]{:S(2)}) collective-permute-start(f32[8,128]{1,0:T(8,128)S(1)} %get-tuple-element.57), channel_id=1, source_target_pairs={{0,8},{4,12},{8,0},{12,4},{1,9},{5,13},{9,1},{13,5},{2,10},{6,14},... | collective-permute-start | bytes 12296 | tf_op jit(solution)/shard_map/ppermute | solution.py:48
  85.5 3.6 %collective-permute-start.24 = (f32[8,128]{1,0:T(8,128)S(1)}, f32[8,128]{1,0:T(8,128)S(1)}, u32[]{:S(2)}, u32[]{:S(2)}) collective-permute-start(f32[8,128]{1,0:T(8,128)S(1)} %get-tuple-element.57), channel_id=1, source_target_pairs={{0,4},{4,0},{8,12},{12,8},{1,5},{5,1},{9,13},{13,9},{2,6},{6,2},{1... | collective-permute-start | bytes 12296 | tf_op jit(solution)/shard_map/ppermute | solution.py:48
  89.1 4.0 %collective-permute-start.28 = (f32[64,128]{1,0:T(8,128)S(1)}, f32[64,128]{1,0:T(8,128)S(1)}, u32[]{:S(2)}, u32[]{:S(2)}) collective-permute-start(f32[64,128]{1,0:T(8,128)S(1)} %constant_dynamic-update-slice_fusion.8.refs_4_), channel_id=1, source_target_pairs={{0,2},{2,0},{1,3},{3,1},{4,6},{6,4},{5,7},{7,5},{8,10},{10,8},{9,1... | collective-permute-start | bytes 98312 | tf_op jit(solution)/shard_map/ppermute | solution.py:48
  91.1 2.0 %collective-permute-start.27 = (f32[64,128]{1,0:T(8,128)S(1)}, f32[64,128]{1,0:T(8,128)S(1)}, u32[]{:S(2)}, u32[]{:S(2)}) collective-permute-start(f32[64,128]{1,0:T(8,128)S(1)} %constant_dynamic-update-slice_fusion.8.refs_4_), channel_id=1, source_target_pairs={{0,1},{1,0},{2,3},{3,2},{4,5},{5,4},{6,7},{7,6},{8,9},{9,8},{10,11... | collective-permute-start | bytes 98312 | tf_op jit(solution)/shard_map/ppermute | solution.py:48
  93.1 1.2 %collective-permute-start.29 = (f32[64,128]{1,0:T(8,128)S(1)}, f32[64,128]{1,0:T(8,128)S(1)}, u32[]{:S(2)}, u32[]{:S(2)}) collective-permute-start(f32[64,128]{1,0:T(8,128)S(1)} %collective-permute-done.28.refs_6_), channel_id=1, source_target_pairs={{0,1},{1,0},{2,3},{3,2},{4,5},{5,4},{6,7},{7,6},{8,9},{9,8},{10,11... | collective-permute-start | bytes 98312 | tf_op jit(solution)/shard_map/ppermute | solution.py:48

commit v7 on v6

--- a/solution.py
+++ b/solution.py
@@ -144,12 +144,12 @@
         base = (c * BS).astype(F32)
         bounds = jnp.where(ends <= base, 1.0, 0.0) + jnp.where(starts < base + BS, 1024.0, 0.0)
         bounds = jnp.sum(bounds).astype(jnp.int32)
-        first = jnp.minimum(lax.shift_right_logical(jnp.bitwise_and(bounds, 1023), 2), at // 4)
-        last = lax.shift_right_logical(lax.shift_right_logical(bounds, 10) + 3, 2)
+        first = jnp.minimum(lax.shift_right_logical(jnp.bitwise_and(bounds, 1023), 3), at // 8)
+        last = lax.shift_right_logical(lax.shift_right_logical(bounds, 10) + 7, 3)
 
         def lines(g, total):
-            for u in range(4):
-                r = 4 * g + u
+            for u in range(8):
+                r = 8 * g + u
                 hit = place[pl.ds(r, 1), :] == slot
                 total = jnp.where(hit, value[pl.ds(r, 1), :], total)
             return total
@@ -361,14 +361,14 @@
     return jnp.sum(jnp.sum(x, axis=0, keepdims=True), axis=1, keepdims=True)
 
 
-def place_block(piece_ref, part, first, rhs_ref):
+def place_block(sz, piece_ref, part, first, rhs_ref):
     def one(k, unused):
         h, m, l = features_of([block_row(piece_ref, c, part, k) for c in range(3)], -2.0, 4, 3)
         feats = jnp.concatenate([h, m, h, m, l, h], axis=0).astype(BF16)
         rhs_ref[pl.ds(pl.multiple_of((first + k) * DEPTH, DEPTH), DEPTH), :] = feats
         return unused
 
-    lax.fori_loop(0, part, one, 0, unroll=4)
+    lax.fori_loop(0, part, one, 0, unroll=max(4, 64 // sz.blks))
 
 
 def first_kernel(sz, *refs):
@@ -389,9 +389,9 @@
         part = sz.local_blocks // sz.reps
         first = jnp.bitwise_xor(blk, code) * sz.local_blocks + jnp.bitwise_xor(rep, turn) * part
         first = pl.multiple_of(first, 8)
-        place_block(piece_ref, part, first, rhs_ref)
+        place_block(sz, piece_ref, part, first, rhs_ref)
         obs_ref[pl.ds(first, part), :] = piece_ref[3 * part : 4 * part, :]
-    place_block(home_ref, sz.local_blocks, blk * sz.local_blocks, rhs_ref)
+    place_block(sz, home_ref, sz.local_blocks, blk * sz.local_blocks, rhs_ref)
     far = lax.broadcasted_iota(jnp.int32, (DEPTH, BS), 0) == 3
     rhs_ref[sz.blocks * DEPTH :, :] = jnp.where(far, 1e6, 0.0).astype(BF16)
     count = count_ref[0]

time: 96.4 us -> 95.6 us (level)
  Pallas kernels: 36.4 us -> 34.6 us
  starting transfers between devices: 31.3 us -> 32.9 us
    pallas_call x6, Pallas kernels: 36.4 us -> 34.6 us  [call(): pl.pallas_call(kernel, in_specs=in_specs, out_shape=shapes, out_specs=out...]
    ppermute x30, starting transfers between devices: 31.3 us -> 32.9 us  [swap(): lax.ppermute(x, axis, [(i, i ^ code) for i in range(lax.axis_size(axis))])]
  transfers between devices with their start and end apart: 30 -> 30, of which waited for: 16 -> 17; matrix products, arithmetic and copies ran while one was open for 2% -> 2% of each run, Pallas kernels for 3% -> 3%
where the time goes in v7:
time: 95.6 us; the launch traced here: 93.8 us
  Pallas kernels  34.6 us (36%)
  starting transfers between devices  32.9 us (34%)
  waiting for transfers between devices  22.4 us (23%)
  other arithmetic  1.48 us (2%)
  between operations  1.4 us (1%)
  local copies, waits for them, and re-layouts  1.01 us (1%)
    pallas_call x6, Pallas kernels, call(): pl.pallas_call(kernel, in_specs=in_specs, out_shape=shapes, out_specs=out...  34.6 us
    ppermute x30, starting transfers between devices, swap(): lax.ppermute(x, axis, [(i, i ^ code) for i in range(lax.axis_size(axis))])  32.9 us
    ppermute x30, waiting for transfers between devices, swap(): lax.ppermute(x, axis, [(i, i ^ code) for i in range(lax.axis_size(axis))])  22.4 us
  transfers between devices with their start and end apart: 30, of which 17 were waited for; matrix products, arithmetic and copies ran while one was open for 2% of the time, Pallas kernels for 3%

profile of v7, /device:TPU:0, one launch (start us, length us, event | category | flops | bytes accessed | tf_op | source)
XLA Modules:
  0.0 93.8 jit_solution(16191424298469267975)
XLA Ops:
  1.3 0.7 broadcast_select_fusion
  2.0 5.0 %collective-permute-start.2 = (s32[4,128]{1,0:T(4,128)S(1)}, s32[4,128]{1,0:T(4,128)S(1)}, u32[]{:S(2)}, u32[]{:S(2)}) collective-permute-start(s32[4,128]{1,0:T(4,128)S(1)} %reshape.28), channel_id=1, source_target_pairs={{0,12},{4,8},{8,4},{12,0},{1,13},{5,9},{9,5},{13,1},{2,14},{6,10},... | collective-permute-start | bytes 6152 | tf_op jit(solution)/shard_map/ppermute | solution.py:48
  7.0 0.0 collective-permute-start.1
  7.0 0.6 collective-permute-start
  7.7 1.0 %copy.9 = f32[1,3,128,128]{3,2,1,0:T(8,128)S(1)} copy(f32[1,3,128,128]{3,1,2,0:T(4,128)} %bitcast.19) | data formatting | bytes 393216
  8.6 0.8 fusion
  9.4 3.8 %collective-permute-start.8 = (f32[256,128]{1,0:T(8,128)S(1)}, f32[256,128]{1,0:T(8,128)S(1)}, u32[]{:S(2)}, u32[]{:S(2)}) collective-permute-start(f32[256,128]{1,0:T(8,128)S(1)} %bitcast.22), channel_id=1, source_target_pairs={{0,12},{4,8},{8,4},{12,0},{1,13},{5,9},{9,5},{13,1},{2,14},{6,10},... | collective-permute-start | bytes 393224 | tf_op jit(solution)/shard_map/ppermute | solution.py:48
  13.2 0.0 collective-permute-done.2
  13.2 0.6 collective-permute-start.6
  13.9 1.7 %collective-permute-start.4 = (s32[16,128]{1,0:T(8,128)S(1)}, s32[16,128]{1,0:T(8,128)S(1)}, u32[]{:S(2)}, u32[]{:S(2)}) collective-permute-start(s32[16,128]{1,0:T(8,128)S(1)} %pad_add_fusion.refs_0_), channel_id=1, source_target_pairs={{0,2},{2,0},{1,3},{3,1},{4,6},{6,4},{5,7},{7,5},{8,10},{10,8},{9,1... | collective-permute-start | bytes 24584 | tf_op jit(solution)/shard_map/ppermute | solution.py:48
  15.6 2.0 %collective-permute-done.4.refs_2_ = s32[16,128]{1,0:T(8,128)S(1)} collective-permute-done((s32[16,128]{1,0:T(8,128)S(1)}, s32[16,128]{1,0:T(8,128)S(1)}, u32[]{:S(2)}, u32[]{:S(2)}) %collective-permute-start.4) | collective-permute-done | bytes 8224 | tf_op jit(solution)/shard_map/ppermute | solution.py:48
  17.6 0.0 collective-permute-start.5
  17.6 0.4 shard_map.69.refs_2_
  18.0 0.0 collective-permute-done.3.refs_1_
  18.0 0.8 collective-permute-done.5.refs_3_
  18.8 2.8 %shard_map.68 = (s32[24,128]{1,0:T(8,128)S(1)}, s32[1]{0:T(128)}) custom-call(s32[16,128]{1,0:T(8,128)S(1)} %pad_add_fusion.refs_0_, s32[16,128]{1,0:T(8,128)S(1)} %collective-permute-done.3.refs_1_, s32[16,128]{1,0:T(8,128)S(1)} %collective-permute-done.4.refs_2_, s32[16,128]{1,0:T(8,128)S(1)} %collective-permute-done.5.refs_3_), custom_call_target="tpu_custom_call" | custom-call | flops 10000000 | bytes 1048576 | tf_op jit(solution)/shard_map/pallas_call | solution.py:490
  21.6 1.8 %collective-permute-done.7.refs_8_ = f32[256,128]{1,0:T(8,128)S(1)} collective-permute-done((f32[256,128]{1,0:T(8,128)S(1)}, f32[256,128]{1,0:T(8,128)S(1)}, u32[]{:S(2)}, u32[]{:S(2)}) %collective-permute-start.7) | collective-permute-done | bytes 131104 | tf_op jit(solution)/shard_map/ppermute | solution.py:48
  23.4 0.5 collective-permute-start.10
  23.9 0.0 collective-permute-start.11
  23.9 0.8 collective-permute-done.9.refs_7_
  24.8 0.2 collective-permute-done.10.refs_9_
  25.0 0.3 collective-permute-done.11.refs_11_
  25.3 19.8 %shard_map.70 = (f32[14336,128]{1,0:T(8,128)S(1)}, f32[14336,128]{1,0:T(8,128)S(1)}, f32[14336,128]{1,0:T(8,128)S(1)}, f32[14336,128]{1,0:T(8,128)S(1)}, bf16[24...) custom-call(s32[3072]{0:T(1024)S(1)} %bitcast.16, ...), custom_call_target="tpu_custom_call" | custom-call | flops 100000000 | bytes 1048576 | tf_op jit(solution)/shard_map/pallas_call | solution.py:490
  45.1 1.9 %collective-permute-start.14 = (f32[32,128]{1,0:T(8,128)S(1)}, f32[32,128]{1,0:T(8,128)S(1)}, u32[]{:S(2)}, u32[]{:S(2)}) collective-permute-start(f32[32,128]{1,0:T(8,128)S(1)} %get-tuple-element.42), channel_id=1, source_target_pairs={{0,12},{4,8},{8,4},{12,0},{1,13},{5,9},{9,5},{13,1},{2,14},{6,10},... | collective-permute-start | bytes 49160 | tf_op jit(solution)/shard_map/ppermute | solution.py:48
  47.0 2.6 %collective-permute-start.12 = (f32[32,128]{1,0:T(8,128)S(1)}, f32[32,128]{1,0:T(8,128)S(1)}, u32[]{:S(2)}, u32[]{:S(2)}) collective-permute-start(f32[32,128]{1,0:T(8,128)S(1)} %get-tuple-element.42), channel_id=1, source_target_pairs={{0,4},{4,0},{8,12},{12,8},{1,5},{5,1},{9,13},{13,9},{2,6},{6,2},{1... | collective-permute-start | bytes 49160 | tf_op jit(solution)/shard_map/ppermute | solution.py:48
  49.6 1.7 %collective-permute-done.12 = f32[32,128]{1,0:T(8,128)S(1)} collective-permute-done((f32[32,128]{1,0:T(8,128)S(1)}, f32[32,128]{1,0:T(8,128)S(1)}, u32[]{:S(2)}, u32[]{:S(2)}) %collective-permute-start.12) | collective-permute-done | bytes 16416 | tf_op jit(solution)/shard_map/ppermute | solution.py:48
  51.3 0.3 collective-permute-done.13
  51.6 2.8 %collective-permute-start.16 = (f32[128,128]{1,0:T(8,128)S(1)}, f32[128,128]{1,0:T(8,128)S(1)}, u32[]{:S(2)}, u32[]{:S(2)}) collective-permute-start(f32[128,128]{1,0:T(8,128)S(1)} %constant_dynamic-update-slice_fusion.refs_9_), channel_id=1, source_target_pairs={{0,2},{2,0},{1,3},{3,1},{4,6},{6,4},{5,7},{7,5},{8,10},{10,8},{9,1... | collective-permute-start | bytes 196616 | tf_op jit(solution)/shard_map/ppermute | solution.py:48
  54.4 2.2 %collective-permute-done.16.refs_11_ = f32[128,128]{1,0:T(8,128)S(1)} collective-permute-done((f32[128,128]{1,0:T(8,128)S(1)}, f32[128,128]{1,0:T(8,128)S(1)}, u32[]{:S(2)}, u32[]{:S(2)}) %collective-permute-start.16) | collective-permute-done | bytes 65568 | tf_op jit(solution)/shard_map/ppermute | solution.py:48
  56.6 1.2 %collective-permute-done.17.refs_12_ = f32[128,128]{1,0:T(8,128)S(1)} collective-permute-done((f32[128,128]{1,0:T(8,128)S(1)}, f32[128,128]{1,0:T(8,128)S(1)}, u32[]{:S(2)}, u32[]{:S(2)}) %collective-permute-start.17) | collective-permute-done | bytes 65568 | tf_op jit(solution)/shard_map/ppermute | solution.py:48
  57.9 5.4 %shard_map.71 = (f32[32,128]{1,0:T(8,128)S(1)}, f32[8,128]{1,0:T(8,128)S(1)}, f32[128,128]{1,0:T(8,128)S(1)}, f32[512,128]{1,0:T(8,128)S(1)}, f32[512,128]{1,0:T(8,128)S(1)}) custom-call(s32[3072]{0:T(1024)S(1)} %bitcast.17, s32[1]{0:T(128)} %get-tuple-element.33.refs_1_, bf16[4224,128]{1,0:T(8,128)(2,1)S(1)} %shard_map.69.refs_2_, ...), custom_call_target="tpu_custom_call" | custom-call | flops 100000000 | bytes 1048576 | tf_op jit(solution)/shard_map/pallas_call | solution.py:490
  63.3 1.5 %collective-permute-start.20 = (f32[32,128]{1,0:T(8,128)S(1)}, f32[32,128]{1,0:T(8,128)S(1)}, u32[]{:S(2)}, u32[]{:S(2)}) collective-permute-start(f32[32,128]{1,0:T(8,128)S(1)} %get-tuple-element.51), channel_id=1, source_target_pairs={{0,12},{4,8},{8,4},{12,0},{1,13},{5,9},{9,5},{13,1},{2,14},{6,10},... | collective-permute-start | bytes 49160 | tf_op jit(solution)/shard_map/ppermute | solution.py:48
  64.9 0.8 collective-permute-start.19
  65.7 2.1 %collective-permute-start.18 = (f32[32,128]{1,0:T(8,128)S(1)}, f32[32,128]{1,0:T(8,128)S(1)}, u32[]{:S(2)}, u32[]{:S(2)}) collective-permute-start(f32[32,128]{1,0:T(8,128)S(1)} %get-tuple-element.51), channel_id=1, source_target_pairs={{0,4},{4,0},{8,12},{12,8},{1,5},{5,1},{9,13},{13,9},{2,6},{6,2},{1... | collective-permute-start | bytes 49160 | tf_op jit(solution)/shard_map/ppermute | solution.py:48
  67.8 1.9 %collective-permute-done.18 = f32[32,128]{1,0:T(8,128)S(1)} collective-permute-done((f32[32,128]{1,0:T(8,128)S(1)}, f32[32,128]{1,0:T(8,128)S(1)}, u32[]{:S(2)}, u32[]{:S(2)}) %collective-permute-start.18) | collective-permute-done | bytes 16416 | tf_op jit(solution)/shard_map/ppermute | solution.py:48
  69.7 2.2 %collective-permute-start.22 = (f32[128,128]{1,0:T(8,128)S(1)}, f32[128,128]{1,0:T(8,128)S(1)}, u32[]{:S(2)}, u32[]{:S(2)}) collective-permute-start(f32[128,128]{1,0:T(8,128)S(1)} %constant_dynamic-update-slice_fusion.4.refs_9_), channel_id=1, source_target_pairs={{0,2},{2,0},{1,3},{3,1},{4,6},{6,4},{5,7},{7,5},{8,10},{10,8},{9,1... | collective-permute-start | bytes 196616 | tf_op jit(solution)/shard_map/ppermute | solution.py:48
  71.9 2.2 %collective-permute-done.22.refs_11_ = f32[128,128]{1,0:T(8,128)S(1)} collective-permute-done((f32[128,128]{1,0:T(8,128)S(1)}, f32[128,128]{1,0:T(8,128)S(1)}, u32[]{:S(2)}, u32[]{:S(2)}) %collective-permute-start.22) | collective-permute-done | bytes 65568 | tf_op jit(solution)/shard_map/ppermute | solution.py:48
  74.1 1.2 %collective-permute-done.23.refs_12_ = f32[128,128]{1,0:T(8,128)S(1)} collective-permute-done((f32[128,128]{1,0:T(8,128)S(1)}, f32[128,128]{1,0:T(8,128)S(1)}, u32[]{:S(2)}, u32[]{:S(2)}) %collective-permute-start.23) | collective-permute-done | bytes 65568 | tf_op jit(solution)/shard_map/ppermute | solution.py:48
  75.4 5.5 %shard_map.72 = (f32[32,128]{1,0:T(8,128)S(1)}, f32[8,128]{1,0:T(8,128)S(1)}, f32[128,128]{1,0:T(8,128)S(1)}, f32[128,128]{1,0:T(8,128)S(1)}, f32[128,128]{1,0:T(8,128)S(1)}, /*index=5*/f32[8,128]{1,0:T(8,128)S(1)}) custom-call(s32[3072]{0:T(1024)S(1)} %bitcast.18, s32[1]{0:T(128)} %get-tuple-element.33.refs_1_, bf16[4224,128]{1,0:T(8,128)(2,1)S(1)} %shard_map.69.refs_2_, ...), custom_call_target="tpu_custom_call" | custom-call | flops 100000000 | bytes 1048576 | tf_op jit(solution)/shard_map/pallas_call | solution.py:490
  80.9 2.3 %collective-permute-start.26 = (f32[8,128]{1,0:T(8,128)S(1)}, f32[8,128]{1,0:T(8,128)S(1)}, u32[]{:S(2)}, u32[]{:S(2)}) collective-permute-start(f32[8,128]{1,0:T(8,128)S(1)} %get-tuple-element.57), channel_id=1, source_target_pairs={{0,12},{4,8},{8,4},{12,0},{1,13},{5,9},{9,5},{13,1},{2,14},{6,10},... | collective-permute-start | bytes 12296 | tf_op jit(solution)/shard_map/ppermute | solution.py:48
  83.2 0.8 collective-permute-start.25
  84.0 1.4 %collective-permute-start.24 = (f32[8,128]{1,0:T(8,128)S(1)}, f32[8,128]{1,0:T(8,128)S(1)}, u32[]{:S(2)}, u32[]{:S(2)}) collective-permute-start(f32[8,128]{1,0:T(8,128)S(1)} %get-tuple-element.57), channel_id=1, source_target_pairs={{0,4},{4,0},{8,12},{12,8},{1,5},{5,1},{9,13},{13,9},{2,6},{6,2},{1... | collective-permute-start | bytes 12296 | tf_op jit(solution)/shard_map/ppermute | solution.py:48
  85.4 2.2 %collective-permute-done.24 = f32[8,128]{1,0:T(8,128)S(1)} collective-permute-done((f32[8,128]{1,0:T(8,128)S(1)}, f32[8,128]{1,0:T(8,128)S(1)}, u32[]{:S(2)}, u32[]{:S(2)}) %collective-permute-start.24) | collective-permute-done | bytes 4128 | tf_op jit(solution)/shard_map/ppermute | solution.py:48
  87.6 0.1 collective-permute-done.25
  87.7 2.3 %collective-permute-start.28 = (f32[64,128]{1,0:T(8,128)S(1)}, f32[64,128]{1,0:T(8,128)S(1)}, u32[]{:S(2)}, u32[]{:S(2)}) collective-permute-start(f32[64,128]{1,0:T(8,128)S(1)} %constant_dynamic-update-slice_fusion.8.refs_4_), channel_id=1, source_target_pairs={{0,2},{2,0},{1,3},{3,1},{4,6},{6,4},{5,7},{7,5},{8,10},{10,8},{9,1... | collective-permute-start | bytes 98312 | tf_op jit(solution)/shard_map/ppermute | solution.py:48
  90.0 1.9 %collective-permute-done.28.refs_6_ = f32[64,128]{1,0:T(8,128)S(1)} collective-permute-done((f32[64,128]{1,0:T(8,128)S(1)}, f32[64,128]{1,0:T(8,128)S(1)}, u32[]{:S(2)}, u32[]{:S(2)}) %collective-permute-start.28) | collective-permute-done | bytes 32800 | tf_op jit(solution)/shard_map/ppermute | solution.py:48
  91.9 1.2 %collective-permute-done.29.refs_7_ = f32[64,128]{1,0:T(8,128)S(1)} collective-permute-done((f32[64,128]{1,0:T(8,128)S(1)}, f32[64,128]{1,0:T(8,128)S(1)}, u32[]{:S(2)}, u32[]{:S(2)}) %collective-permute-start.29) | collective-permute-done | bytes 32800 | tf_op jit(solution)/shard_map/ppermute | solution.py:48
  93.1 0.7 shard_map.73
  (37 shorter events, 0.1 us)
Async XLA Ops:
  2.0 11.3 %collective-permute-start.2 = (s32[4,128]{1,0:T(4,128)S(1)}, s32[4,128]{1,0:T(4,128)S(1)}, u32[]{:S(2)}, u32[]{:S(2)}) collective-permute-start(s32[4,128]{1,0:T(4,128)S(1)} %reshape.28), channel_id=1, source_target_pairs={{0,12},{4,8},{8,4},{12,0},{1,13},{5,9},{9,5},{13,1},{2,14},{6,10},... | collective-permute-start | bytes 6152 | tf_op jit(solution)/shard_map/ppermute | solution.py:48
  7.0 6.8 %collective-permute-start.1 = (s32[4,128]{1,0:T(4,128)S(1)}, s32[4,128]{1,0:T(4,128)S(1)}, u32[]{:S(2)}, u32[]{:S(2)}) collective-permute-start(s32[4,128]{1,0:T(4,128)S(1)} %reshape.28), channel_id=1, source_target_pairs={{0,8},{4,12},{8,0},{12,4},{1,9},{5,13},{9,1},{13,5},{2,10},{6,14},... | collective-permute-start | bytes 6152 | tf_op jit(solution)/shard_map/ppermute | solution.py:48
  7.0 6.8 %collective-permute-start = (s32[4,128]{1,0:T(4,128)S(1)}, s32[4,128]{1,0:T(4,128)S(1)}, u32[]{:S(2)}, u32[]{:S(2)}) collective-permute-start(s32[4,128]{1,0:T(4,128)S(1)} %reshape.28), channel_id=1, source_target_pairs={{0,4},{4,0},{8,12},{12,8},{1,5},{5,1},{9,13},{13,9},{2,6},{6,2},{1... | collective-permute-start | bytes 6152 | tf_op jit(solution)/shard_map/ppermute | solution.py:48
  9.4 12.2 %collective-permute-start.8 = (f32[256,128]{1,0:T(8,128)S(1)}, f32[256,128]{1,0:T(8,128)S(1)}, u32[]{:S(2)}, u32[]{:S(2)}) collective-permute-start(f32[256,128]{1,0:T(8,128)S(1)} %bitcast.22), channel_id=1, source_target_pairs={{0,12},{4,8},{8,4},{12,0},{1,13},{5,9},{9,5},{13,1},{2,14},{6,10},... | collective-permute-start | bytes 393224 | tf_op jit(solution)/shard_map/ppermute | solution.py:48
  13.2 10.2 %collective-permute-start.7 = (f32[256,128]{1,0:T(8,128)S(1)}, f32[256,128]{1,0:T(8,128)S(1)}, u32[]{:S(2)}, u32[]{:S(2)}) collective-permute-start(f32[256,128]{1,0:T(8,128)S(1)} %bitcast.23), channel_id=1, source_target_pairs={{0,8},{4,12},{8,0},{12,4},{1,9},{5,13},{9,1},{13,5},{2,10},{6,14},... | collective-permute-start | bytes 393224 | tf_op jit(solution)/shard_map/ppermute | solution.py:48
  13.2 10.2 %collective-permute-start.6 = (f32[256,128]{1,0:T(8,128)S(1)}, f32[256,128]{1,0:T(8,128)S(1)}, u32[]{:S(2)}, u32[]{:S(2)}) collective-permute-start(f32[256,128]{1,0:T(8,128)S(1)} %bitcast.24), channel_id=1, source_target_pairs={{0,4},{4,0},{8,12},{12,8},{1,5},{5,1},{9,13},{13,9},{2,6},{6,2},{1... | collective-permute-start | bytes 393224 | tf_op jit(solution)/shard_map/ppermute | solution.py:48
  13.9 3.7 %collective-permute-start.4 = (s32[16,128]{1,0:T(8,128)S(1)}, s32[16,128]{1,0:T(8,128)S(1)}, u32[]{:S(2)}, u32[]{:S(2)}) collective-permute-start(s32[16,128]{1,0:T(8,128)S(1)} %pad_add_fusion.refs_0_), channel_id=1, source_target_pairs={{0,2},{2,0},{1,3},{3,1},{4,6},{6,4},{5,7},{7,5},{8,10},{10,8},{9,1... | collective-permute-start | bytes 24584 | tf_op jit(solution)/shard_map/ppermute | solution.py:48
  15.6 2.4 %collective-permute-start.3 = (s32[16,128]{1,0:T(8,128)S(1)}, s32[16,128]{1,0:T(8,128)S(1)}, u32[]{:S(2)}, u32[]{:S(2)}) collective-permute-start(s32[16,128]{1,0:T(8,128)S(1)} %pad_add_fusion.refs_0_), channel_id=1, source_target_pairs={{0,1},{1,0},{2,3},{3,2},{4,5},{5,4},{6,7},{7,6},{8,9},{9,8},{10,11... | collective-permute-start | bytes 24584 | tf_op jit(solution)/shard_map/ppermute | solution.py:48
  17.6 1.2 %collective-permute-start.5 = (s32[16,128]{1,0:T(8,128)S(1)}, s32[16,128]{1,0:T(8,128)S(1)}, u32[]{:S(2)}, u32[]{:S(2)}) collective-permute-start(s32[16,128]{1,0:T(8,128)S(1)} %collective-permute-done.4.refs_2_), channel_id=1, source_target_pairs={{0,1},{1,0},{2,3},{3,2},{4,5},{5,4},{6,7},{7,6},{8,9},{9,8},{10,11... | collective-permute-start | bytes 24584 | tf_op jit(solution)/shard_map/ppermute | solution.py:48
  23.4 1.3 %collective-permute-start.9 = (f32[256,128]{1,0:T(8,128)S(1)}, f32[256,128]{1,0:T(8,128)S(1)}, u32[]{:S(2)}, u32[]{:S(2)}) collective-permute-start(f32[256,128]{1,0:T(8,128)S(1)} %collective-permute-done.6.refs_6_), channel_id=1, source_target_pairs={{0,1},{1,0},{2,3},{3,2},{4,5},{5,4},{6,7},{7,6},{8,9},{9,8},{10,11... | collective-permute-start | bytes 393224 | tf_op jit(solution)/shard_map/ppermute | solution.py:48
  23.4 1.5 %collective-permute-start.10 = (f32[256,128]{1,0:T(8,128)S(1)}, f32[256,128]{1,0:T(8,128)S(1)}, u32[]{:S(2)}, u32[]{:S(2)}) collective-permute-start(f32[256,128]{1,0:T(8,128)S(1)} %collective-permute-done.7.refs_8_), channel_id=1, source_target_pairs={{0,1},{1,0},{2,3},{3,2},{4,5},{5,4},{6,7},{7,6},{8,9},{9,8},{10,11... | collective-permute-start | bytes 393224 | tf_op jit(solution)/shard_map/ppermute | solution.py:48
  23.9 1.3 %collective-permute-start.11 = (f32[256,128]{1,0:T(8,128)S(1)}, f32[256,128]{1,0:T(8,128)S(1)}, u32[]{:S(2)}, u32[]{:S(2)}) collective-permute-start(f32[256,128]{1,0:T(8,128)S(1)} %collective-permute-done.8.refs_10_), channel_id=1, source_target_pairs={{0,1},{1,0},{2,3},{3,2},{4,5},{5,4},{6,7},{7,6},{8,9},{9,8},{10,11... | collective-permute-start | bytes 393224 | tf_op jit(solution)/shard_map/ppermute | solution.py:48
  45.1 6.5 %collective-permute-start.14 = (f32[32,128]{1,0:T(8,128)S(1)}, f32[32,128]{1,0:T(8,128)S(1)}, u32[]{:S(2)}, u32[]{:S(2)}) collective-permute-start(f32[32,128]{1,0:T(8,128)S(1)} %get-tuple-element.42), channel_id=1, source_target_pairs={{0,12},{4,8},{8,4},{12,0},{1,13},{5,9},{9,5},{13,1},{2,14},{6,10},... | collective-permute-start | bytes 49160 | tf_op jit(solution)/shard_map/ppermute | solution.py:48
  47.0 4.6 %collective-permute-start.13 = (f32[32,128]{1,0:T(8,128)S(1)}, f32[32,128]{1,0:T(8,128)S(1)}, u32[]{:S(2)}, u32[]{:S(2)}) collective-permute-start(f32[32,128]{1,0:T(8,128)S(1)} %get-tuple-element.42), channel_id=1, source_target_pairs={{0,8},{4,12},{8,0},{12,4},{1,9},{5,13},{9,1},{13,5},{2,10},{6,14},... | collective-permute-start | bytes 49160 | tf_op jit(solution)/shard_map/ppermute | solution.py:48
  47.0 4.3 %collective-permute-start.12 = (f32[32,128]{1,0:T(8,128)S(1)}, f32[32,128]{1,0:T(8,128)S(1)}, u32[]{:S(2)}, u32[]{:S(2)}) collective-permute-start(f32[32,128]{1,0:T(8,128)S(1)} %get-tuple-element.42), channel_id=1, source_target_pairs={{0,4},{4,0},{8,12},{12,8},{1,5},{5,1},{9,13},{13,9},{2,6},{6,2},{1... | collective-permute-start | bytes 49160 | tf_op jit(solution)/shard_map/ppermute | solution.py:48
  51.6 5.0 %collective-permute-start.16 = (f32[128,128]{1,0:T(8,128)S(1)}, f32[128,128]{1,0:T(8,128)S(1)}, u32[]{:S(2)}, u32[]{:S(2)}) collective-permute-start(f32[128,128]{1,0:T(8,128)S(1)} %constant_dynamic-update-slice_fusion.refs_9_), channel_id=1, source_target_pairs={{0,2},{2,0},{1,3},{3,1},{4,6},{6,4},{5,7},{7,5},{8,10},{10,8},{9,1... | collective-permute-start | bytes 196616 | tf_op jit(solution)/shard_map/ppermute | solution.py:48
  54.4 2.3 %collective-permute-start.15 = (f32[128,128]{1,0:T(8,128)S(1)}, f32[128,128]{1,0:T(8,128)S(1)}, u32[]{:S(2)}, u32[]{:S(2)}) collective-permute-start(f32[128,128]{1,0:T(8,128)S(1)} %constant_dynamic-update-slice_fusion.refs_9_), channel_id=1, source_target_pairs={{0,1},{1,0},{2,3},{3,2},{4,5},{5,4},{6,7},{7,6},{8,9},{9,8},{10,11... | collective-permute-start | bytes 196616 | tf_op jit(solution)/shard_map/ppermute | solution.py:48
  56.6 1.3 %collective-permute-start.17 = (f32[128,128]{1,0:T(8,128)S(1)}, f32[128,128]{1,0:T(8,128)S(1)}, u32[]{:S(2)}, u32[]{:S(2)}) collective-permute-start(f32[128,128]{1,0:T(8,128)S(1)} %collective-permute-done.16.refs_11_), channel_id=1, source_target_pairs={{0,1},{1,0},{2,3},{3,2},{4,5},{5,4},{6,7},{7,6},{8,9},{9,8},{10,11... | collective-permute-start | bytes 196616 | tf_op jit(solution)/shard_map/ppermute | solution.py:48
  63.3 6.4 %collective-permute-start.20 = (f32[32,128]{1,0:T(8,128)S(1)}, f32[32,128]{1,0:T(8,128)S(1)}, u32[]{:S(2)}, u32[]{:S(2)}) collective-permute-start(f32[32,128]{1,0:T(8,128)S(1)} %get-tuple-element.51), channel_id=1, source_target_pairs={{0,12},{4,8},{8,4},{12,0},{1,13},{5,9},{9,5},{13,1},{2,14},{6,10},... | collective-permute-start | bytes 49160 | tf_op jit(solution)/shard_map/ppermute | solution.py:48
  64.9 4.8 %collective-permute-start.19 = (f32[32,128]{1,0:T(8,128)S(1)}, f32[32,128]{1,0:T(8,128)S(1)}, u32[]{:S(2)}, u32[]{:S(2)}) collective-permute-start(f32[32,128]{1,0:T(8,128)S(1)} %get-tuple-element.51), channel_id=1, source_target_pairs={{0,8},{4,12},{8,0},{12,4},{1,9},{5,13},{9,1},{13,5},{2,10},{6,14},... | collective-permute-start | bytes 49160 | tf_op jit(solution)/shard_map/ppermute | solution.py:48
  65.7 4.0 %collective-permute-start.18 = (f32[32,128]{1,0:T(8,128)S(1)}, f32[32,128]{1,0:T(8,128)S(1)}, u32[]{:S(2)}, u32[]{:S(2)}) collective-permute-start(f32[32,128]{1,0:T(8,128)S(1)} %get-tuple-element.51), channel_id=1, source_target_pairs={{0,4},{4,0},{8,12},{12,8},{1,5},{5,1},{9,13},{13,9},{2,6},{6,2},{1... | collective-permute-start | bytes 49160 | tf_op jit(solution)/shard_map/ppermute | solution.py:48
  69.7 4.4 %collective-permute-start.22 = (f32[128,128]{1,0:T(8,128)S(1)}, f32[128,128]{1,0:T(8,128)S(1)}, u32[]{:S(2)}, u32[]{:S(2)}) collective-permute-start(f32[128,128]{1,0:T(8,128)S(1)} %constant_dynamic-update-slice_fusion.4.refs_9_), channel_id=1, source_target_pairs={{0,2},{2,0},{1,3},{3,1},{4,6},{6,4},{5,7},{7,5},{8,10},{10,8},{9,1... | collective-permute-start | bytes 196616 | tf_op jit(solution)/shard_map/ppermute | solution.py:48
  71.9 2.3 %collective-permute-start.21 = (f32[128,128]{1,0:T(8,128)S(1)}, f32[128,128]{1,0:T(8,128)S(1)}, u32[]{:S(2)}, u32[]{:S(2)}) collective-permute-start(f32[128,128]{1,0:T(8,128)S(1)} %constant_dynamic-update-slice_fusion.4.refs_9_), channel_id=1, source_target_pairs={{0,1},{1,0},{2,3},{3,2},{4,5},{5,4},{6,7},{7,6},{8,9},{9,8},{10,11... | collective-permute-start | bytes 196616 | tf_op jit(solution)/shard_map/ppermute | solution.py:48
  74.1 1.3 %collective-permute-start.23 = (f32[128,128]{1,0:T(8,128)S(1)}, f32[128,128]{1,0:T(8,128)S(1)}, u32[]{:S(2)}, u32[]{:S(2)}) collective-permute-start(f32[128,128]{1,0:T(8,128)S(1)} %collective-permute-done.22.refs_11_), channel_id=1, source_target_pairs={{0,1},{1,0},{2,3},{3,2},{4,5},{5,4},{6,7},{7,6},{8,9},{9,8},{10,11... | collective-permute-start | bytes 196616 | tf_op jit(solution)/shard_map/ppermute | solution.py:48
  80.9 6.8 %collective-permute-start.26 = (f32[8,128]{1,0:T(8,128)S(1)}, f32[8,128]{1,0:T(8,128)S(1)}, u32[]{:S(2)}, u32[]{:S(2)}) collective-permute-start(f32[8,128]{1,0:T(8,128)S(1)} %get-tuple-element.57), channel_id=1, source_target_pairs={{0,12},{4,8},{8,4},{12,0},{1,13},{5,9},{9,5},{13,1},{2,14},{6,10},... | collective-permute-start | bytes 12296 | tf_op jit(solution)/shard_map/ppermute | solution.py:48
  83.2 4.5 %collective-permute-start.25 = (f32[8,128]{1,0:T(8,128)S(1)}, f32[8,128]{1,0:T(8,128)S(1)}, u32[]{:S(2)}, u32[]{:S(2)}) collective-permute-start(f32[8,128]{1,0:T(8,128)S(1)} %get-tuple-element.57), channel_id=1, source_target_pairs={{0,8},{4,12},{8,0},{12,4},{1,9},{5,13},{9,1},{13,5},{2,10},{6,14},... | collective-permute-start | bytes 12296 | tf_op jit(solution)/shard_map/ppermute | solution.py:48
  84.0 3.6 %collective-permute-start.24 = (f32[8,128]{1,0:T(8,128)S(1)}, f32[8,128]{1,0:T(8,128)S(1)}, u32[]{:S(2)}, u32[]{:S(2)}) collective-permute-start(f32[8,128]{1,0:T(8,128)S(1)} %get-tuple-element.57), channel_id=1, source_target_pairs={{0,4},{4,0},{8,12},{12,8},{1,5},{5,1},{9,13},{13,9},{2,6},{6,2},{1... | collective-permute-start | bytes 12296 | tf_op jit(solution)/shard_map/ppermute | solution.py:48
  87.7 4.2 %collective-permute-start.28 = (f32[64,128]{1,0:T(8,128)S(1)}, f32[64,128]{1,0:T(8,128)S(1)}, u32[]{:S(2)}, u32[]{:S(2)}) collective-permute-start(f32[64,128]{1,0:T(8,128)S(1)} %constant_dynamic-update-slice_fusion.8.refs_4_), channel_id=1, source_target_pairs={{0,2},{2,0},{1,3},{3,1},{4,6},{6,4},{5,7},{7,5},{8,10},{10,8},{9,1... | collective-permute-start | bytes 98312 | tf_op jit(solution)/shard_map/ppermute | solution.py:48
  90.0 1.9 %collective-permute-start.27 = (f32[64,128]{1,0:T(8,128)S(1)}, f32[64,128]{1,0:T(8,128)S(1)}, u32[]{:S(2)}, u32[]{:S(2)}) collective-permute-start(f32[64,128]{1,0:T(8,128)S(1)} %constant_dynamic-update-slice_fusion.8.refs_4_), channel_id=1, source_target_pairs={{0,1},{1,0},{2,3},{3,2},{4,5},{5,4},{6,7},{7,6},{8,9},{9,8},{10,11... | collective-permute-start | bytes 98312 | tf_op jit(solution)/shard_map/ppermute | solution.py:48
  91.9 1.2 %collective-permute-start.29 = (f32[64,128]{1,0:T(8,128)S(1)}, f32[64,128]{1,0:T(8,128)S(1)}, u32[]{:S(2)}, u32[]{:S(2)}) collective-permute-start(f32[64,128]{1,0:T(8,128)S(1)} %collective-permute-done.28.refs_6_), channel_id=1, source_target_pairs={{0,1},{1,0},{2,3},{3,2},{4,5},{5,4},{6,7},{7,6},{8,9},{9,8},{10,11... | collective-permute-start | bytes 98312 | tf_op jit(solution)/shard_map/ppermute | solution.py:48

commit v8 on v7

--- a/solution.py
+++ b/solution.py
@@ -186,29 +186,38 @@
     full = count + jnp.sum(pad).astype(jnp.int32)
     count_ref[0] = full
 
+    pairs = lax.shift_right_logical(chunks + 1, 1)
+    key_column[pl.ds(pl.multiple_of(chunks * BS, BS), BS), :] = jnp.full((BS, BS), 1e9, F32)
+
     def rank(c, unused):
         keys = key_row[pl.ds(c, 1), :]
 
         def below(k, total):
-            lower = key_column[pl.ds(pl.multiple_of(k * BS, BS), BS), :] < keys
-            return total + jnp.where(lower, 1.0, 0.0)
+            for u in range(2):
+                lower = key_column[pl.ds(pl.multiple_of((2 * k + u) * BS, BS), BS), :] < keys
+                total = total + jnp.where(lower, 1.0, 0.0)
+            return total
 
         past = (sub + 1).astype(F32) * 65536.0 <= keys
-        total = lax.fori_loop(0, chunks, below, jnp.where(past, pad_column, 0.0))
+        total = lax.fori_loop(0, pairs, below, jnp.where(past, pad_column, 0.0))
         place[pl.ds(c, 1), :] = jnp.sum(total, axis=0, keepdims=True)
         return unused
 
     lax.fori_loop(0, chunks, rank, 0)
 
+    place[pl.ds(chunks, 1), :] = jnp.full((1, BS), -1.0, F32)
+
     def arrange(c, unused):
         slot = (sub + c * BS).astype(F32)
 
-        def line(r, total):
-            hit = place[pl.ds(r, 1), :] == slot
-            return total + jnp.where(hit, entry_row[pl.ds(r, 1), :], 0.0)
+        def line(k, total):
+            for u in range(2):
+                hit = place[pl.ds(2 * k + u, 1), :] == slot
+                total = jnp.where(hit, entry_row[pl.ds(2 * k + u, 1), :], total)
+            return total
 
         nulls = jnp.logical_or(null_places[0] == slot, null_places[1] == slot)
-        total = lax.fori_loop(0, chunks, line, jnp.where(nulls, null_entry, 0.0))
+        total = lax.fori_loop(0, pairs, line, jnp.where(nulls, null_entry, 0.0))
         found = jnp.sum(total.T, axis=0, keepdims=True).astype(jnp.int32)
         out_ref[pl.ds(c, 1), :] = jnp.where(lane + c * BS < full, found, sz.own)
         return unused

time: 95.6 us -> 94.8 us (level); the launches traced: 93.8 us -> 95.1 us
  waiting for transfers between devices: 22.4 us -> 29.1 us
  starting transfers between devices: 32.9 us -> 28.5 us
    ppermute x30, waiting for transfers between devices: 22.4 us -> 29.1 us  [swap(): lax.ppermute(x, axis, [(i, i ^ code) for i in range(lax.axis_size(axis))])]
    ppermute x30, starting transfers between devices: 32.9 us -> 28.5 us  [swap(): lax.ppermute(x, axis, [(i, i ^ code) for i in range(lax.axis_size(axis))])]
  transfers between devices with their start and end apart: 30 -> 30, of which waited for: 17 -> 18; matrix products, arithmetic and copies ran while one was open for 2% -> 2% of each run, Pallas kernels for 3% -> 3%
where the time goes in v8:
time: 94.8 us; the launch traced here: 95.1 us
  Pallas kernels  33.7 us (36%)
  waiting for transfers between devices  29.1 us (31%)
  starting transfers between devices  28.5 us (30%)
  other arithmetic  1.48 us (2%)
  between operations  1.39 us (1%)
  local copies, waits for them, and re-layouts  1 us (1%)
    pallas_call x6, Pallas kernels, call(): pl.pallas_call(kernel, in_specs=in_specs, out_shape=shapes, out_specs=out...  33.7 us
    ppermute x30, waiting for transfers between devices, swap(): lax.ppermute(x, axis, [(i, i ^ code) for i in range(lax.axis_size(axis))])  29.1 us
    ppermute x30, starting transfers between devices, swap(): lax.ppermute(x, axis, [(i, i ^ code) for i in range(lax.axis_size(axis))])  28.5 us
  transfers between devices with their start and end apart: 30, of which 18 were waited for; matrix products, arithmetic and copies ran while one was open for 2% of the time, Pallas kernels for 3%

profile of v8, /device:TPU:0, one launch (start us, length us, event | category | flops | bytes accessed | tf_op | source)
XLA Modules:
  0.0 95.1 jit_solution(7733682175319886276)
XLA Ops:
  1.3 0.7 broadcast_select_fusion
  2.0 5.0 %collective-permute-start.2 = (s32[4,128]{1,0:T(4,128)S(1)}, s32[4,128]{1,0:T(4,128)S(1)}, u32[]{:S(2)}, u32[]{:S(2)}) collective-permute-start(s32[4,128]{1,0:T(4,128)S(1)} %reshape.28), channel_id=1, source_target_pairs={{0,12},{4,8},{8,4},{12,0},{1,13},{5,9},{9,5},{13,1},{2,14},{6,10},... | collective-permute-start | bytes 6152 | tf_op jit(solution)/shard_map/ppermute | solution.py:48
  7.0 0.0 collective-permute-start.1
  7.0 0.6 collective-permute-start
  7.7 1.0 %copy.9 = f32[1,3,128,128]{3,2,1,0:T(8,128)S(1)} copy(f32[1,3,128,128]{3,1,2,0:T(4,128)} %bitcast.19) | data formatting | bytes 393216
  8.6 0.8 fusion
  9.4 3.8 %collective-permute-start.8 = (f32[256,128]{1,0:T(8,128)S(1)}, f32[256,128]{1,0:T(8,128)S(1)}, u32[]{:S(2)}, u32[]{:S(2)}) collective-permute-start(f32[256,128]{1,0:T(8,128)S(1)} %bitcast.22), channel_id=1, source_target_pairs={{0,12},{4,8},{8,4},{12,0},{1,13},{5,9},{9,5},{13,1},{2,14},{6,10},... | collective-permute-start | bytes 393224 | tf_op jit(solution)/shard_map/ppermute | solution.py:48
  13.2 0.6 collective-permute-start.6
  13.9 0.0 collective-permute-done.1
  13.9 1.7 %collective-permute-start.4 = (s32[16,128]{1,0:T(8,128)S(1)}, s32[16,128]{1,0:T(8,128)S(1)}, u32[]{:S(2)}, u32[]{:S(2)}) collective-permute-start(s32[16,128]{1,0:T(8,128)S(1)} %pad_add_fusion.refs_0_), channel_id=1, source_target_pairs={{0,2},{2,0},{1,3},{3,1},{4,6},{6,4},{5,7},{7,5},{8,10},{10,8},{9,1... | collective-permute-start | bytes 24584 | tf_op jit(solution)/shard_map/ppermute | solution.py:48
  15.6 0.0 collective-permute-start.3
  15.6 2.0 %collective-permute-done.4.refs_2_ = s32[16,128]{1,0:T(8,128)S(1)} collective-permute-done((s32[16,128]{1,0:T(8,128)S(1)}, s32[16,128]{1,0:T(8,128)S(1)}, u32[]{:S(2)}, u32[]{:S(2)}) %collective-permute-start.4) | collective-permute-done | bytes 8224 | tf_op jit(solution)/shard_map/ppermute | solution.py:48
  17.6 0.4 shard_map.69.refs_2_
  18.0 0.8 collective-permute-done.5.refs_3_
  18.8 2.7 %shard_map.68 = (s32[24,128]{1,0:T(8,128)S(1)}, s32[1]{0:T(128)}) custom-call(s32[16,128]{1,0:T(8,128)S(1)} %pad_add_fusion.refs_0_, s32[16,128]{1,0:T(8,128)S(1)} %collective-permute-done.3.refs_1_, s32[16,128]{1,0:T(8,128)S(1)} %collective-permute-done.4.refs_2_, s32[16,128]{1,0:T(8,128)S(1)} %collective-permute-done.5.refs_3_), custom_call_target="tpu_custom_call" | custom-call | flops 10000000 | bytes 1048576 | tf_op jit(solution)/shard_map/pallas_call | solution.py:499
  21.6 1.9 %collective-permute-done.7.refs_8_ = f32[256,128]{1,0:T(8,128)S(1)} collective-permute-done((f32[256,128]{1,0:T(8,128)S(1)}, f32[256,128]{1,0:T(8,128)S(1)}, u32[]{:S(2)}, u32[]{:S(2)}) %collective-permute-start.7) | collective-permute-done | bytes 131104 | tf_op jit(solution)/shard_map/ppermute | solution.py:48
  23.4 0.5 collective-permute-start.10
  23.9 0.0 collective-permute-start.11
  23.9 0.8 collective-permute-done.9.refs_7_
  24.8 0.2 collective-permute-done.10.refs_9_
  25.0 0.3 collective-permute-done.11.refs_11_
  25.3 19.2 %shard_map.70 = (f32[14336,128]{1,0:T(8,128)S(1)}, f32[14336,128]{1,0:T(8,128)S(1)}, f32[14336,128]{1,0:T(8,128)S(1)}, f32[14336,128]{1,0:T(8,128)S(1)}, bf16[24...) custom-call(s32[3072]{0:T(1024)S(1)} %bitcast.16, ...), custom_call_target="tpu_custom_call" | custom-call | flops 100000000 | bytes 1048576 | tf_op jit(solution)/shard_map/pallas_call | solution.py:499
  44.5 4.4 %collective-permute-start.14 = (f32[32,128]{1,0:T(8,128)S(1)}, f32[32,128]{1,0:T(8,128)S(1)}, u32[]{:S(2)}, u32[]{:S(2)}) collective-permute-start(f32[32,128]{1,0:T(8,128)S(1)} %get-tuple-element.42), channel_id=1, source_target_pairs={{0,12},{4,8},{8,4},{12,0},{1,13},{5,9},{9,5},{13,1},{2,14},{6,10},... | collective-permute-start | bytes 49160 | tf_op jit(solution)/shard_map/ppermute | solution.py:48
  48.9 0.6 collective-permute-start.12
  49.6 3.1 %collective-permute-done.12 = f32[32,128]{1,0:T(8,128)S(1)} collective-permute-done((f32[32,128]{1,0:T(8,128)S(1)}, f32[32,128]{1,0:T(8,128)S(1)}, u32[]{:S(2)}, u32[]{:S(2)}) %collective-permute-start.12) | collective-permute-done | bytes 16416 | tf_op jit(solution)/shard_map/ppermute | solution.py:48
  52.7 0.9 collective-permute-done.13
  53.6 0.8 collective-permute-start.16
  54.4 3.5 %collective-permute-done.16.refs_11_ = f32[128,128]{1,0:T(8,128)S(1)} collective-permute-done((f32[128,128]{1,0:T(8,128)S(1)}, f32[128,128]{1,0:T(8,128)S(1)}, u32[]{:S(2)}, u32[]{:S(2)}) %collective-permute-start.16) | collective-permute-done | bytes 65568 | tf_op jit(solution)/shard_map/ppermute | solution.py:48
  57.9 1.2 %collective-permute-done.17.refs_12_ = f32[128,128]{1,0:T(8,128)S(1)} collective-permute-done((f32[128,128]{1,0:T(8,128)S(1)}, f32[128,128]{1,0:T(8,128)S(1)}, u32[]{:S(2)}, u32[]{:S(2)}) %collective-permute-start.17) | collective-permute-done | bytes 65568 | tf_op jit(solution)/shard_map/ppermute | solution.py:48
  59.2 5.3 %shard_map.71 = (f32[32,128]{1,0:T(8,128)S(1)}, f32[8,128]{1,0:T(8,128)S(1)}, f32[128,128]{1,0:T(8,128)S(1)}, f32[512,128]{1,0:T(8,128)S(1)}, f32[512,128]{1,0:T(8,128)S(1)}) custom-call(s32[3072]{0:T(1024)S(1)} %bitcast.17, s32[1]{0:T(128)} %get-tuple-element.33.refs_1_, bf16[4224,128]{1,0:T(8,128)(2,1)S(1)} %shard_map.69.refs_2_, ...), custom_call_target="tpu_custom_call" | custom-call | flops 100000000 | bytes 1048576 | tf_op jit(solution)/shard_map/pallas_call | solution.py:499
  64.5 1.9 %collective-permute-start.20 = (f32[32,128]{1,0:T(8,128)S(1)}, f32[32,128]{1,0:T(8,128)S(1)}, u32[]{:S(2)}, u32[]{:S(2)}) collective-permute-start(f32[32,128]{1,0:T(8,128)S(1)} %get-tuple-element.51), channel_id=1, source_target_pairs={{0,12},{4,8},{8,4},{12,0},{1,13},{5,9},{9,5},{13,1},{2,14},{6,10},... | collective-permute-start | bytes 49160 | tf_op jit(solution)/shard_map/ppermute | solution.py:48
  66.4 0.3 collective-permute-start.19
  66.7 2.3 %collective-permute-start.18 = (f32[32,128]{1,0:T(8,128)S(1)}, f32[32,128]{1,0:T(8,128)S(1)}, u32[]{:S(2)}, u32[]{:S(2)}) collective-permute-start(f32[32,128]{1,0:T(8,128)S(1)} %get-tuple-element.51), channel_id=1, source_target_pairs={{0,4},{4,0},{8,12},{12,8},{1,5},{5,1},{9,13},{13,9},{2,6},{6,2},{1... | collective-permute-start | bytes 49160 | tf_op jit(solution)/shard_map/ppermute | solution.py:48
  69.0 1.7 %collective-permute-done.18 = f32[32,128]{1,0:T(8,128)S(1)} collective-permute-done((f32[32,128]{1,0:T(8,128)S(1)}, f32[32,128]{1,0:T(8,128)S(1)}, u32[]{:S(2)}, u32[]{:S(2)}) %collective-permute-start.18) | collective-permute-done | bytes 16416 | tf_op jit(solution)/shard_map/ppermute | solution.py:48
  70.7 0.4 collective-permute-done.19
  71.1 0.7 collective-permute-start.22
  71.7 3.7 %collective-permute-done.22.refs_11_ = f32[128,128]{1,0:T(8,128)S(1)} collective-permute-done((f32[128,128]{1,0:T(8,128)S(1)}, f32[128,128]{1,0:T(8,128)S(1)}, u32[]{:S(2)}, u32[]{:S(2)}) %collective-permute-start.22) | collective-permute-done | bytes 65568 | tf_op jit(solution)/shard_map/ppermute | solution.py:48
  75.4 1.2 %collective-permute-done.23.refs_12_ = f32[128,128]{1,0:T(8,128)S(1)} collective-permute-done((f32[128,128]{1,0:T(8,128)S(1)}, f32[128,128]{1,0:T(8,128)S(1)}, u32[]{:S(2)}, u32[]{:S(2)}) %collective-permute-start.23) | collective-permute-done | bytes 65568 | tf_op jit(solution)/shard_map/ppermute | solution.py:48
  76.7 5.4 %shard_map.72 = (f32[32,128]{1,0:T(8,128)S(1)}, f32[8,128]{1,0:T(8,128)S(1)}, f32[128,128]{1,0:T(8,128)S(1)}, f32[128,128]{1,0:T(8,128)S(1)}, f32[128,128]{1,0:T(8,128)S(1)}, /*index=5*/f32[8,128]{1,0:T(8,128)S(1)}) custom-call(s32[3072]{0:T(1024)S(1)} %bitcast.18, s32[1]{0:T(128)} %get-tuple-element.33.refs_1_, bf16[4224,128]{1,0:T(8,128)(2,1)S(1)} %shard_map.69.refs_2_, ...), custom_call_target="tpu_custom_call" | custom-call | flops 100000000 | bytes 1048576 | tf_op jit(solution)/shard_map/pallas_call | solution.py:499
  82.1 2.7 %collective-permute-start.26 = (f32[8,128]{1,0:T(8,128)S(1)}, f32[8,128]{1,0:T(8,128)S(1)}, u32[]{:S(2)}, u32[]{:S(2)}) collective-permute-start(f32[8,128]{1,0:T(8,128)S(1)} %get-tuple-element.57), channel_id=1, source_target_pairs={{0,12},{4,8},{8,4},{12,0},{1,13},{5,9},{9,5},{13,1},{2,14},{6,10},... | collective-permute-start | bytes 12296 | tf_op jit(solution)/shard_map/ppermute | solution.py:48
  84.8 0.8 collective-permute-start.25
  85.5 1.0 %collective-permute-start.24 = (f32[8,128]{1,0:T(8,128)S(1)}, f32[8,128]{1,0:T(8,128)S(1)}, u32[]{:S(2)}, u32[]{:S(2)}) collective-permute-start(f32[8,128]{1,0:T(8,128)S(1)} %get-tuple-element.57), channel_id=1, source_target_pairs={{0,4},{4,0},{8,12},{12,8},{1,5},{5,1},{9,13},{13,9},{2,6},{6,2},{1... | collective-permute-start | bytes 12296 | tf_op jit(solution)/shard_map/ppermute | solution.py:48
  86.5 2.6 %collective-permute-done.24 = f32[8,128]{1,0:T(8,128)S(1)} collective-permute-done((f32[8,128]{1,0:T(8,128)S(1)}, f32[8,128]{1,0:T(8,128)S(1)}, u32[]{:S(2)}, u32[]{:S(2)}) %collective-permute-start.24) | collective-permute-done | bytes 4128 | tf_op jit(solution)/shard_map/ppermute | solution.py:48
  89.1 0.1 collective-permute-done.25
  89.3 0.7 collective-permute-start.28
  90.0 3.3 %collective-permute-done.28.refs_6_ = f32[64,128]{1,0:T(8,128)S(1)} collective-permute-done((f32[64,128]{1,0:T(8,128)S(1)}, f32[64,128]{1,0:T(8,128)S(1)}, u32[]{:S(2)}, u32[]{:S(2)}) %collective-permute-start.28) | collective-permute-done | bytes 32800 | tf_op jit(solution)/shard_map/ppermute | solution.py:48
  93.3 1.2 %collective-permute-done.29.refs_7_ = f32[64,128]{1,0:T(8,128)S(1)} collective-permute-done((f32[64,128]{1,0:T(8,128)S(1)}, f32[64,128]{1,0:T(8,128)S(1)}, u32[]{:S(2)}, u32[]{:S(2)}) %collective-permute-start.29) | collective-permute-done | bytes 32800 | tf_op jit(solution)/shard_map/ppermute | solution.py:48
  94.5 0.7 shard_map.73
  (37 shorter events, 0.1 us)
Async XLA Ops:
  2.0 11.3 %collective-permute-start.2 = (s32[4,128]{1,0:T(4,128)S(1)}, s32[4,128]{1,0:T(4,128)S(1)}, u32[]{:S(2)}, u32[]{:S(2)}) collective-permute-start(s32[4,128]{1,0:T(4,128)S(1)} %reshape.28), channel_id=1, source_target_pairs={{0,12},{4,8},{8,4},{12,0},{1,13},{5,9},{9,5},{13,1},{2,14},{6,10},... | collective-permute-start | bytes 6152 | tf_op jit(solution)/shard_map/ppermute | solution.py:48
  7.0 6.8 %collective-permute-start.1 = (s32[4,128]{1,0:T(4,128)S(1)}, s32[4,128]{1,0:T(4,128)S(1)}, u32[]{:S(2)}, u32[]{:S(2)}) collective-permute-start(s32[4,128]{1,0:T(4,128)S(1)} %reshape.28), channel_id=1, source_target_pairs={{0,8},{4,12},{8,0},{12,4},{1,9},{5,13},{9,1},{13,5},{2,10},{6,14},... | collective-permute-start | bytes 6152 | tf_op jit(solution)/shard_map/ppermute | solution.py:48
  7.0 6.8 %collective-permute-start = (s32[4,128]{1,0:T(4,128)S(1)}, s32[4,128]{1,0:T(4,128)S(1)}, u32[]{:S(2)}, u32[]{:S(2)}) collective-permute-start(s32[4,128]{1,0:T(4,128)S(1)} %reshape.28), channel_id=1, source_target_pairs={{0,4},{4,0},{8,12},{12,8},{1,5},{5,1},{9,13},{13,9},{2,6},{6,2},{1... | collective-permute-start | bytes 6152 | tf_op jit(solution)/shard_map/ppermute | solution.py:48
  9.4 12.1 %collective-permute-start.8 = (f32[256,128]{1,0:T(8,128)S(1)}, f32[256,128]{1,0:T(8,128)S(1)}, u32[]{:S(2)}, u32[]{:S(2)}) collective-permute-start(f32[256,128]{1,0:T(8,128)S(1)} %bitcast.22), channel_id=1, source_target_pairs={{0,12},{4,8},{8,4},{12,0},{1,13},{5,9},{9,5},{13,1},{2,14},{6,10},... | collective-permute-start | bytes 393224 | tf_op jit(solution)/shard_map/ppermute | solution.py:48
  13.2 10.2 %collective-permute-start.7 = (f32[256,128]{1,0:T(8,128)S(1)}, f32[256,128]{1,0:T(8,128)S(1)}, u32[]{:S(2)}, u32[]{:S(2)}) collective-permute-start(f32[256,128]{1,0:T(8,128)S(1)} %bitcast.23), channel_id=1, source_target_pairs={{0,8},{4,12},{8,0},{12,4},{1,9},{5,13},{9,1},{13,5},{2,10},{6,14},... | collective-permute-start | bytes 393224 | tf_op jit(solution)/shard_map/ppermute | solution.py:48
  13.2 10.2 %collective-permute-start.6 = (f32[256,128]{1,0:T(8,128)S(1)}, f32[256,128]{1,0:T(8,128)S(1)}, u32[]{:S(2)}, u32[]{:S(2)}) collective-permute-start(f32[256,128]{1,0:T(8,128)S(1)} %bitcast.24), channel_id=1, source_target_pairs={{0,4},{4,0},{8,12},{12,8},{1,5},{5,1},{9,13},{13,9},{2,6},{6,2},{1... | collective-permute-start | bytes 393224 | tf_op jit(solution)/shard_map/ppermute | solution.py:48
  13.9 3.7 %collective-permute-start.4 = (s32[16,128]{1,0:T(8,128)S(1)}, s32[16,128]{1,0:T(8,128)S(1)}, u32[]{:S(2)}, u32[]{:S(2)}) collective-permute-start(s32[16,128]{1,0:T(8,128)S(1)} %pad_add_fusion.refs_0_), channel_id=1, source_target_pairs={{0,2},{2,0},{1,3},{3,1},{4,6},{6,4},{5,7},{7,5},{8,10},{10,8},{9,1... | collective-permute-start | bytes 24584 | tf_op jit(solution)/shard_map/ppermute | solution.py:48
  15.6 2.4 %collective-permute-start.3 = (s32[16,128]{1,0:T(8,128)S(1)}, s32[16,128]{1,0:T(8,128)S(1)}, u32[]{:S(2)}, u32[]{:S(2)}) collective-permute-start(s32[16,128]{1,0:T(8,128)S(1)} %pad_add_fusion.refs_0_), channel_id=1, source_target_pairs={{0,1},{1,0},{2,3},{3,2},{4,5},{5,4},{6,7},{7,6},{8,9},{9,8},{10,11... | collective-permute-start | bytes 24584 | tf_op jit(solution)/shard_map/ppermute | solution.py:48
  17.6 1.2 %collective-permute-start.5 = (s32[16,128]{1,0:T(8,128)S(1)}, s32[16,128]{1,0:T(8,128)S(1)}, u32[]{:S(2)}, u32[]{:S(2)}) collective-permute-start(s32[16,128]{1,0:T(8,128)S(1)} %collective-permute-done.4.refs_2_), channel_id=1, source_target_pairs={{0,1},{1,0},{2,3},{3,2},{4,5},{5,4},{6,7},{7,6},{8,9},{9,8},{10,11... | collective-permute-start | bytes 24584 | tf_op jit(solution)/shard_map/ppermute | solution.py:48
  23.4 1.3 %collective-permute-start.9 = (f32[256,128]{1,0:T(8,128)S(1)}, f32[256,128]{1,0:T(8,128)S(1)}, u32[]{:S(2)}, u32[]{:S(2)}) collective-permute-start(f32[256,128]{1,0:T(8,128)S(1)} %collective-permute-done.6.refs_6_), channel_id=1, source_target_pairs={{0,1},{1,0},{2,3},{3,2},{4,5},{5,4},{6,7},{7,6},{8,9},{9,8},{10,11... | collective-permute-start | bytes 393224 | tf_op jit(solution)/shard_map/ppermute | solution.py:48
  23.4 1.5 %collective-permute-start.10 = (f32[256,128]{1,0:T(8,128)S(1)}, f32[256,128]{1,0:T(8,128)S(1)}, u32[]{:S(2)}, u32[]{:S(2)}) collective-permute-start(f32[256,128]{1,0:T(8,128)S(1)} %collective-permute-done.7.refs_8_), channel_id=1, source_target_pairs={{0,1},{1,0},{2,3},{3,2},{4,5},{5,4},{6,7},{7,6},{8,9},{9,8},{10,11... | collective-permute-start | bytes 393224 | tf_op jit(solution)/shard_map/ppermute | solution.py:48
  23.9 1.3 %collective-permute-start.11 = (f32[256,128]{1,0:T(8,128)S(1)}, f32[256,128]{1,0:T(8,128)S(1)}, u32[]{:S(2)}, u32[]{:S(2)}) collective-permute-start(f32[256,128]{1,0:T(8,128)S(1)} %collective-permute-done.8.refs_10_), channel_id=1, source_target_pairs={{0,1},{1,0},{2,3},{3,2},{4,5},{5,4},{6,7},{7,6},{8,9},{9,8},{10,11... | collective-permute-start | bytes 393224 | tf_op jit(solution)/shard_map/ppermute | solution.py:48
  44.5 9.1 %collective-permute-start.14 = (f32[32,128]{1,0:T(8,128)S(1)}, f32[32,128]{1,0:T(8,128)S(1)}, u32[]{:S(2)}, u32[]{:S(2)}) collective-permute-start(f32[32,128]{1,0:T(8,128)S(1)} %get-tuple-element.42), channel_id=1, source_target_pairs={{0,12},{4,8},{8,4},{12,0},{1,13},{5,9},{9,5},{13,1},{2,14},{6,10},... | collective-permute-start | bytes 49160 | tf_op jit(solution)/shard_map/ppermute | solution.py:48
  48.9 4.6 %collective-permute-start.13 = (f32[32,128]{1,0:T(8,128)S(1)}, f32[32,128]{1,0:T(8,128)S(1)}, u32[]{:S(2)}, u32[]{:S(2)}) collective-permute-start(f32[32,128]{1,0:T(8,128)S(1)} %get-tuple-element.42), channel_id=1, source_target_pairs={{0,8},{4,12},{8,0},{12,4},{1,9},{5,13},{9,1},{13,5},{2,10},{6,14},... | collective-permute-start | bytes 49160 | tf_op jit(solution)/shard_map/ppermute | solution.py:48
  48.9 3.7 %collective-permute-start.12 = (f32[32,128]{1,0:T(8,128)S(1)}, f32[32,128]{1,0:T(8,128)S(1)}, u32[]{:S(2)}, u32[]{:S(2)}) collective-permute-start(f32[32,128]{1,0:T(8,128)S(1)} %get-tuple-element.42), channel_id=1, source_target_pairs={{0,4},{4,0},{8,12},{12,8},{1,5},{5,1},{9,13},{13,9},{2,6},{6,2},{1... | collective-permute-start | bytes 49160 | tf_op jit(solution)/shard_map/ppermute | solution.py:48
  53.6 4.3 %collective-permute-start.16 = (f32[128,128]{1,0:T(8,128)S(1)}, f32[128,128]{1,0:T(8,128)S(1)}, u32[]{:S(2)}, u32[]{:S(2)}) collective-permute-start(f32[128,128]{1,0:T(8,128)S(1)} %constant_dynamic-update-slice_fusion.refs_9_), channel_id=1, source_target_pairs={{0,2},{2,0},{1,3},{3,1},{4,6},{6,4},{5,7},{7,5},{8,10},{10,8},{9,1... | collective-permute-start | bytes 196616 | tf_op jit(solution)/shard_map/ppermute | solution.py:48
  54.4 3.5 %collective-permute-start.15 = (f32[128,128]{1,0:T(8,128)S(1)}, f32[128,128]{1,0:T(8,128)S(1)}, u32[]{:S(2)}, u32[]{:S(2)}) collective-permute-start(f32[128,128]{1,0:T(8,128)S(1)} %constant_dynamic-update-slice_fusion.refs_9_), channel_id=1, source_target_pairs={{0,1},{1,0},{2,3},{3,2},{4,5},{5,4},{6,7},{7,6},{8,9},{9,8},{10,11... | collective-permute-start | bytes 196616 | tf_op jit(solution)/shard_map/ppermute | solution.py:48
  57.9 1.3 %collective-permute-start.17 = (f32[128,128]{1,0:T(8,128)S(1)}, f32[128,128]{1,0:T(8,128)S(1)}, u32[]{:S(2)}, u32[]{:S(2)}) collective-permute-start(f32[128,128]{1,0:T(8,128)S(1)} %collective-permute-done.16.refs_11_), channel_id=1, source_target_pairs={{0,1},{1,0},{2,3},{3,2},{4,5},{5,4},{6,7},{7,6},{8,9},{9,8},{10,11... | collective-permute-start | bytes 196616 | tf_op jit(solution)/shard_map/ppermute | solution.py:48
  64.5 6.6 %collective-permute-start.20 = (f32[32,128]{1,0:T(8,128)S(1)}, f32[32,128]{1,0:T(8,128)S(1)}, u32[]{:S(2)}, u32[]{:S(2)}) collective-permute-start(f32[32,128]{1,0:T(8,128)S(1)} %get-tuple-element.51), channel_id=1, source_target_pairs={{0,12},{4,8},{8,4},{12,0},{1,13},{5,9},{9,5},{13,1},{2,14},{6,10},... | collective-permute-start | bytes 49160 | tf_op jit(solution)/shard_map/ppermute | solution.py:48
  66.4 4.6 %collective-permute-start.19 = (f32[32,128]{1,0:T(8,128)S(1)}, f32[32,128]{1,0:T(8,128)S(1)}, u32[]{:S(2)}, u32[]{:S(2)}) collective-permute-start(f32[32,128]{1,0:T(8,128)S(1)} %get-tuple-element.51), channel_id=1, source_target_pairs={{0,8},{4,12},{8,0},{12,4},{1,9},{5,13},{9,1},{13,5},{2,10},{6,14},... | collective-permute-start | bytes 49160 | tf_op jit(solution)/shard_map/ppermute | solution.py:48
  66.7 4.0 %collective-permute-start.18 = (f32[32,128]{1,0:T(8,128)S(1)}, f32[32,128]{1,0:T(8,128)S(1)}, u32[]{:S(2)}, u32[]{:S(2)}) collective-permute-start(f32[32,128]{1,0:T(8,128)S(1)} %get-tuple-element.51), channel_id=1, source_target_pairs={{0,4},{4,0},{8,12},{12,8},{1,5},{5,1},{9,13},{13,9},{2,6},{6,2},{1... | collective-permute-start | bytes 49160 | tf_op jit(solution)/shard_map/ppermute | solution.py:48
  71.1 4.3 %collective-permute-start.22 = (f32[128,128]{1,0:T(8,128)S(1)}, f32[128,128]{1,0:T(8,128)S(1)}, u32[]{:S(2)}, u32[]{:S(2)}) collective-permute-start(f32[128,128]{1,0:T(8,128)S(1)} %constant_dynamic-update-slice_fusion.4.refs_9_), channel_id=1, source_target_pairs={{0,2},{2,0},{1,3},{3,1},{4,6},{6,4},{5,7},{7,5},{8,10},{10,8},{9,1... | collective-permute-start | bytes 196616 | tf_op jit(solution)/shard_map/ppermute | solution.py:48
  71.7 3.7 %collective-permute-start.21 = (f32[128,128]{1,0:T(8,128)S(1)}, f32[128,128]{1,0:T(8,128)S(1)}, u32[]{:S(2)}, u32[]{:S(2)}) collective-permute-start(f32[128,128]{1,0:T(8,128)S(1)} %constant_dynamic-update-slice_fusion.4.refs_9_), channel_id=1, source_target_pairs={{0,1},{1,0},{2,3},{3,2},{4,5},{5,4},{6,7},{7,6},{8,9},{9,8},{10,11... | collective-permute-start | bytes 196616 | tf_op jit(solution)/shard_map/ppermute | solution.py:48
  75.4 1.3 %collective-permute-start.23 = (f32[128,128]{1,0:T(8,128)S(1)}, f32[128,128]{1,0:T(8,128)S(1)}, u32[]{:S(2)}, u32[]{:S(2)}) collective-permute-start(f32[128,128]{1,0:T(8,128)S(1)} %collective-permute-done.22.refs_11_), channel_id=1, source_target_pairs={{0,1},{1,0},{2,3},{3,2},{4,5},{5,4},{6,7},{7,6},{8,9},{9,8},{10,11... | collective-permute-start | bytes 196616 | tf_op jit(solution)/shard_map/ppermute | solution.py:48
  82.1 7.2 %collective-permute-start.26 = (f32[8,128]{1,0:T(8,128)S(1)}, f32[8,128]{1,0:T(8,128)S(1)}, u32[]{:S(2)}, u32[]{:S(2)}) collective-permute-start(f32[8,128]{1,0:T(8,128)S(1)} %get-tuple-element.57), channel_id=1, source_target_pairs={{0,12},{4,8},{8,4},{12,0},{1,13},{5,9},{9,5},{13,1},{2,14},{6,10},... | collective-permute-start | bytes 12296 | tf_op jit(solution)/shard_map/ppermute | solution.py:48
  84.8 4.5 %collective-permute-start.25 = (f32[8,128]{1,0:T(8,128)S(1)}, f32[8,128]{1,0:T(8,128)S(1)}, u32[]{:S(2)}, u32[]{:S(2)}) collective-permute-start(f32[8,128]{1,0:T(8,128)S(1)} %get-tuple-element.57), channel_id=1, source_target_pairs={{0,8},{4,12},{8,0},{12,4},{1,9},{5,13},{9,1},{13,5},{2,10},{6,14},... | collective-permute-start | bytes 12296 | tf_op jit(solution)/shard_map/ppermute | solution.py:48
  85.5 3.6 %collective-permute-start.24 = (f32[8,128]{1,0:T(8,128)S(1)}, f32[8,128]{1,0:T(8,128)S(1)}, u32[]{:S(2)}, u32[]{:S(2)}) collective-permute-start(f32[8,128]{1,0:T(8,128)S(1)} %get-tuple-element.57), channel_id=1, source_target_pairs={{0,4},{4,0},{8,12},{12,8},{1,5},{5,1},{9,13},{13,9},{2,6},{6,2},{1... | collective-permute-start | bytes 12296 | tf_op jit(solution)/shard_map/ppermute | solution.py:48
  89.3 4.0 %collective-permute-start.28 = (f32[64,128]{1,0:T(8,128)S(1)}, f32[64,128]{1,0:T(8,128)S(1)}, u32[]{:S(2)}, u32[]{:S(2)}) collective-permute-start(f32[64,128]{1,0:T(8,128)S(1)} %constant_dynamic-update-slice_fusion.8.refs_4_), channel_id=1, source_target_pairs={{0,2},{2,0},{1,3},{3,1},{4,6},{6,4},{5,7},{7,5},{8,10},{10,8},{9,1... | collective-permute-start | bytes 98312 | tf_op jit(solution)/shard_map/ppermute | solution.py:48
  89.9 3.3 %collective-permute-start.27 = (f32[64,128]{1,0:T(8,128)S(1)}, f32[64,128]{1,0:T(8,128)S(1)}, u32[]{:S(2)}, u32[]{:S(2)}) collective-permute-start(f32[64,128]{1,0:T(8,128)S(1)} %constant_dynamic-update-slice_fusion.8.refs_4_), channel_id=1, source_target_pairs={{0,1},{1,0},{2,3},{3,2},{4,5},{5,4},{6,7},{7,6},{8,9},{9,8},{10,11... | collective-permute-start | bytes 98312 | tf_op jit(solution)/shard_map/ppermute | solution.py:48
  93.3 1.2 %collective-permute-start.29 = (f32[64,128]{1,0:T(8,128)S(1)}, f32[64,128]{1,0:T(8,128)S(1)}, u32[]{:S(2)}, u32[]{:S(2)}) collective-permute-start(f32[64,128]{1,0:T(8,128)S(1)} %collective-permute-done.28.refs_6_), channel_id=1, source_target_pairs={{0,1},{1,0},{2,3},{3,2},{4,5},{5,4},{6,7},{7,6},{8,9},{9,8},{10,11... | collective-permute-start | bytes 98312 | tf_op jit(solution)/shard_map/ppermute | solution.py:48
